TPU v7x, 256 devices: a whole 4x4x8 slice. The times are simulated.
256 devices in a mesh: replica: 32 (over y_hi, z, core), tensor: 8 (over x, y_lo).
Axes of the slice: x: 4, y: 4 (y_hi: 2, y_lo: 2; y = y_hi * 2 + y_lo), z: 8, core: 2. Of those that a mesh axis runs over, the one named last changes fastest.
Arguments:
- hidden: bfloat16 [4096, 4, 8192], P('replica', None, 'tensor'), may hold values from -6 to 6
- queries: bfloat16 [4096, 4, 8192], P('replica', None, 'tensor'), may hold values from -90 to 90
- key_cache_rows: bfloat16 [4096, 48, 1024], P('replica', None, 'tensor'), may hold values from -7 to 7
- value_cache_rows: bfloat16 [4096, 48, 1024], P('replica', None, 'tensor'), may hold values from -6 to 6
- lengths: int32 [4096], P('replica'), may hold values from 2 to 48, as said below
- request_adapter: int32 [4096], P('replica'), may hold values from 0 to 511, as said below
- block_first_row: int32 [1024], P('replica'), may hold values from 0 to 127, as said below
- adapter_owner_group: int32 [512], replicated, may hold values from 0 to 31, as said below
- key_value_weight: bfloat16 [8192, 2, 1024], P(None, None, 'tensor'), may hold values from -0.0625 to 0.0625
- adapter_down_weight: bfloat16 [512, 2, 32, 8192], P('replica', None, None, 'tensor'), may hold values from -0.0625 to 0.0625
- adapter_up_weight: bfloat16 [512, 2, 32, 1024], P('replica', None, None, 'tensor'), may hold values from -1 to 1
Outputs:
- fresh_kv: bfloat16 [4096, 4, 2, 1024], P('replica', None, None, 'tensor')
- attended: bfloat16 [4096, 4, 8192], P('replica', None, 'tensor')
Inputs may be any that keep to these rules, and one draw needn't show every extreme that they name: `adapter_owner_group`: each replica group index holds exactly 16 adapters. block_first_row counts rows within its replica group; each group has 32 blocks in rising order starting at 0, of 1 to 7 rows each, and some block of every group has exactly 7 rows. `request_adapter`: all rows of one block name the same adapter; among the 32 blocks of one replica group at most 2 name adapters of one owner, and in every group some owner has exactly 2. `lengths`: some request of every replica group has exactly 48 live positions.
All inputs are finite; a program needn't handle non-finite values.
Results may differ from a plain program's by a relative error of at most 0.0065.
Values may be sent and summed in bfloat16 or wider, within the bound.
No kernel may reach another device: no remote copies, remote signals or barrier semaphores. Data moves between devices by JAX's collectives and lax.ppermute only.
A program may use at most 128 MiB of HBM per device.

v0:
```python
import jax
import jax.numpy as jnp
from jax import lax
from jax.sharding import PartitionSpec as P

HD = 128
BLK = 7


masked_score = -1e30


def attend_local(queries, key_cache_rows, value_cache_rows, lengths, fresh):
    row_count = queries.shape[0]
    step_count = queries.shape[1]
    head_count = fresh.shape[3] // HD
    query_heads = queries.reshape(row_count, step_count, head_count, -1, HD)
    old_keys = key_cache_rows.reshape(row_count, -1, head_count, HD)
    old_values = value_cache_rows.reshape(row_count, -1, head_count, HD)
    new_keys = fresh[:, :, 0].reshape(row_count, step_count, head_count, HD)
    new_values = fresh[:, :, 1].reshape(row_count, step_count, head_count, HD)
    scale = HD ** (-0.5)
    cached_scores = (
        jnp.einsum("rsgjh,rpgh->rsgjp", query_heads, old_keys, preferred_element_type=jnp.float32)
        * scale
    )
    fresh_scores = (
        jnp.einsum("rsgjh,rtgh->rsgjt", query_heads, new_keys, preferred_element_type=jnp.float32)
        * scale
    )
    live = jnp.arange(old_keys.shape[1])[None, :] < lengths[:, None]
    cached_scores = jnp.where(live[:, None, None, None, :], cached_scores, masked_score)
    causal = jnp.arange(step_count)[None, :] <= jnp.arange(step_count)[:, None]
    fresh_scores = jnp.where(causal[None, :, None, None, :], fresh_scores, masked_score)
    highest = jnp.maximum(jnp.max(cached_scores, axis=-1), jnp.max(fresh_scores, axis=-1))
    cached_exp = jnp.exp(cached_scores - highest[..., None])
    fresh_exp = jnp.exp(fresh_scores - highest[..., None])
    total = jnp.sum(cached_exp, axis=-1) + jnp.sum(fresh_exp, axis=-1)
    cached_probs = (cached_exp / total[..., None]).astype(jnp.bfloat16)
    fresh_probs = (fresh_exp / total[..., None]).astype(jnp.bfloat16)
    mixed = jnp.einsum(
        "rsgjp,rpgh->rsgjh", cached_probs, old_values, preferred_element_type=jnp.float32
    )
    mixed = mixed + jnp.einsum(
        "rsgjt,rtgh->rsgjh", fresh_probs, new_values, preferred_element_type=jnp.float32
    )
    return mixed.astype(jnp.bfloat16).reshape(row_count, step_count, -1)


def per_device(
    hidden,
    queries,
    key_cache_rows,
    value_cache_rows,
    lengths,
    request_adapter,
    block_first_row,
    adapter_owner_group,
    key_value_weight,
    adapter_down_weight,
    adapter_up_weight,
):
    row_count = hidden.shape[0]
    replicas = lax.axis_size("replica")
    block_count = block_first_row.shape[0]
    capacity = max(2, 2 * ((block_count + replicas - 1) // replicas))
    base = jnp.einsum(
        "rsd,dck->rsck",
        lax.all_gather(hidden, "tensor", axis=2, tiled=True),
        key_value_weight,
        preferred_element_type=jnp.float32,
    )
    adapter_ids = jnp.arange(adapter_owner_group.shape[0], dtype=jnp.int32)
    earlier = (adapter_owner_group[None, :] == adapter_owner_group[:, None]) & (
        adapter_ids[None, :] < adapter_ids[:, None]
    )
    local_slot = jnp.sum(earlier.astype(jnp.int32), axis=1)
    block_adapter = request_adapter[block_first_row]
    block_owner = adapter_owner_group[block_adapter]
    block_local = local_slot[block_adapter]
    block_ids = jnp.arange(block_count, dtype=jnp.int32)
    before = (block_owner[None, :] == block_owner[:, None]) & (
        block_ids[None, :] < block_ids[:, None]
    )
    bucket = block_owner * capacity + jnp.sum(before.astype(jnp.int32), axis=1)
    request = (
        jnp.zeros((replicas * capacity,), jnp.int32)
        .at[bucket]
        .set(block_local)
        .reshape(replicas, capacity)
    )
    row_offsets = jnp.arange(BLK, dtype=jnp.int32)
    row_index = jnp.minimum(block_first_row[:, None] + row_offsets[None, :], row_count - 1)
    blocked = hidden[row_index]
    incoming_slots = lax.all_to_all(request, "replica", split_axis=0, concat_axis=0, tiled=True)
    down_returned = lax.all_to_all(
        adapter_down_weight[incoming_slots], "replica", split_axis=0, concat_axis=0, tiled=True
    )
    up_returned = lax.all_to_all(
        adapter_up_weight[incoming_slots], "replica", split_axis=0, concat_axis=0, tiled=True
    )
    down_fetched = down_returned.reshape((-1,) + down_returned.shape[2:])[bucket]
    up_fetched = up_returned.reshape((-1,) + up_returned.shape[2:])[bucket]
    partial_value = jnp.einsum(
        "nbsd,ncid->nbsci", blocked, down_fetched, preferred_element_type=jnp.float32
    )
    low_rank = lax.psum(partial_value, "tensor").astype(jnp.bfloat16)
    delta = jnp.einsum(
        "nbsci,ncik->nbsck", low_rank, up_fetched, preferred_element_type=jnp.float32
    )
    row_ids = jnp.arange(row_count, dtype=jnp.int32)
    row_block = (
        jnp.sum((block_first_row[None, :] <= row_ids[:, None]).astype(jnp.int32), axis=1) - 1
    )
    flat_index = row_block * BLK + row_ids - block_first_row[row_block]
    row_delta = delta.reshape((-1,) + delta.shape[2:])[flat_index]
    fresh = (base + row_delta).astype(jnp.bfloat16)
    attended = attend_local(queries, key_cache_rows, value_cache_rows, lengths, fresh)
    return (fresh, attended)


def solution(mesh):
    placed = (
        P("replica", None, "tensor"),
        P("replica", None, "tensor"),
        P("replica", None, "tensor"),
        P("replica", None, "tensor"),
        P("replica"),
        P("replica"),
        P("replica"),
        P(),
        P(None, None, "tensor"),
        P("replica", None, None, "tensor"),
        P("replica", None, None, "tensor"),
    )
    return jax.shard_map(
        per_device,
        mesh=mesh,
        in_specs=placed,
        out_specs=(P("replica", None, None, "tensor"), P("replica", None, "tensor")),
        check_vma=False,
    )
```

profile of v0, /device:TPU:32, one launch (start us, length us, event | category | flops | bytes accessed | tf_op | source)
XLA Modules:
  0.0 415.2 jit_solution(15241889357473140776)
XLA Ops:
  7.2 0.0 copy-start
  7.2 0.0 copy-start.4
  7.2 0.8 compare_select_fusion.6
  8.0 1.4 gather_fusion
  9.4 1.0 convert_reduce_fusion
  10.4 1.4 gather_fusion.1
  11.8 0.2 convert_reduce_fusion.2
  12.0 0.7 gather_fusion.2
  12.7 0.7 scatter_custom_fusion
  13.4 0.1 all_to_all.14
  13.5 19.9 %all_to_all.22 = s32[32,1,2]{2,1,0:T(1,128)S(1)} all-to-all(s32[32,1,2]{2,1,0:T(1,128)S(1)} %bitcast.146), channel_id=1, replica_groups=mesh['replica'=32,'tensor'=8] {'replica'}, dimensions={0} | all-to-all | bytes 512 | tf_op jit(solution)/shard_map/all_to_all | solution.py:95
  33.4 0.1 copy.45
  33.4 0.1 copy.46
  33.5 0.1 reshape.322
  33.7 0.0 copy-done.4
  33.7 1.7 gather_fusion.3
  35.3 5.0 %all-to-all-start.1 = ((bf16[32,2,2,32,128]{4,3,2,1,0:T(8,128)(2,1)}), bf16[32,2,2,32,128]{4,3,2,1,0:T(8,128)(2,1)S(1)}, u32[]{:S(2)}, u32[]{:S(2)}) async-start(bf16[32,2,2,32,128]{4,3,2,1,0:T(8,128)(2,1)} %bitcast.9), calls=%async_computation.1 | async-start | bytes 2097152 | tf_op jit(solution)/shard_map/all_to_all | solution.py:99
  40.3 0.0 copy-done
  40.4 5.4 %gather_fusion.6 = bf16[64,2,32,1024]{3,2,1,0:T(8,128)(2,1)} fusion(bf16[16,2,32,1024]{3,2,1,0:T(8,128)(2,1)S(1)} %copy-done, s32[1024]{0:T(1024)S(1)} %pad_clamp_fusion.4), kind=kCustom, calls=%fused_computation.6 | custom fusion | bytes 16777472 | tf_op jit(solution)/shard_map/gather | solution.py:97
  45.8 25.2 %all-to-all-done.1 = bf16[32,2,2,32,128]{4,3,2,1,0:T(8,128)(2,1)S(1)} async-done(((bf16[32,2,2,32,128]{4,3,2,1,0:T(8,128)(2,1)}), bf16[32,2,2,32,128]{4,3,2,1,0:T(8,128)(2,1)S(1)}, u32[]{:S(2)}, u32[]{:S(2)}) %all-to-all-start.1) | async-done | bytes 1048608 | tf_op jit(solution)/shard_map/all_to_all | solution.py:99
  71.0 0.0 copy-start.5
  71.0 1.0 copy-done.5
  72.0 0.0 copy-start.3
  72.0 4.9 %all-to-all-start.2 = ((bf16[32,2,2,32,1024]{4,3,2,1,0:T(8,128)(2,1)}), bf16[32,2,2,32,1024]{4,3,2,1,0:T(8,128)(2,1)}, u32[]{:S(2)}, u32[]{:S(2)}) async-start(bf16[32,2,2,32,1024]{4,3,2,1,0:T(8,128)(2,1)} %bitcast.142), calls=%async_computation.2 | async-start | bytes 16777216 | tf_op jit(solution)/shard_map/all_to_all | solution.py:96
  76.9 0.0 copy-start.1
  76.9 0.0 all-gather.2.cloned.1.call-start
  77.0 0.0 copy-done.3
  77.0 1.3 copy.42
  78.2 0.0 all-gather.2.cloned.1.call-update
  78.3 0.0 copy-done.1
  78.3 0.1 compare_select_fusion
  78.4 0.1 reshape.338
  78.5 3.4 gather_fusion.5
  81.8 0.0 copy-start.6
  81.8 0.1 convert_reduce_fusion.1
  81.9 1.2 gather_fusion.8
  83.2 1.5 reshape.290
  84.7 0.0 copy-done.6
  84.7 0.1 iota_compare_fusion.1
  84.8 3.8 bitcast_reduce_fusion
  88.6 2.6 gather_fusion.4
  91.3 179.2 %all-to-all-done.2 = bf16[32,2,2,32,1024]{4,3,2,1,0:T(8,128)(2,1)} async-done(((bf16[32,2,2,32,1024]{4,3,2,1,0:T(8,128)(2,1)}), bf16[32,2,2,32,1024]{4,3,2,1,0:T(8,128)(2,1)}, u32[]{:S(2)}, u32[]{:S(2)}) %all-to-all-start.2) | async-done | bytes 8388640 | tf_op jit(solution)/shard_map/all_to_all | solution.py:96
  270.5 6.1 %gather_fusion.7 = bf16[32,2,32,1024]{3,2,1,0:T(8,128)(2,1)} fusion(bf16[64,2,32,1024]{3,2,1,0:T(8,128)(2,1)} %bitcast.16, s32[1024]{0:T(1024)S(1)} %pad_clamp_fusion.3), kind=kCustom, calls=%fused_computation.7 | custom fusion | bytes 8388736 | tf_op jit(solution)/shard_map/gather | solution.py:102
  276.6 7.3 %fusion.2 = f32[32,7,4,2,32]{4,1,2,3,0:T(8,128)} fusion(bf16[32,2,32,1024]{3,2,1,0:T(8,128)(2,1)} %gather_fusion.7, bf16[32,7,4,1024,1]{3,2,1,0,4:T(4,128)(2,1)} %bitcast.143), kind=kOutput, calls=%fused_computation.13 | convolution fusion | flops 117440512 | bytes 6258688 | tf_op jit(solution)/shard_map/nbsd,ncid->nbsci/dot_general | solution.py:104
  283.9 98.3 %all-reduce.1 = bf16[32,7,4,2,32]{4,1,2,3,0:T(8,128)(2,1)} all-reduce(f32[32,7,4,2,32]{4,1,2,3,0:T(8,128)} %fusion.2), channel_id=1, replica_groups=mesh['replica'=32,'tensor'=8] {'tensor'}, use_global_device_ids=true, to_apply=%region_3.0 | all-reduce | flops 57344 | bytes 344064 | tf_op jit(solution)/shard_map/psum | solution.py:107
  382.2 1.5 convolution_bitcast_fusion
  383.7 0.7 copy.48
  384.4 1.2 copy.49
  385.7 2.8 gather_fusion.9
  388.5 0.0 all-gather.2.cloned.1.call-done
  388.5 7.0 %fusion.21 = bf16[128,4,2,128]{3,0,2,1:T(8,128)(2,1)S(1)} fusion(bf16[8192,2,128]{2,1,0:T(2,128)(2,1)} %param.19, bf16[128,4,8192]{2,0,1:T(8,128)(2,1)} %all-gather.2.cloned.1.call-done, f32[128,4,2,128]{3,1,2,0:T(4,128)} %gather_fusion.9), kind=kOutput, calls=%fused_computation.35 | convolution fusion | flops 2147745792 | bytes 13369344 | tf_op jit(solution)/shard_map/rsd,dck->rsck/dot_general | solution.py:67
  395.6 1.0 copy.53
  396.5 0.0 copy-start.2
  396.5 4.7 %fusion.50 = (f32[128,4,8]{2,1,0:T(4,128)S(1)}, f32[128,4,1,8,4]{3,4,1,0,2:T(4,128)S(1)}) fusion(bf16[128,4,8,128]{3,2,1,0:T(8,128)(2,1)S(1)} %reshape.290, bf16[128,4,128,1]{2,0,1,3:T(8,128)(2,1)S(1)} %get-tuple-element.11, pred[4,4]{1,0:T(4,128)(4,1)S(1)} %iota_compare_fusion.4), kind=kOutput, calls=%fused_computation.88 | convolution fusion | flops 4239360 | bytes 1261584 | tf_op jit(solution)/shard_map/rsgjh,rtgh->rsgjt/dot_general | solution.py:28
  401.3 0.1 max.9
  401.3 1.0 fusion.33
  402.3 0.0 copy-start.7
  402.3 0.0 copy-done.2
  402.3 1.4 fusion.9
  403.7 0.1 add.178
  403.8 0.0 copy-done.7
  403.8 2.6 fusion.10
  406.4 0.9 fusion.14
  407.3 1.1 reshape.295
  (14 shorter events, 0.1 us)
Async XLA Ops:
  7.2 33.2 %copy-start = (bf16[16,2,32,1024]{3,2,1,0:T(8,128)(2,1)S(1)}, bf16[16,2,32,1024]{3,2,1,0:T(8,128)(2,1)}, u32[]{:S(2)}) copy-start(bf16[16,2,32,1024]{3,2,1,0:T(8,128)(2,1)} %param.20) | copy-start | bytes 6291460
  7.2 26.5 %copy-start.4 = (bf16[16,2,32,128]{3,2,1,0:T(8,128)(2,1)S(1)}, bf16[16,2,32,128]{3,2,1,0:T(8,128)(2,1)}, u32[]{:S(2)}) copy-start(bf16[16,2,32,128]{3,2,1,0:T(8,128)(2,1)} %param.21) | copy-start | bytes 786436
  35.3 35.6 %all-to-all-start.1 = ((bf16[32,2,2,32,128]{4,3,2,1,0:T(8,128)(2,1)}), bf16[32,2,2,32,128]{4,3,2,1,0:T(8,128)(2,1)S(1)}, u32[]{:S(2)}, u32[]{:S(2)}) async-start(bf16[32,2,2,32,128]{4,3,2,1,0:T(8,128)(2,1)} %bitcast.9), calls=%async_computation.1 | async-start | bytes 2097152 | tf_op jit(solution)/shard_map/all_to_all | solution.py:99
  71.0 1.0 copy-start.5
  72.0 5.0 %copy-start.3 = (bf16[128,4,1024]{2,1,0:T(4,128)(2,1)S(1)}, bf16[128,4,1024]{2,1,0:T(4,128)(2,1)}, u32[]{:S(2)}) copy-start(bf16[128,4,1024]{2,1,0:T(4,128)(2,1)} %param.11) | copy-start | bytes 3145732
  72.0 198.5 %all-to-all-start.2 = ((bf16[32,2,2,32,1024]{4,3,2,1,0:T(8,128)(2,1)}), bf16[32,2,2,32,1024]{4,3,2,1,0:T(8,128)(2,1)}, u32[]{:S(2)}, u32[]{:S(2)}) async-start(bf16[32,2,2,32,1024]{4,3,2,1,0:T(8,128)(2,1)} %bitcast.142), calls=%async_computation.2 | async-start | bytes 16777216 | tf_op jit(solution)/shard_map/all_to_all | solution.py:96
  76.9 1.4 copy-start.1
  76.9 311.6 %all-gather.2.cloned.1.call-start = ((), (), s32[]{:S(2)}) async-start(), calls=%async_computation.3 | async-start | bytes 9437184 | tf_op jit(solution)/shard_map/all_gather | solution.py:69
  81.8 2.9 copy-start.6
  396.5 5.8 %copy-start.2 = (f32[128,48,4,8]{1,3,2,0:T(8,128)S(1)}, f32[128,48,4,8]{1,3,2,0:T(8,128)}, u32[]{:S(2)}) copy-start(f32[128,48,4,8]{1,3,2,0:T(8,128)} %get-tuple-element.13) | copy-start | bytes 2359300
  402.3 1.5 copy-start.7
Sparse Core Ops, SparseCore 0:
  80.1 273.4 all-gather.1
where the time goes:
time: 419 us; the launch traced here: 415 us
  waiting for transfers between devices  204 us (49%)
  blocking collectives  118 us (28%)
  local copies, waits for them, and re-layouts  35.7 us (9%)
  matrix products  27.7 us (7%)
  between operations  14.3 us (3%)
  starting transfers between devices  9.97 us (2%)
  other arithmetic  4.84 us (1%)
    all_to_all x1, waiting for transfers between devices, per_device(): lax.all_to_all(adapter_down_weight[incoming_slots], 'replica', split_axis...  179 us
    psum x1, blocking collectives, per_device(): low_rank = lax.psum(partial_value, 'tensor').astype(jnp.bfloat16)  98.3 us
    all_to_all x1, waiting for transfers between devices, per_device(): lax.all_to_all(adapter_up_weight[incoming_slots], 'replica', split_axis=0...  25.2 us
    all_to_all x1, blocking collectives, per_device(): lax.all_to_all(request, 'replica', split_axis=0, concat_axis=0, tiled=True)  19.9 us
  transfers between devices with their start and end apart: 3, of which 2 were waited for; matrix products, arithmetic and copies ran while one was open for 9% of the time, Pallas kernels for 0%

commit v1 on v0

v1 whole, which is shorter than its diff:
```python
import jax
import jax.numpy as jnp
from jax import lax
from jax.sharding import PartitionSpec as P

HD = 128
BLK = 7
PAIR = 2
PAIR_ROWS = PAIR * BLK


masked_score = -1e30


def attend_local(queries, key_cache_rows, value_cache_rows, lengths, fresh):
    row_count = queries.shape[0]
    step_count = queries.shape[1]
    head_count = fresh.shape[3] // HD
    query_heads = queries.reshape(row_count, step_count, head_count, -1, HD)
    old_keys = key_cache_rows.reshape(row_count, -1, head_count, HD)
    old_values = value_cache_rows.reshape(row_count, -1, head_count, HD)
    new_keys = fresh[:, :, 0].reshape(row_count, step_count, head_count, HD)
    new_values = fresh[:, :, 1].reshape(row_count, step_count, head_count, HD)
    scale = HD ** (-0.5)
    cached_scores = (
        jnp.einsum("rsgjh,rpgh->rsgjp", query_heads, old_keys, preferred_element_type=jnp.float32)
        * scale
    )
    fresh_scores = (
        jnp.einsum("rsgjh,rtgh->rsgjt", query_heads, new_keys, preferred_element_type=jnp.float32)
        * scale
    )
    live = jnp.arange(old_keys.shape[1])[None, :] < lengths[:, None]
    cached_scores = jnp.where(live[:, None, None, None, :], cached_scores, masked_score)
    causal = jnp.arange(step_count)[None, :] <= jnp.arange(step_count)[:, None]
    fresh_scores = jnp.where(causal[None, :, None, None, :], fresh_scores, masked_score)
    highest = jnp.maximum(jnp.max(cached_scores, axis=-1), jnp.max(fresh_scores, axis=-1))
    cached_exp = jnp.exp(cached_scores - highest[..., None])
    fresh_exp = jnp.exp(fresh_scores - highest[..., None])
    total = jnp.sum(cached_exp, axis=-1) + jnp.sum(fresh_exp, axis=-1)
    cached_probs = (cached_exp / total[..., None]).astype(jnp.bfloat16)
    fresh_probs = (fresh_exp / total[..., None]).astype(jnp.bfloat16)
    mixed = jnp.einsum(
        "rsgjp,rpgh->rsgjh", cached_probs, old_values, preferred_element_type=jnp.float32
    )
    mixed = mixed + jnp.einsum(
        "rsgjt,rtgh->rsgjh", fresh_probs, new_values, preferred_element_type=jnp.float32
    )
    return mixed.astype(jnp.bfloat16).reshape(row_count, step_count, -1)


def shifted(value, dx, dy):
    pairs = [(t, ((t // 2 + dx) % 4) * 2 + ((t % 2) ^ dy)) for t in range(8)]
    return lax.ppermute(value, "tensor", pairs)


def sum_over_tensor(value):
    value = value + shifted(value, 0, 1)
    return (value + shifted(value, 2, 0)) + (shifted(value, 1, 0) + shifted(value, -1, 0))


def project(tokens, key_value_weight):
    half = tokens.shape[0] // 2
    here = lax.axis_index("tensor")
    x, y = here // 2, here % 2
    depth = tokens.shape[1]

    def product(piece, dx, dy):
        start = (lax.rem(x - dx + 4, 4) * 2 + (y ^ dy)) * depth
        part = lax.dynamic_slice_in_dim(key_value_weight, start, depth, 0)
        return jnp.einsum("td,dck->tck", piece, part, preferred_element_type=jnp.float32)

    right = shifted(tokens, 1, 0)
    left = shifted(tokens, -1, 0)
    across = shifted(tokens, 0, 1)
    right_across = shifted(across, 1, 0)
    left_across = shifted(across, -1, 0)
    far = jnp.concatenate([shifted(right[:half], 1, 0), shifted(left[half:], -1, 0)], axis=0)
    far_across = shifted(far, 0, 1)
    base = product(tokens, 0, 0) + product(across, 0, 1)
    base = base + product(right, 1, 0) + product(left, -1, 0)
    base = base + product(right_across, 1, 1) + product(left_across, -1, 1)
    return base + product(far, 2, 0) + product(far_across, 2, 1)


def per_device(
    hidden,
    queries,
    key_cache_rows,
    value_cache_rows,
    lengths,
    request_adapter,
    block_first_row,
    adapter_owner_group,
    key_value_weight,
    adapter_down_weight,
    adapter_up_weight,
):
    row_count, step_count, depth = hidden.shape
    replicas = lax.axis_size("replica")
    block_count = block_first_row.shape[0]
    token_count = row_count * step_count
    held, sides, rank = adapter_down_weight.shape[:3]
    tokens = hidden.reshape(token_count, depth)

    rows = jnp.arange(row_count, dtype=jnp.int32)
    pool = jnp.arange(adapter_owner_group.shape[0], dtype=jnp.int32)
    first = block_first_row
    after = jnp.concatenate([first[1:], jnp.full((1,), row_count, jnp.int32)])
    block_adapter = jnp.sum(
        jnp.where(first[:, None] == rows[None, :], request_adapter[None, :], 0), axis=1
    )
    block_owner = jnp.sum(
        jnp.where(block_adapter[:, None] == pool[None, :], adapter_owner_group[None, :], 0), axis=1
    )
    block_slot = jnp.sum(
        (adapter_owner_group[None, :] == block_owner[:, None]) & (pool[None, :] < block_adapter[:, None]),
        axis=1, dtype=jnp.int32,
    )
    ids = jnp.arange(block_count, dtype=jnp.int32)
    before = (block_owner[None, :] == block_owner[:, None]) & (ids[None, :] < ids[:, None])
    block_turn = jnp.sum(before, axis=1, dtype=jnp.int32)
    block_offset = jnp.sum(jnp.where(before, (after - first)[None, :], 0), axis=1)

    member = (first[None, :] <= rows[:, None]) & (rows[:, None] < after[None, :])
    row_place = rows + jnp.sum(
        jnp.where(member, (block_owner * PAIR_ROWS + block_offset - first)[None, :], 0), axis=1
    )
    row_slot = jnp.sum(jnp.where(member, block_slot[None, :], 0), axis=1)
    row_fetch = jnp.sum(jnp.where(member, (block_owner * PAIR + block_turn)[None, :], 0), axis=1)
    places = jnp.arange(replicas * PAIR_ROWS, dtype=jnp.int32)
    place_slot = jnp.sum(jnp.where(places[:, None] == row_place[None, :], row_slot[None, :], 0), axis=1)
    fetches = jnp.arange(replicas * PAIR, dtype=jnp.int32)
    fetch_slot = jnp.sum(
        jnp.where(fetches[:, None] == (block_owner * PAIR + block_turn)[None, :], block_slot[None, :], 0),
        axis=1,
    )
    wanted = lax.all_gather(jnp.concatenate([place_slot, fetch_slot]), "replica", axis=0)

    token_place = (row_place[:, None] * step_count + jnp.arange(step_count, dtype=jnp.int32)[None, :]).reshape(-1)
    token_places = jnp.arange(replicas * PAIR_ROWS * step_count, dtype=jnp.int32)
    sent = jnp.dot(
        (token_places[:, None] == token_place[None, :]).astype(jnp.bfloat16), tokens,
        preferred_element_type=jnp.float32,
    ).astype(jnp.bfloat16)
    received = lax.all_to_all(
        sent.reshape(replicas, PAIR_ROWS * step_count, depth), "replica", split_axis=0, concat_axis=0, tiled=True
    ).reshape(-1, depth)

    me = lax.axis_index("replica")
    received_slot = lax.dynamic_slice(wanted, (0, me * PAIR_ROWS), (replicas, PAIR_ROWS))
    asked_slot = lax.dynamic_slice(
        wanted, (0, replicas * PAIR_ROWS + me * PAIR), (replicas, PAIR)
    )
    up_fetched = lax.all_to_all(
        adapter_up_weight[asked_slot], "replica", split_axis=0, concat_axis=0, tiled=True
    ).reshape(replicas * PAIR, sides, rank, -1)

    base = project(tokens, key_value_weight)

    every = jnp.einsum(
        "td,acid->taci", received, adapter_down_weight, preferred_element_type=jnp.float32
    )
    token_slot = jnp.repeat(received_slot.reshape(-1), step_count)
    chosen = token_slot[:, None] == jnp.arange(held, dtype=jnp.int32)[None, :]
    partial_low = jnp.sum(jnp.where(chosen[:, :, None, None], every, 0.0), axis=1)
    returned = lax.all_to_all(
        partial_low.reshape(replicas, -1, 128), "replica", split_axis=0, concat_axis=0, tiled=True
    ).reshape(-1, sides * rank)
    mine = returned[token_place]
    low = sum_over_tensor(mine.reshape(-1, 128)).astype(jnp.bfloat16).reshape(token_count, sides, rank)

    token_fetch = jnp.repeat(row_fetch, step_count)
    spread = jnp.where(
        (token_fetch[:, None] == fetches[None, :])[:, None, :, None], low[:, :, None, :], 0
    ).astype(jnp.bfloat16)
    delta = jnp.einsum("tcui,ucif->tcf", spread, up_fetched, preferred_element_type=jnp.float32)
    fresh = (base + delta).astype(jnp.bfloat16).reshape(row_count, step_count, sides, -1)
    attended = attend_local(queries, key_cache_rows, value_cache_rows, lengths, fresh)
    return (fresh, attended)


def solution(mesh):
    placed = (
        P("replica", None, "tensor"),
        P("replica", None, "tensor"),
        P("replica", None, "tensor"),
        P("replica", None, "tensor"),
        P("replica"),
        P("replica"),
        P("replica"),
        P(),
        P(None, None, "tensor"),
        P("replica", None, None, "tensor"),
        P("replica", None, None, "tensor"),
    )
    return jax.shard_map(
        per_device,
        mesh=mesh,
        in_specs=placed,
        out_specs=(P("replica", None, None, "tensor"), P("replica", None, "tensor")),
        check_vma=False,
    )
```

time: 419 us -> 275 us (0.66)
  waiting for transfers between devices: 204 us -> 23.9 us
  starting transfers between devices: 9.97 us -> 42 us
  matrix products: 27.7 us -> 46.1 us
  between operations: 14.3 us -> 1.26 us
  blocking collectives: 118 us -> 110 us
  other arithmetic: 4.84 us -> 9.81 us
  local copies, waits for them, and re-layouts: 35.7 us -> 40.6 us
    all_to_all x2 -> x3, waiting for transfers between devices: 204 us -> 6.38 us  [the longest x1 6.38 us: per_device(): lax.all_to_all(partial_low.reshape(replicas, -1, 128), 'replica', split_a...]
    all_gather x0 -> x1, blocking collectives: none -> 110 us  [per_device(): lax.all_gather(jnp.concatenate([place_slot, fetch_slot]), 'replica', axis=0)]
    psum x1 -> x0, blocking collectives: 98.3 us -> none  [per_device(): low_rank = lax.psum(partial_value, 'tensor').astype(jnp.bfloat16)]
    gather x10 -> x3, local copies, waits for them, and re-layouts: 26.7 us -> 4.72 us  [the longest x2 2.8 us: per_device(): adapter_up_weight[asked_slot]]
    all_to_all x1 -> x0, blocking collectives: 19.9 us -> none  [per_device(): lax.all_to_all(request, 'replica', split_axis=0, concat_axis=0, tiled=True)]
    ppermute x0 -> x12, waiting for transfers between devices: none -> 17.5 us  [shifted(): return lax.ppermute(value, 'tensor', pairs)]
    all_to_all x2 -> x3, starting transfers between devices: 9.93 us -> 27.4 us  [the longest x1 11.4 us: per_device(): lax.all_to_all(sent.reshape(replicas, PAIR_ROWS * step_count, depth), 're...]
    dot_general x3 -> x11, matrix products: 15.8 us -> 32.1 us  [the longest x8 18.5 us: product(): jnp.einsum('td,dck->tck', piece, part, preferred_element_type=jnp.float32)]
  transfers between devices with their start and end apart: 3 -> 15, of which waited for: 2 -> 5; matrix products, arithmetic and copies ran while one was open for 9% -> 23% of each run, Pallas kernels for 0% -> 0%
where the time goes in v1:
time: 275 us; the launch traced here: 273 us
  blocking collectives  110 us (40%)
  matrix products  46.1 us (17%)
  starting transfers between devices  42 us (15%)
  local copies, waits for them, and re-layouts  40.6 us (15%)
  waiting for transfers between devices  23.9 us (9%)
  other arithmetic  9.81 us (4%)
    all_gather x1, blocking collectives, per_device(): lax.all_gather(jnp.concatenate([place_slot, fetch_slot]), 'replica', axis=0)  110 us
    dot_general x8, matrix products, product(): jnp.einsum('td,dck->tck', piece, part, preferred_element_type=jnp.float32)  18.5 us
    ppermute x12, waiting for transfers between devices, shifted(): return lax.ppermute(value, 'tensor', pairs)  17.5 us
    ppermute x12, starting transfers between devices, shifted(): return lax.ppermute(value, 'tensor', pairs)  14.6 us
    all_to_all x1, starting transfers between devices, per_device(): lax.all_to_all(sent.reshape(replicas, PAIR_ROWS * step_count, depth), 're...  11.4 us
    all_to_all x1, starting transfers between devices, per_device(): lax.all_to_all(partial_low.reshape(replicas, -1, 128), 'replica', split_a...  9.92 us
    all_to_all x1, waiting for transfers between devices, per_device(): lax.all_to_all(partial_low.reshape(replicas, -1, 128), 'replica', split_a...  6.38 us
    dot_general x1, matrix products, per_device(): jnp.einsum('td,acid->taci', received, adapter_down_weight, preferred_elem...  6.3 us
  transfers between devices with their start and end apart: 15, of which 5 were waited for; matrix products, arithmetic and copies ran while one was open for 23% of the time, Pallas kernels for 0%

profile of v1, /device:TPU:32, one launch (start us, length us, event | category | flops | bytes accessed | tf_op | source)
XLA Modules:
  0.0 273.3 jit_solution(1834302528580399118)
XLA Ops:
  0.6 0.9 slice.17
  1.5 0.8 select_reduce_fusion.8
  2.4 0.9 select_reduce_fusion.2
  3.2 0.9 convert_reduce_fusion
  4.1 0.7 pad_add_fusion.1
  5.0 0.7 add_subtract_fusion
  5.7 0.8 select_reduce_fusion.3
  6.5 2.1 reshape.260
  8.8 5.1 %convolution_convert_fusion = bf16[1792,1024]{1,0:T(8,128)(2,1)} fusion(bf16[512,1024]{1,0:T(8,128)(2,1)} %reshape.260, s32[512]{0:T(512)S(1)} %add.253), kind=kOutput, calls=%fused_computation.6 | convolution fusion | flops 1881800704 | bytes 4720640 | tf_op jit(solution)/shard_map/dot_general | solution.py:142
  13.9 11.4 %all-to-all-start.1 = ((bf16[32,56,1024]{2,1,0:T(8,128)(2,1)}), bf16[32,56,1024]{2,1,0:T(8,128)(2,1)}, u32[]{:S(2)}, u32[]{:S(2)}) async-start(bf16[32,56,1024]{2,1,0:T(8,128)(2,1)} %bitcast.134), calls=%async_computation.1 | async-start | bytes 7340032 | tf_op jit(solution)/shard_map/all_to_all | solution.py:146
  25.4 1.6 collective-permute-start.1
  26.9 1.7 collective-permute-start.2
  28.7 0.7 collective-permute-start
  29.7 109.7 %all-gather.1 = s32[32,1,512]{2,1,0:T(1,128)S(1)} all-gather(s32[1,1,512]{2,1,0:T(1,128)S(1)} %bitcast.140), channel_id=2, replica_groups=mesh['replica'=32,'tensor'=8] {'replica'}, dimensions={0}, use_global_device_ids=true | all-gather | bytes 67584 | tf_op jit(solution)/shard_map/all_gather | solution.py:138
  140.1 1.5 reshape.269
  141.7 4.8 %bitcast_reduce_fusion = (f32[128,4,8]{2,1,0:T(4,128)}, f32[128,48,4,8]{1,3,2,0:T(8,128)}) fusion(pred[128,48]{1,0:T(8,128)(4,1)S(1)} %iota_compare_fusion.5, bf16[128,4,8,128]{3,2,1,0:T(8,128)(2,1)S(1)} %reshape.269, bf16[128,48,128]{2,1,0:T(8,128)(2,1)} %param.13), kind=kOutput, calls=%fused_computation.11 | convolution fusion | flops 50917376 | bytes 3430400 | tf_op jit(solution)/shard_map/rsgjh,rpgh->rsgjp/dot_general | solution.py:26
  147.0 0.7 gather_fusion
  147.7 2.1 copy.92
  149.8 5.6 %constant_dynamic-slice_fusion.4 = (bf16[1024,2,128]{2,1,0:T(2,128)(2,1)}, bf16[1024,2,128]{2,1,0:T(2,128)(2,1)}, bf16[1024,2,128]{2,1,0:T(2,128)(2,1)}, bf16[10...) fusion(bf16[8192,2,128]{2,1,0:T(2,128)(2,1)} %param.19, ...), kind=kLoop, calls=%fused_computation.107 | loop fusion | bytes 8388640 | tf_op jit(solution)/shard_map/dynamic_slice | solution.py:70
  155.3 6.0 %all-to-all-start = ((bf16[32,2,2,32,128]{4,1,3,2,0:T(2,128)(2,1)}), bf16[32,2,2,32,128]{4,1,3,2,0:T(2,128)(2,1)}, u32[]{:S(2)}, u32[]{:S(2)}) async-start(bf16[32,2,2,32,128]{4,1,3,2,0:T(2,128)(2,1)} %copy.92), calls=%async_computation | async-start | bytes 2097152 | tf_op jit(solution)/shard_map/all_to_all | solution.py:155
  161.4 0.6 pad_clamp_fusion
  162.0 1.1 reshape.300
  163.1 1.9 fusion.50
  165.0 1.9 slice.24
  166.8 1.5 collective-permute-start.5
  168.3 0.6 iota_compare_fusion.13
  169.1 0.6 iota_compare_fusion.3
  169.8 1.9 slice.25
  171.7 1.7 collective-permute-start.6
  173.4 1.5 collective-permute-start.4
  175.4 1.9 convolution_add_fusion.2
  177.3 5.8 %collective-permute-done.5 = bf16[256,1024]{1,0:T(8,128)(2,1)} collective-permute-done((bf16[256,1024]{1,0:T(8,128)(2,1)}, bf16[256,1024]{1,0:T(8,128)(2,1)}, u32[]{:S(2)}, u32[]{:S(2)}) %collective-permute-start.5) | collective-permute-done | bytes 524320 | tf_op jit(solution)/shard_map/ppermute | solution.py:54
  183.1 1.9 constant_dynamic-update-slice_fusion.1
  185.0 6.3 %select_reduce_fusion = f32[1792,2,32]{0,2,1:T(8,128)S(1)} fusion(bf16[1792,1024,1,1]{1,0,3,2:T(8,128)(2,1)} %bitcast.15, bf16[16,2,32,1024]{3,2,1,0:T(8,128)(2,1)S(1)} %copy-done, pred[1792,16]{0,1:T(8,128)(4,1)S(1)} %iota_compare_fusion.4), kind=kOutput, calls=%fused_computation.2 | convolution fusion | flops 3761651712 | bytes 6254592 | tf_op jit(solution)/shard_map/td,acid->taci/dot_general | solution.py:161
  191.3 2.3 copy.94
  193.6 3.6 %reshape.265 = f32[32,28,128]{2,1,0:T(8,128)} reshape(f32[1792,2,32]{2,1,0:T(2,128)} %copy.94) | data formatting | bytes 917504 | tf_op jit(solution)/shard_map/reshape | solution.py:168
  197.2 9.9 %all-to-all-start.2 = ((f32[32,28,128]{2,1,0:T(8,128)}), f32[32,28,128]{2,1,0:T(8,128)S(1)}, u32[]{:S(2)}, u32[]{:S(2)}) async-start(f32[32,28,128]{2,1,0:T(8,128)} %reshape.265), calls=%async_computation.2 | async-start | bytes 1048576 | tf_op jit(solution)/shard_map/all_to_all | solution.py:167
  207.1 1.9 constant_dynamic-update-slice_fusion
  209.0 0.7 collective-permute-start.7
  209.7 1.9 fusion.34
  211.6 2.6 fusion.15
  214.2 2.5 fusion.29
  216.7 3.3 %copy.93 = bf16[32,2,2,32,128]{4,1,0,3,2:T(2,128)(2,1)} copy(bf16[32,2,2,32,128]{4,1,3,2,0:T(2,128)(2,1)} %all-to-all-done) | data formatting | bytes 2097152 | tf_op jit(solution)/shard_map/all_to_all | solution.py:155
  220.1 6.4 %all-to-all-done.2 = f32[32,28,128]{2,1,0:T(8,128)S(1)} async-done(((f32[32,28,128]{2,1,0:T(8,128)}), f32[32,28,128]{2,1,0:T(8,128)S(1)}, u32[]{:S(2)}, u32[]{:S(2)}) %all-to-all-start.2) | async-done | bytes 458784 | tf_op jit(solution)/shard_map/all_to_all | solution.py:167
  226.7 1.9 gather_fusion.1
  228.6 1.0 reshape.267
  229.6 0.8 collective-permute-start.8
  230.4 2.7 fusion.31
  233.1 8.3 %collective-permute-done.8 = f32[256,128]{1,0:T(8,128)S(1)} collective-permute-done((f32[256,128]{1,0:T(8,128)S(1)}, f32[256,128]{1,0:T(8,128)S(1)}, u32[]{:S(2)}, u32[]{:S(2)}) %collective-permute-start.8) | collective-permute-done | bytes 131104 | tf_op jit(solution)/shard_map/ppermute | solution.py:54
  241.8 3.0 %collective-permute-start.11 = (f32[256,128]{1,0:T(8,128)S(1)}, f32[256,128]{1,0:T(8,128)S(1)}, u32[]{:S(2)}, u32[]{:S(2)}) collective-permute-start(f32[256,128]{1,0:T(8,128)S(1)} %add.257), channel_id=1, source_target_pairs={{0,6},{1,7},{2,0},{3,1},{4,2},{5,3},{6,4},{7,5},{8,14},{9,15},{10,... | collective-permute-start | bytes 393224 | tf_op jit(solution)/shard_map/ppermute | solution.py:54
  244.7 0.6 collective-permute-start.9
  245.4 2.5 fusion.27
  247.9 2.1 collective-permute-done.11
  250.0 1.2 collective-permute-done.9
  251.6 2.2 fusion.18
  253.9 2.6 fusion.24
  256.4 1.8 copy.96
  258.3 2.2 copy.97
  260.5 5.7 %fusion.61 = (f32[128,4,8]{2,1,0:T(4,128)S(1)}, f32[128,4,1,8,4]{3,4,1,0,2:T(4,128)S(1)}) fusion(bf16[128,4,8,128]{3,2,1,0:T(8,128)(2,1)S(1)} %copy-done.3, bf16[128,4,2,128]{3,1,0,2:T(4,128)(2,1)} %bitcast.137, pred[4,4]{1,0:T(4,128)(4,1)S(1)} %copy-done.19), kind=kOutput, calls=%fused_computation.123 | convolution fusion | flops 4239360 | bytes 1261584 | tf_op jit(solution)/shard_map/rsgjh,rtgh->rsgjt/dot_general | solution.py:30
  266.3 1.4 fusion.8
  267.7 1.0 fusion.42
  268.8 2.6 fusion.9
  271.4 0.8 fusion.13
  272.2 1.1 reshape.274
  (82 shorter events, 3.6 us)
Async XLA Ops:
  0.6 184.4 %copy-start = (bf16[16,2,32,1024]{3,2,1,0:T(8,128)(2,1)S(1)}, bf16[16,2,32,1024]{3,2,1,0:T(8,128)(2,1)}, u32[]{:S(2)}) copy-start(bf16[16,2,32,1024]{3,2,1,0:T(8,128)(2,1)} %param.20) | copy-start | bytes 6291460
  13.9 141.4 %all-to-all-start.1 = ((bf16[32,56,1024]{2,1,0:T(8,128)(2,1)}), bf16[32,56,1024]{2,1,0:T(8,128)(2,1)}, u32[]{:S(2)}, u32[]{:S(2)}) async-start(bf16[32,56,1024]{2,1,0:T(8,128)(2,1)} %bitcast.134), calls=%async_computation.1 | async-start | bytes 7340032 | tf_op jit(solution)/shard_map/all_to_all | solution.py:146
  25.3 116.2 %copy-start.17 = (s32[128]{0:T(128)S(1)}, s32[128]{0:T(128)}, u32[]{:S(2)}) copy-start(s32[128]{0:T(128)} %param.15) | copy-start | bytes 1540
  25.4 139.6 %collective-permute-start.1 = (bf16[512,1024]{1,0:T(8,128)(2,1)}, bf16[512,1024]{1,0:T(8,128)(2,1)}, u32[]{:S(2)}, u32[]{:S(2)}) collective-permute-start(bf16[512,1024]{1,0:T(8,128)(2,1)} %reshape.260), channel_id=1, source_target_pairs={{0,2},{1,3},{2,4},{3,5},{4,6},{5,7},{6,0},{7,1},{8,10},{9,11},{10,... | collective-permute-start | bytes 3145736 | tf_op jit(solution)/shard_map/ppermute | solution.py:54
  26.9 142.8 %collective-permute-start.2 = (bf16[512,1024]{1,0:T(8,128)(2,1)}, bf16[512,1024]{1,0:T(8,128)(2,1)}, u32[]{:S(2)}, u32[]{:S(2)}) collective-permute-start(bf16[512,1024]{1,0:T(8,128)(2,1)} %reshape.260), channel_id=1, source_target_pairs={{0,6},{1,7},{2,0},{3,1},{4,2},{5,3},{6,4},{7,5},{8,14},{9,15},{10,... | collective-permute-start | bytes 3145736 | tf_op jit(solution)/shard_map/ppermute | solution.py:54
  28.7 144.7 %collective-permute-start = (bf16[512,1024]{1,0:T(8,128)(2,1)}, bf16[512,1024]{1,0:T(8,128)(2,1)}, u32[]{:S(2)}, u32[]{:S(2)}) collective-permute-start(bf16[512,1024]{1,0:T(8,128)(2,1)} %reshape.260), channel_id=1, source_target_pairs={{0,1},{1,0},{2,3},{3,2},{4,5},{5,4},{6,7},{7,6},{8,9},{9,8},{10,11... | collective-permute-start | bytes 3145736 | tf_op jit(solution)/shard_map/ppermute | solution.py:54
  141.5 5.0 %copy-start.2 = (bf16[128,4,8,128]{3,2,1,0:T(8,128)(2,1)}, bf16[128,4,8,128]{3,2,1,0:T(8,128)(2,1)S(1)}, u32[]{:S(2)}) copy-start(bf16[128,4,8,128]{3,2,1,0:T(8,128)(2,1)S(1)} %reshape.269) | copy-start | bytes 3145732
  141.6 5.3 %copy-start.5 = (bf16[16,2,32,128]{3,2,1,0:T(8,128)(2,1)S(1)}, bf16[16,2,32,128]{3,2,1,0:T(8,128)(2,1)}, u32[]{:S(2)}) copy-start(bf16[16,2,32,128]{3,2,1,0:T(8,128)(2,1)} %param.21) | copy-start | bytes 786436
  155.3 6.7 %copy-start.4 = (bf16[128,4,1024]{2,1,0:T(4,128)(2,1)S(1)}, bf16[128,4,1024]{2,1,0:T(4,128)(2,1)}, u32[]{:S(2)}) copy-start(bf16[128,4,1024]{2,1,0:T(4,128)(2,1)} %param.11) | copy-start | bytes 3145732
  155.3 41.8 %all-to-all-start = ((bf16[32,2,2,32,128]{4,1,3,2,0:T(2,128)(2,1)}), bf16[32,2,2,32,128]{4,1,3,2,0:T(2,128)(2,1)}, u32[]{:S(2)}, u32[]{:S(2)}) async-start(bf16[32,2,2,32,128]{4,1,3,2,0:T(2,128)(2,1)} %copy.92), calls=%async_computation | async-start | bytes 2097152 | tf_op jit(solution)/shard_map/all_to_all | solution.py:155
  166.8 16.3 %collective-permute-start.5 = (bf16[256,1024]{1,0:T(8,128)(2,1)}, bf16[256,1024]{1,0:T(8,128)(2,1)}, u32[]{:S(2)}, u32[]{:S(2)}) collective-permute-start(bf16[256,1024]{1,0:T(8,128)(2,1)} %slice.24), channel_id=1, source_target_pairs={{0,2},{1,3},{2,4},{3,5},{4,6},{5,7},{6,0},{7,1},{8,10},{9,11},{10,... | collective-permute-start | bytes 1572872 | tf_op jit(solution)/shard_map/ppermute | solution.py:54
  171.7 35.4 %collective-permute-start.6 = (bf16[256,1024]{1,0:T(8,128)(2,1)}, bf16[256,1024]{1,0:T(8,128)(2,1)}, u32[]{:S(2)}, u32[]{:S(2)}) collective-permute-start(bf16[256,1024]{1,0:T(8,128)(2,1)} %slice.25), channel_id=1, source_target_pairs={{0,6},{1,7},{2,0},{3,1},{4,2},{5,3},{6,4},{7,5},{8,14},{9,15},{10,... | collective-permute-start | bytes 1572872 | tf_op jit(solution)/shard_map/ppermute | solution.py:54
  173.4 57.0 %collective-permute-start.4 = (bf16[512,1024]{1,0:T(8,128)(2,1)}, bf16[512,1024]{1,0:T(8,128)(2,1)}, u32[]{:S(2)}, u32[]{:S(2)}) collective-permute-start(bf16[512,1024]{1,0:T(8,128)(2,1)} %collective-permute-done), channel_id=1, source_target_pairs={{0,6},{1,7},{2,0},{3,1},{4,2},{5,3},{6,4},{7,5},{8,14},{9,15},{10,... | collective-permute-start | bytes 3145736 | tf_op jit(solution)/shard_map/ppermute | solution.py:54
  175.0 78.8 %collective-permute-start.3 = (bf16[512,1024]{1,0:T(8,128)(2,1)}, bf16[512,1024]{1,0:T(8,128)(2,1)}, u32[]{:S(2)}, u32[]{:S(2)}) collective-permute-start(bf16[512,1024]{1,0:T(8,128)(2,1)} %collective-permute-done), channel_id=1, source_target_pairs={{0,2},{1,3},{2,4},{3,5},{4,6},{5,7},{6,0},{7,1},{8,10},{9,11},{10,... | collective-permute-start | bytes 3145736 | tf_op jit(solution)/shard_map/ppermute | solution.py:54
  197.2 29.3 %all-to-all-start.2 = ((f32[32,28,128]{2,1,0:T(8,128)}), f32[32,28,128]{2,1,0:T(8,128)S(1)}, u32[]{:S(2)}, u32[]{:S(2)}) async-start(f32[32,28,128]{2,1,0:T(8,128)} %reshape.265), calls=%async_computation.2 | async-start | bytes 1048576 | tf_op jit(solution)/shard_map/all_to_all | solution.py:167
  207.1 4.5 %copy-start.13 = (bf16[1024,2,128]{2,1,0:T(2,128)(2,1)S(1)}, bf16[1024,2,128]{2,1,0:T(2,128)(2,1)}, u32[]{:S(2)}) copy-start(bf16[1024,2,128]{2,1,0:T(2,128)(2,1)} %get-tuple-element.20) | copy-start | bytes 1572868
  209.0 36.3 %collective-permute-start.7 = (bf16[512,1024]{1,0:T(8,128)(2,1)}, bf16[512,1024]{1,0:T(8,128)(2,1)}, u32[]{:S(2)}, u32[]{:S(2)}) collective-permute-start(bf16[512,1024]{1,0:T(8,128)(2,1)} %constant_dynamic-update-slice_fusion), channel_id=1, source_target_pairs={{0,1},{1,0},{2,3},{3,2},{4,5},{5,4},{6,7},{7,6},{8,9},{9,8},{10,11... | collective-permute-start | bytes 3145736 | tf_op jit(solution)/shard_map/ppermute | solution.py:54
  211.6 2.6 copy-start.12
  226.6 18.7 %copy-start.11 = (bf16[1024,2,128]{2,1,0:T(2,128)(2,1)S(1)}, bf16[1024,2,128]{2,1,0:T(2,128)(2,1)}, u32[]{:S(2)}) copy-start(bf16[1024,2,128]{2,1,0:T(2,128)(2,1)} %get-tuple-element.24) | copy-start | bytes 1572868
  229.6 11.8 %collective-permute-start.8 = (f32[256,128]{1,0:T(8,128)S(1)}, f32[256,128]{1,0:T(8,128)S(1)}, u32[]{:S(2)}, u32[]{:S(2)}) collective-permute-start(f32[256,128]{1,0:T(8,128)S(1)} %reshape.267), channel_id=1, source_target_pairs={{0,1},{1,0},{2,3},{3,2},{4,5},{5,4},{6,7},{7,6},{8,9},{9,8},{10,11... | collective-permute-start | bytes 393224 | tf_op jit(solution)/shard_map/ppermute | solution.py:54
  233.1 18.5 %copy-start.16 = (pred[512,64]{0,1:T(8,128)(4,1)S(1)}, pred[512,64]{0,1:T(8,128)(4,1)}, u32[]{:S(2)}) copy-start(pred[512,64]{0,1:T(8,128)(4,1)} %iota_compare_fusion.3) | copy-start | bytes 98308
  241.4 6.5 %collective-permute-start.10 = (f32[256,128]{1,0:T(8,128)S(1)}, f32[256,128]{1,0:T(8,128)S(1)}, u32[]{:S(2)}, u32[]{:S(2)}) collective-permute-start(f32[256,128]{1,0:T(8,128)S(1)} %add.257), channel_id=1, source_target_pairs={{0,2},{1,3},{2,4},{3,5},{4,6},{5,7},{6,0},{7,1},{8,10},{9,11},{10,... | collective-permute-start | bytes 393224 | tf_op jit(solution)/shard_map/ppermute | solution.py:54
  241.8 8.2 %collective-permute-start.11 = (f32[256,128]{1,0:T(8,128)S(1)}, f32[256,128]{1,0:T(8,128)S(1)}, u32[]{:S(2)}, u32[]{:S(2)}) collective-permute-start(f32[256,128]{1,0:T(8,128)S(1)} %add.257), channel_id=1, source_target_pairs={{0,6},{1,7},{2,0},{3,1},{4,2},{5,3},{6,4},{7,5},{8,14},{9,15},{10,... | collective-permute-start | bytes 393224 | tf_op jit(solution)/shard_map/ppermute | solution.py:54
  244.7 6.5 %collective-permute-start.9 = (f32[256,128]{1,0:T(8,128)S(1)}, f32[256,128]{1,0:T(8,128)S(1)}, u32[]{:S(2)}, u32[]{:S(2)}) collective-permute-start(f32[256,128]{1,0:T(8,128)S(1)} %add.257), channel_id=1, source_target_pairs={{0,4},{1,5},{2,6},{3,7},{4,0},{5,1},{6,2},{7,3},{8,12},{9,13},{10,... | collective-permute-start | bytes 393224 | tf_op jit(solution)/shard_map/ppermute | solution.py:54
  251.6 2.2 copy-start.6
  251.6 2.2 copy-start.7
  251.6 2.2 copy-start.8
  251.6 2.2 copy-start.9
  251.6 2.2 copy-start.10
  253.9 6.6 %copy-start.3 = (bf16[128,4,8,128]{3,2,1,0:T(8,128)(2,1)S(1)}, bf16[128,4,8,128]{3,2,1,0:T(8,128)(2,1)}, u32[]{:S(2)}) copy-start(bf16[128,4,8,128]{3,2,1,0:T(8,128)(2,1)} %copy-done.2) | copy-start | bytes 3145732
  253.9 6.6 %copy-start.19 = (pred[4,4]{1,0:T(4,128)(4,1)S(1)}, pred[4,4]{1,0:T(4,128)(4,1)}, u32[]{:S(2)}) copy-start(pred[4,4]{1,0:T(4,128)(4,1)} %iota_compare_fusion.13) | copy-start | bytes 52
  256.4 9.8 %copy-start.14 = (f32[128,4,8]{2,1,0:T(4,128)S(1)}, f32[128,4,8]{2,1,0:T(4,128)}, u32[]{:S(2)}) copy-start(f32[128,4,8]{2,1,0:T(4,128)} %get-tuple-element.31) | copy-start | bytes 49156
  258.3 8.0 %copy-start.1 = (f32[128,48,4,8]{1,3,2,0:T(8,128)S(1)}, f32[128,48,4,8]{1,3,2,0:T(8,128)}, u32[]{:S(2)}) copy-start(f32[128,48,4,8]{1,3,2,0:T(8,128)} %get-tuple-element.32) | copy-start | bytes 2359300
  266.3 2.5 copy-start.18
  268.8 2.6 copy-start.15

commit v2 on v1

v2 whole, which is shorter than its diff:
```python
import functools

import jax
import jax.numpy as jnp
from jax import lax
from jax.experimental import pallas as pl
from jax.experimental.pallas import tpu as pltpu
from jax.sharding import PartitionSpec as P

HD = 128
BLK = 7
PAIR = 2
PAIR_ROWS = PAIR * BLK
SPAN = PAIR_ROWS + PAIR
GROUP = 8

masked_score = -1e30


def iota(shape, dim):
    return lax.broadcasted_iota(jnp.int32, shape, dim)


def total(value, axis):
    return jnp.sum(value, axis=axis, keepdims=True)


def place_kernel(steps, first_ref, request_ref, owner_ref, tokens_ref, sent_ref, wanted_ref, column_ref, fetch_ref, row_ref):
    part = sent_ref.shape[0]
    token_count = tokens_ref.shape[0]

    @pl.when(pl.program_id(0) == 0)
    def _():
        first = first_ref[...]
        blocks = first.shape[1]
        rows = request_ref.shape[1]
        pool = owner_ref.shape[1]
        owners = owner_ref[...]
        i, j = iota((blocks, blocks), 0), iota((blocks, blocks), 1)

        def down(value):
            return total(jnp.where(i == j, value, 0), 1)

        def across(value):
            return total(jnp.where(i == j, value, 0), 0)

        first_c = down(first)
        after_c = total(jnp.where(j == i + 1, first, 0), 1) + jnp.where(i[:, :1] == blocks - 1, rows, 0)
        after = across(after_c)
        adapter_c = total(jnp.where(iota((blocks, rows), 1) == first_c, request_ref[...], 0), 1)
        ids = iota((blocks, pool), 1)
        owner_c = total(jnp.where(ids == adapter_c, owners, 0), 1)
        slot_c = total(jnp.where((owners == owner_c) & (ids < adapter_c), 1, 0), 1)
        owner, slot = across(owner_c), across(slot_c)
        before = (owner == owner_c) & (j < i)
        turn_c = total(jnp.where(before, 1, 0), 1)
        offset_c = total(jnp.where(before, after - first, 0), 1)
        turn, offset = across(turn_c), across(offset_c)

        r, b = iota((rows, blocks), 0), iota((rows, blocks), 1)
        member = (first <= r) & (r < after)
        spot = r[:, :1] + total(jnp.where(member, owner * SPAN + offset - first, 0), 1)
        row_slot = total(jnp.where(member, slot, 0), 1)
        lanes = wanted_ref.shape[1]
        wanted = total(jnp.where(iota((rows, lanes), 1) == spot, row_slot, 0), 0)
        asked = owner_c * SPAN + PAIR_ROWS + turn_c
        wanted_ref[...] = wanted + total(jnp.where(iota((blocks, lanes), 1) == asked, slot_c, 0), 0)

        t = iota((blocks, token_count), 1)
        member = (first_c * steps <= t) & (t < after_c * steps)
        row_ref[...] = t[:1] + total(
            jnp.where(member, (owner_c * PAIR_ROWS + offset_c - first_c) * steps, 0), 0
        )
        t = iota((token_count, blocks), 0)
        member = (first * steps <= t) & (t < after * steps)
        column_ref[...] = t[:, :1] + total(
            jnp.where(member, (owner * PAIR_ROWS + offset - first) * steps, 0), 1
        )
        fetch_ref[...] = total(jnp.where(member, owner * PAIR + turn, 0), 1)

    spots = iota((part, token_count), 0) + pl.program_id(0) * part
    pick = jnp.where(spots == row_ref[...], 1.0, 0.0).astype(jnp.bfloat16)
    sent_ref[...] = jnp.dot(pick, tokens_ref[...], preferred_element_type=jnp.float32).astype(jnp.bfloat16)


def place(first, request, owners, tokens, steps, replicas):
    token_count, depth = tokens.shape
    sent_count = replicas * PAIR_ROWS * steps
    part = sent_count // 7
    whole = lambda shape: pl.BlockSpec(shape, lambda i: (0, 0))
    return pl.pallas_call(
        functools.partial(place_kernel, steps),
        grid=(7,),
        in_specs=[
            whole((1, first.shape[0])), whole((1, request.shape[0])), whole((1, owners.shape[0])),
            whole((token_count, depth)),
        ],
        out_specs=[
            pl.BlockSpec((part, depth), lambda i: (i, 0)), whole((1, replicas * SPAN)),
            whole((token_count, 1)), whole((token_count, 1)),
        ],
        out_shape=[
            jax.ShapeDtypeStruct((sent_count, depth), jnp.bfloat16),
            jax.ShapeDtypeStruct((1, replicas * SPAN), jnp.int32),
            jax.ShapeDtypeStruct((token_count, 1), jnp.int32),
            jax.ShapeDtypeStruct((token_count, 1), jnp.int32),
        ],
        scratch_shapes=[pltpu.VMEM((1, token_count), jnp.int32)],
        compiler_params=pltpu.CompilerParams(vmem_limit_bytes=24 * 2**20),
        name="place_rows",
    )(first[None], request[None], owners[None], tokens)


def rank_kernel(steps, slots_ref, rows_ref, maps_ref, out_ref):
    part = rows_ref.shape[0]
    width = out_ref.shape[1] // 2
    every = lax.dot_general(
        rows_ref[...], maps_ref[...], (((1,), (1,)), ((), ())), preferred_element_type=jnp.float32
    )
    i = iota((part, 1), 0)
    each = PAIR_ROWS * steps
    source = i // each
    lane = (source + pl.program_id(0) * (part // each)) * SPAN + (i - source * each) // steps
    lanes = slots_ref.shape[1]
    slot = total(jnp.where(iota((part, lanes), 1) == lane, slots_ref[...], 0), 1)
    two = jnp.zeros((part, 2 * width), jnp.float32)
    for pair in range(every.shape[1] // (2 * width)):
        two = jnp.where(slot // 2 == pair, every[:, pair * 2 * width:(pair + 1) * 2 * width], two)
    own = jnp.where(slot % 2 == 1, two[:, width:], two[:, :width])
    high = own.astype(jnp.bfloat16)
    low = (own - high.astype(jnp.float32)).astype(jnp.bfloat16)
    out_ref[...] = jnp.concatenate([high, low], axis=1)


def rank_products(slots, rows, maps, steps, width):
    count, depth = rows.shape
    part = count // 8
    return pl.pallas_call(
        functools.partial(rank_kernel, steps),
        grid=(8,),
        in_specs=[
            pl.BlockSpec(slots.shape, lambda i: (0, 0)), pl.BlockSpec((part, depth), lambda i: (i, 0)),
            pl.BlockSpec(maps.shape, lambda i: (0, 0)),
        ],
        out_specs=pl.BlockSpec((part, 2 * width), lambda i: (i, 0)),
        out_shape=jax.ShapeDtypeStruct((count, 2 * width), jnp.bfloat16),
        compiler_params=pltpu.CompilerParams(vmem_limit_bytes=24 * 2**20),
        cost_estimate=pl.CostEstimate(flops=2 * count * depth * maps.shape[0], bytes_accessed=6 * 2**20, transcendentals=0),
        name="rank_products",
    )(slots, rows, maps)


def collect_kernel(column_ref, returned_ref, out_ref):
    tokens, width = column_ref.shape[0], returned_ref.shape[1] // 2
    pick = jnp.where(iota((tokens, returned_ref.shape[0]), 1) == column_ref[...], 1.0, 0.0).astype(jnp.bfloat16)
    both = jnp.dot(pick, returned_ref[...], preferred_element_type=jnp.float32)
    value = both[:, :width] + both[:, width:]
    out_ref[...] = jnp.concatenate([value[: tokens // 2], value[tokens // 2:]], axis=1)


def collect(column, returned):
    tokens, width = column.shape[0], returned.shape[1]
    return pl.pallas_call(
        collect_kernel,
        out_shape=jax.ShapeDtypeStruct((tokens // 2, width), jnp.float32),
        compiler_params=pltpu.CompilerParams(vmem_limit_bytes=24 * 2**20),
        name="collect",
    )(column, returned)


def heads_first(value, heads):
    return jnp.concatenate([value[:, h * HD:(h + 1) * HD] for h in range(heads)], axis=0)


def cached_kernel(steps, bias_ref, queries_ref, keys_ref, values_ref, mixed_ref, weight_ref):
    heads = queries_ref.shape[1] // HD
    rows = keys_ref.shape[0] // GROUP if keys_ref.ndim == 3 else 1
    cache = keys_ref.shape[1]
    count = GROUP * steps
    for g in range(rows):
        query = heads_first(queries_ref[g * count:(g + 1) * count, :], heads)
        keys = keys_ref[g * GROUP:(g + 1) * GROUP].reshape(GROUP * cache, HD)
        values = values_ref[g * GROUP:(g + 1) * GROUP].reshape(GROUP * cache, HD)
        score = lax.dot_general(query, keys, (((1,), (1,)), ((), ())), preferred_element_type=jnp.float32)
        shape = score.shape
        own = (iota(shape, 0) // steps) % GROUP == iota(shape, 1) // cache
        score = jnp.where(own, score * HD ** -0.5 + bias_ref[g], masked_score)
        highest = jnp.max(score, axis=1, keepdims=True)
        exped = jnp.exp(score - highest)
        summed = total(exped, 1)
        mixed = jnp.dot(exped.astype(jnp.bfloat16), values, preferred_element_type=jnp.float32)
        mixed_ref[g] = mixed / summed
        weight_ref[g] = jnp.broadcast_to(highest + jnp.log(summed), mixed.shape)


def cached_attention(lengths, queries, keys, values, steps):
    rows, cache = keys.shape[:2]
    heads = queries.shape[1] // HD
    groups = rows // GROUP
    count = GROUP * steps * heads
    live = jnp.arange(cache, dtype=jnp.int32)[None, :] < lengths[:, None]
    bias = jnp.where(live, 0.0, masked_score).astype(jnp.float32).reshape(groups, 1, GROUP * cache)
    per = 2
    return pl.pallas_call(
        functools.partial(cached_kernel, steps),
        grid=(groups // per,),
        in_specs=[
            pl.BlockSpec((per, 1, GROUP * cache), lambda i: (i, 0, 0)),
            pl.BlockSpec((per * GROUP * steps, heads * HD), lambda i: (i, 0)),
            pl.BlockSpec((per * GROUP, cache, HD), lambda i: (i, 0, 0)),
            pl.BlockSpec((per * GROUP, cache, HD), lambda i: (i, 0, 0)),
        ],
        out_specs=[pl.BlockSpec((per, count, HD), lambda i: (i, 0, 0))] * 2,
        out_shape=[jax.ShapeDtypeStruct((groups, count, HD), jnp.float32)] * 2,
        compiler_params=pltpu.CompilerParams(vmem_limit_bytes=24 * 2**20),
        cost_estimate=pl.CostEstimate(flops=2**31, bytes_accessed=8 * 2**20, transcendentals=2**20),
        name="cached_attention",
    )(bias, queries, keys, values)


def finish_kernel(steps, rank, fetch_ref, a_ref, b_ref, c_ref, d_ref, maps_ref, base_ref, queries_ref, mixed_ref, weight_ref, fresh_ref, out_ref, held_ref):
    heads = queries_ref.shape[1] // HD
    count = GROUP * steps
    tokens = fetch_ref.shape[0]

    @pl.when(pl.program_id(0) == 0)
    def _():
        summed = (a_ref[...] + b_ref[...]) + (c_ref[...] + d_ref[...])
        width = summed.shape[1] // 2
        low = jnp.concatenate([summed[:, :width], summed[:, width:]], axis=0)
        fetch = fetch_ref[...]
        lanes = iota((tokens, 128), 1) // rank
        for side in range(2):
            four = jnp.concatenate([low[:, side * rank:(side + 1) * rank]] * (128 // rank), axis=1)
            spread = jnp.concatenate(
                [
                    jnp.where(fetch == lanes + k * (128 // rank), four, 0.0).astype(jnp.bfloat16)
                    for k in range(maps_ref.shape[1] // 128)
                ],
                axis=1,
            )
            delta = jnp.dot(spread, maps_ref[side], preferred_element_type=jnp.float32)
            new = base_ref[:, side * HD:(side + 1) * HD] + delta
            held_ref[:, side * HD:(side + 1) * HD] = new.astype(jnp.bfloat16)
        fresh_ref[...] = held_ref[...]

    for g in range(mixed_ref.shape[0]):
        start = pl.multiple_of((pl.program_id(0) * mixed_ref.shape[0] + g) * count, count)
        new = held_ref[pl.ds(start, count), :]
        query = heads_first(queries_ref[g * count:(g + 1) * count, :], heads)
        score = lax.dot_general(
            query, new[:, :HD], (((1,), (1,)), ((), ())), preferred_element_type=jnp.float32
        )
        i, j = iota(score.shape, 0), iota(score.shape, 1)
        seen = ((i // steps) % GROUP == j // steps) & (j % steps <= i % steps)
        score = jnp.where(seen, score * HD ** -0.5, masked_score)
        weight = weight_ref[g][:, :1]
        highest = jnp.maximum(jnp.max(score, axis=1, keepdims=True), weight)
        exped = jnp.exp(score - highest)
        cached = jnp.exp(weight - highest)
        summed = total(exped, 1) + cached
        probs = (exped / summed).astype(jnp.bfloat16)
        mixed = mixed_ref[g] * (cached / summed) + jnp.dot(
            probs, new[:, HD:], preferred_element_type=jnp.float32
        )
        mixed = mixed.astype(jnp.bfloat16)
        for h in range(heads):
            out_ref[g * count:(g + 1) * count, h * HD:(h + 1) * HD] = mixed[h * count:(h + 1) * count]


def finish(fetch, parts, maps, base, queries, mixed, weight, steps, rank):
    tokens, features = queries.shape
    groups, rows = mixed.shape[:2]
    per = 2
    whole = lambda x: pl.BlockSpec(x.shape, lambda i: (0,) * x.ndim)
    block = pl.BlockSpec((per * GROUP * steps, features), lambda i: (i, 0))
    return pl.pallas_call(
        functools.partial(finish_kernel, steps, rank),
        grid=(groups // per,),
        in_specs=[whole(fetch)] + [whole(p) for p in parts] + [whole(maps), whole(base), block]
        + [pl.BlockSpec((per, rows, HD), lambda i: (i, 0, 0))] * 2,
        out_specs=[pl.BlockSpec(base.shape, lambda i: (0, 0)), block],
        out_shape=[
            jax.ShapeDtypeStruct(base.shape, jnp.bfloat16),
            jax.ShapeDtypeStruct((tokens, features), jnp.bfloat16),
        ],
        scratch_shapes=[pltpu.VMEM(base.shape, jnp.bfloat16)],
        compiler_params=pltpu.CompilerParams(vmem_limit_bytes=32 * 2**20),
        name="finish",
    )(fetch, *parts, maps, base, queries, mixed, weight)


def shifted(value, dx, dy):
    pairs = [(t, ((t // 2 + dx) % 4) * 2 + ((t % 2) ^ dy)) for t in range(8)]
    return lax.ppermute(value, "tensor", pairs)


def exchange(value):
    me = lax.axis_index("replica")
    y, z, core = me >> 4, (me >> 1) & 7, me & 1
    rest = value.shape[1:]
    value = value.reshape((2, 8, 2) + rest)

    def send(piece, move):
        pairs = []
        for k in range(32):
            to_y, to_z, to_core = move(k >> 4, (k >> 1) & 7, k & 1)
            pairs.append((k, to_y * 16 + (to_z % 8) * 2 + to_core))
        return lax.ppermute(piece, "replica", pairs)

    pieces = [lax.dynamic_index_in_dim(value, (z + k) & 7, 1, keepdims=False) for k in range(8)]
    arrived = [pieces[0]] + [
        send(pieces[k], lambda a, b, c, k=k: (a, b + k, c)) for k in range(1, 8)
    ]
    turned = jnp.stack([arrived[(-k) % 8] for k in range(8)], axis=0)
    value = lax.dynamic_slice_in_dim(jnp.concatenate([turned, turned], axis=0), 8 - z, 8, 0)
    other = send(lax.dynamic_index_in_dim(value, 1 - y, 1, keepdims=False), lambda a, b, c: (1 - a, b, c))
    own = lax.dynamic_index_in_dim(value, y, 1, keepdims=False)
    value = jnp.where(y == 0, jnp.stack([own, other]), jnp.stack([other, own]))
    other = send(lax.dynamic_index_in_dim(value, 1 - core, 2, keepdims=False), lambda a, b, c: (a, b, 1 - c))
    own = lax.dynamic_index_in_dim(value, core, 2, keepdims=False)
    value = jnp.where(core == 0, jnp.stack([own, other], axis=2), jnp.stack([other, own], axis=2))
    return value.reshape((32,) + rest)


def project(tokens, key_value_weight):
    half = tokens.shape[0] // 2
    here = lax.axis_index("tensor")
    x, y = here >> 1, here & 1
    depth = tokens.shape[1]

    def product(piece, dx, dy):
        start = ((((x - dx) & 3) << 1) | (y ^ dy)) * depth
        part = lax.dynamic_slice_in_dim(key_value_weight, start, depth, 0)
        return jnp.dot(piece, part.reshape(depth, -1), preferred_element_type=jnp.float32)

    right = shifted(tokens, 1, 0)
    left = shifted(tokens, -1, 0)
    across = shifted(tokens, 0, 1)
    right_across = shifted(across, 1, 0)
    left_across = shifted(across, -1, 0)
    far = jnp.concatenate([shifted(right[:half], 1, 0), shifted(left[half:], -1, 0)], axis=0)
    far_across = shifted(far, 0, 1)
    base = product(tokens, 0, 0) + product(across, 0, 1)
    base = base + product(right, 1, 0) + product(left, -1, 0)
    base = base + product(right_across, 1, 1) + product(left_across, -1, 1)
    return base + product(far, 2, 0) + product(far_across, 2, 1)


def per_device(
    hidden,
    queries,
    key_cache_rows,
    value_cache_rows,
    lengths,
    request_adapter,
    block_first_row,
    adapter_owner_group,
    key_value_weight,
    adapter_down_weight,
    adapter_up_weight,
):
    row_count, steps, depth = hidden.shape
    replicas = lax.axis_size("replica")
    token_count = row_count * steps
    held, sides, rank = adapter_down_weight.shape[:3]
    tokens = hidden.reshape(token_count, depth)

    sent, wanted, column, fetch = place(
        block_first_row, request_adapter, adapter_owner_group, tokens, steps, replicas
    )
    received = lax.all_to_all(
        sent.reshape(replicas, PAIR_ROWS * steps, depth), "replica", split_axis=0, concat_axis=0, tiled=True
    ).reshape(-1, depth)
    wanted = exchange(wanted.reshape(replicas, SPAN))
    up_asked = adapter_up_weight[wanted[:, PAIR_ROWS:]].reshape(replicas, -1, HD)
    up = exchange(up_asked).reshape(replicas * PAIR, sides, rank, HD)
    up = up.transpose(1, 0, 2, 3).reshape(sides, replicas * PAIR * rank, HD)

    base = project(tokens, key_value_weight)
    query_tokens = queries.reshape(token_count, -1)
    mixed, weight = cached_attention(lengths, query_tokens, key_cache_rows, value_cache_rows, steps)

    products = rank_products(
        wanted.reshape(1, -1), received, adapter_down_weight.reshape(held * sides * rank, depth), steps, sides * rank
    )
    returned = lax.all_to_all(
        products.reshape(replicas, PAIR_ROWS * steps, -1), "replica", split_axis=0, concat_axis=0, tiled=True
    ).reshape(products.shape)
    mine = collect(column, returned)
    mine = mine + shifted(mine, 0, 1)
    parts = (mine, shifted(mine, 2, 0), shifted(mine, 1, 0), shifted(mine, -1, 0))
    fresh, attended = finish(fetch, parts, up, base, query_tokens, mixed, weight, steps, rank)
    return (
        fresh.reshape(row_count, steps, sides, HD),
        attended.reshape(row_count, steps, -1),
    )


def solution(mesh):
    placed = (
        P("replica", None, "tensor"),
        P("replica", None, "tensor"),
        P("replica", None, "tensor"),
        P("replica", None, "tensor"),
        P("replica"),
        P("replica"),
        P("replica"),
        P(),
        P(None, None, "tensor"),
        P("replica", None, None, "tensor"),
        P("replica", None, None, "tensor"),
    )
    return jax.shard_map(
        per_device,
        mesh=mesh,
        in_specs=placed,
        out_specs=(P("replica", None, None, "tensor"), P("replica", None, "tensor")),
        check_vma=False,
    )
```

time: 275 us -> 285 us (1.036)
  blocking collectives: 110 us -> 0 us
  waiting for transfers between devices: 23.9 us -> 117 us
  starting transfers between devices: 42 us -> 82.4 us
  Pallas kernels: 0 us -> 31.6 us
  matrix products: 46.1 us -> 16.8 us
  local copies, waits for them, and re-layouts: 40.6 us -> 29.9 us
  other arithmetic: 9.81 us -> 3.98 us
    all_gather x1 -> x0, blocking collectives: 110 us -> none  [per_device(): lax.all_gather(jnp.concatenate([place_slot, fetch_slot]), 'replica', axis=0)]
    ppermute x0 -> x18, waiting for transfers between devices: none -> 101 us  [send(): return lax.ppermute(piece, 'replica', pairs)]
    ppermute x0 -> x18, starting transfers between devices: none -> 50 us  [send(): return lax.ppermute(piece, 'replica', pairs)]
    pallas_call x0 -> x5, Pallas kernels: none -> 31.6 us  [the longest x1 10.6 us: rank_products(): pl.pallas_call(functools.partial(rank_kernel, steps), grid=(8,), in_specs...]
    dot_general x15 -> x8, matrix products: 46.1 us -> 16.8 us  [product(): jnp.dot(piece, part.reshape(depth, -1), preferred_element_type=jnp.float32)]
    all_to_all x3 -> x2, starting transfers between devices: 27.4 us -> 13.4 us  [the longest x1 7.1 us: per_device(): lax.all_to_all(products.reshape(replicas, PAIR_ROWS * steps, -1), 'replic...]
    ppermute x12, waiting for transfers between devices: 17.5 us -> 7.77 us  [shifted(): return lax.ppermute(value, 'tensor', pairs)]
    unnamed x42 -> x87, local copies, waits for them, and re-layouts: 4.16 us -> 11.6 us
  transfers between devices with their start and end apart: 15 -> 32, of which waited for: 5 -> 15; matrix products, arithmetic and copies ran while one was open for 23% -> 13% of each run, Pallas kernels for 0% -> 8%
where the time goes in v2:
time: 285 us; the launch traced here: 283 us
  waiting for transfers between devices  117 us (41%)
  starting transfers between devices  82.4 us (29%)
  Pallas kernels  31.6 us (11%)
  local copies, waits for them, and re-layouts  29.9 us (10%)
  matrix products  16.8 us (6%)
  other arithmetic  3.98 us (1%)
    ppermute x18, waiting for transfers between devices, send(): return lax.ppermute(piece, 'replica', pairs)  101 us
    ppermute x18, starting transfers between devices, send(): return lax.ppermute(piece, 'replica', pairs)  50 us
    ppermute x12, starting transfers between devices, shifted(): return lax.ppermute(value, 'tensor', pairs)  19 us
    dot_general x8, matrix products, product(): jnp.dot(piece, part.reshape(depth, -1), preferred_element_type=jnp.float32)  16.8 us
    unnamed x87, local copies, waits for them, and re-layouts  11.6 us
    pallas_call x1, Pallas kernels, rank_products(): pl.pallas_call(functools.partial(rank_kernel, steps), grid=(8,), in_specs...  10.6 us
    pallas_call x1, Pallas kernels, finish(): pl.pallas_call(functools.partial(finish_kernel, steps, rank), grid=(group...  10.2 us
    all_to_all x1, waiting for transfers between devices, per_device(): lax.all_to_all(products.reshape(replicas, PAIR_ROWS * steps, -1), 'replic...  8.61 us
  transfers between devices with their start and end apart: 32, of which 15 were waited for; matrix products, arithmetic and copies ran while one was open for 13% of the time, Pallas kernels for 8%

profile of v2, /device:TPU:32, one launch (start us, length us, event | category | flops | bytes accessed | tf_op | source)
XLA Modules:
  0.0 282.9 jit_solution(8582835908045099112)
XLA Ops:
  0.7 1.4 reshape.134.tokens_ref
  2.1 1.7 collective-permute-start.22
  3.7 2.8 collective-permute-start.24
  6.5 4.0 %place_rows.1 = (bf16[1792,1024]{1,0:T(8,128)(2,1)S(1)}, s32[1,512]{1,0:T(1,128)S(1)}, s32[512,1]{1,0:T(8,128)S(1)}, s32[512,1]{1,0:T(8,128)S(1)}) custom-call(s32[1,32]{1,0:T(1,128)S(1)} %bitcast.174, s32[1,128]{1,0:T(1,128)S(1)} %bitcast.175, s32[1,512]{1,0:T(1,128)S(1)} %bitcast.173, bf16[512,1024]{1,0:T(8,128)(2,1)S(1)} %reshape.134.tokens_ref), custom_call_target="tpu_custom_call" | custom-call | tf_op jit(solution)/shard_map/place_rows/pallas_call | solution.py:91
  10.5 1.8 copy-done.1
  14.5 6.3 %collective-permute-start.1 = (s32[2,2,16]{2,1,0:T(2,128)S(1)}, s32[2,2,16]{2,1,0:T(2,128)S(1)}, u32[]{:S(2)}, u32[]{:S(2)}) collective-permute-start(s32[2,2,16]{2,1,0:T(2,128)S(1)} %get-tuple-element.46), channel_id=1, source_target_pairs={{0,96},{8,104},{16,112},{24,120},{32,0},{40,8},{48,16},{56,24},{64... | collective-permute-start | bytes 776 | tf_op jit(solution)/shard_map/ppermute | solution.py:309
  20.8 6.3 %all-to-all-start = ((bf16[32,56,1024]{2,1,0:T(8,128)(2,1)}), bf16[32,56,1024]{2,1,0:T(8,128)(2,1)}, u32[]{:S(2)}, u32[]{:S(2)}) async-start(bf16[32,56,1024]{2,1,0:T(8,128)(2,1)} %bitcast.171), calls=%async_computation | async-start | bytes 7340032 | tf_op jit(solution)/shard_map/all_to_all | solution.py:372
  27.2 3.7 %collective-permute-start.2 = (s32[2,2,16]{2,1,0:T(2,128)S(1)}, s32[2,2,16]{2,1,0:T(2,128)S(1)}, u32[]{:S(2)}, u32[]{:S(2)}) collective-permute-start(s32[2,2,16]{2,1,0:T(2,128)S(1)} %get-tuple-element.45), channel_id=1, source_target_pairs={{0,80},{8,88},{16,96},{24,104},{32,112},{40,120},{48,0},{56,8},{64... | collective-permute-start | bytes 776 | tf_op jit(solution)/shard_map/ppermute | solution.py:309
  30.9 2.4 collective-permute-start.3
  33.3 73.0 %collective-permute-done.2 = s32[2,2,16]{2,1,0:T(2,128)S(1)} collective-permute-done((s32[2,2,16]{2,1,0:T(2,128)S(1)}, s32[2,2,16]{2,1,0:T(2,128)S(1)}, u32[]{:S(2)}, u32[]{:S(2)}) %collective-permute-start.2) | collective-permute-done | bytes 288 | tf_op jit(solution)/shard_map/ppermute | solution.py:309
  106.3 6.2 %collective-permute-start.4 = (s32[2,2,16]{2,1,0:T(2,128)S(1)}, s32[2,2,16]{2,1,0:T(2,128)S(1)}, u32[]{:S(2)}, u32[]{:S(2)}) collective-permute-start(s32[2,2,16]{2,1,0:T(2,128)S(1)} %get-tuple-element.43), channel_id=1, source_target_pairs={{0,48},{8,56},{16,64},{24,72},{32,80},{40,88},{48,96},{56,104},{64... | collective-permute-start | bytes 776 | tf_op jit(solution)/shard_map/ppermute | solution.py:309
  112.5 2.1 collective-permute-start.5
  114.9 3.3 %collective-permute-done.5 = s32[2,2,16]{2,1,0:T(2,128)S(1)} collective-permute-done((s32[2,2,16]{2,1,0:T(2,128)S(1)}, s32[2,2,16]{2,1,0:T(2,128)S(1)}, u32[]{:S(2)}, u32[]{:S(2)}) %collective-permute-start.5) | collective-permute-done | bytes 288 | tf_op jit(solution)/shard_map/ppermute | solution.py:309
  119.3 3.0 %collective-permute-start.7 = (s32[8,2,16]{2,1,0:T(2,128)S(1)}, s32[8,2,16]{2,1,0:T(2,128)S(1)}, u32[]{:S(2)}, u32[]{:S(2)}) collective-permute-start(s32[8,2,16]{2,1,0:T(2,128)S(1)} %get-tuple-element.38), channel_id=1, source_target_pairs={{0,128},{8,136},{16,144},{24,152},{32,160},{40,168},{48,176},{56,1... | collective-permute-start | bytes 3080 | tf_op jit(solution)/shard_map/ppermute | solution.py:309
  122.3 2.3 collective-permute-done.7
  124.7 1.1 collective-permute-done.8
  127.6 3.2 %collective-permute-start.13 = (bf16[2,2,128,128]{3,2,1,0:T(8,128)(2,1)S(1)}, bf16[2,2,128,128]{3,2,1,0:T(8,128)(2,1)S(1)}, u32[]{:S(2)}, u32[]{:S(2)}) collective-permute-start(bf16[2,2,128,128]{3,2,1,0:T(8,128)(2,1)S(1)} %get-tuple-element.36), channel_id=1, source_target_pairs={{0,112},{8,120},{16,0},{24,8},{32,16},{40,24},{48,32},{56,40},{64,... | collective-permute-start | bytes 393224 | tf_op jit(solution)/shard_map/ppermute | solution.py:309
  130.9 5.5 %constant_dynamic-slice_fusion.3 = (bf16[1024,2,128]{2,1,0:T(2,128)(2,1)}, bf16[1024,2,128]{2,1,0:T(2,128)(2,1)}, bf16[1024,2,128]{2,1,0:T(2,128)(2,1)}, bf16[10...) fusion(bf16[8192,2,128]{2,1,0:T(2,128)(2,1)} %param.19, ...), kind=kLoop, calls=%fused_computation.85 | loop fusion | bytes 8388640 | tf_op jit(solution)/shard_map/dynamic_slice | solution.py:334
  136.8 1.4 collective-permute-start.14
  138.2 3.9 %collective-permute-start.15 = (bf16[2,2,128,128]{3,2,1,0:T(8,128)(2,1)}, bf16[2,2,128,128]{3,2,1,0:T(8,128)(2,1)S(1)}, u32[]{:S(2)}, u32[]{:S(2)}) collective-permute-start(bf16[2,2,128,128]{3,2,1,0:T(8,128)(2,1)} %get-tuple-element.34), channel_id=1, source_target_pairs={{0,80},{8,88},{16,96},{24,104},{32,112},{40,120},{48,0},{56,8},{64... | collective-permute-start | bytes 393224 | tf_op jit(solution)/shard_map/ppermute | solution.py:309
  142.1 5.8 %collective-permute-done.14 = bf16[2,2,128,128]{3,2,1,0:T(8,128)(2,1)S(1)} collective-permute-done((bf16[2,2,128,128]{3,2,1,0:T(8,128)(2,1)}, bf16[2,2,128,128]{3,2,1,0:T(8,128)(2,1)S(1)}, u32[]{:S(2)}, u32[]{:S(2)}) %collective-permute-start.14) | collective-permute-done | bytes 131104 | tf_op jit(solution)/shard_map/ppermute | solution.py:309
  148.0 2.7 collective-permute-start.16
  150.7 3.1 %collective-permute-done.15 = bf16[2,2,128,128]{3,2,1,0:T(8,128)(2,1)S(1)} collective-permute-done((bf16[2,2,128,128]{3,2,1,0:T(8,128)(2,1)}, bf16[2,2,128,128]{3,2,1,0:T(8,128)(2,1)S(1)}, u32[]{:S(2)}, u32[]{:S(2)}) %collective-permute-start.15) | collective-permute-done | bytes 131104 | tf_op jit(solution)/shard_map/ppermute | solution.py:309
  153.7 2.3 collective-permute-start.17
  156.1 3.0 %collective-permute-done.16 = bf16[2,2,128,128]{3,2,1,0:T(8,128)(2,1)S(1)} collective-permute-done((bf16[2,2,128,128]{3,2,1,0:T(8,128)(2,1)}, bf16[2,2,128,128]{3,2,1,0:T(8,128)(2,1)S(1)}, u32[]{:S(2)}, u32[]{:S(2)}) %collective-permute-start.16) | collective-permute-done | bytes 131104 | tf_op jit(solution)/shard_map/ppermute | solution.py:309
  159.1 4.7 %collective-permute-start.18 = (bf16[2,2,128,128]{3,2,1,0:T(8,128)(2,1)S(1)}, bf16[2,2,128,128]{3,2,1,0:T(8,128)(2,1)S(1)}, u32[]{:S(2)}, u32[]{:S(2)}) collective-permute-start(bf16[2,2,128,128]{3,2,1,0:T(8,128)(2,1)S(1)} %get-tuple-element.31), channel_id=1, source_target_pairs={{0,32},{8,40},{16,48},{24,56},{32,64},{40,72},{48,80},{56,88},{64,... | collective-permute-start | bytes 393224 | tf_op jit(solution)/shard_map/ppermute | solution.py:309
  163.8 3.3 %collective-permute-done.17 = bf16[2,2,128,128]{3,2,1,0:T(8,128)(2,1)S(1)} collective-permute-done((bf16[2,2,128,128]{3,2,1,0:T(8,128)(2,1)S(1)}, bf16[2,2,128,128]{3,2,1,0:T(8,128)(2,1)S(1)}, u32[]{:S(2)}, u32[]{:S(2)}) %collective-permute-start.17) | collective-permute-done | bytes 131104 | tf_op jit(solution)/shard_map/ppermute | solution.py:309
  167.1 4.6 %collective-permute-start.19 = (bf16[2,2,128,128]{3,2,1,0:T(8,128)(2,1)S(1)}, bf16[2,2,128,128]{3,2,1,0:T(8,128)(2,1)S(1)}, u32[]{:S(2)}, u32[]{:S(2)}) collective-permute-start(bf16[2,2,128,128]{3,2,1,0:T(8,128)(2,1)S(1)} %get-tuple-element.30), channel_id=1, source_target_pairs={{0,16},{8,24},{16,32},{24,40},{32,48},{40,56},{48,64},{56,72},{64,... | collective-permute-start | bytes 393224 | tf_op jit(solution)/shard_map/ppermute | solution.py:309
  172.3 4.0 %collective-permute-done.19 = bf16[2,2,128,128]{3,2,1,0:T(8,128)(2,1)S(1)} collective-permute-done((bf16[2,2,128,128]{3,2,1,0:T(8,128)(2,1)S(1)}, bf16[2,2,128,128]{3,2,1,0:T(8,128)(2,1)S(1)}, u32[]{:S(2)}, u32[]{:S(2)}) %collective-permute-start.19) | collective-permute-done | bytes 131104 | tf_op jit(solution)/shard_map/ppermute | solution.py:309
  176.6 1.1 dynamic-slice_bitcast_fusion.2
  177.6 3.1 %collective-permute-start.20 = (bf16[8,2,128,128]{3,2,1,0:T(8,128)(2,1)}, bf16[8,2,128,128]{3,2,1,0:T(8,128)(2,1)}, u32[]{:S(2)}, u32[]{:S(2)}) collective-permute-start(bf16[8,2,128,128]{3,2,1,0:T(8,128)(2,1)} %get-tuple-element.27), channel_id=1, source_target_pairs={{0,128},{8,136},{16,144},{24,152},{32,160},{40,168},{48,176},{56,1... | collective-permute-start | bytes 1572872 | tf_op jit(solution)/shard_map/ppermute | solution.py:309
  180.8 1.3 reshape.149.queries_ref
  182.1 1.4 copy-done.14
  183.5 1.4 copy-done.15
  184.9 6.0 %cached_attention.1 = (f32[16,256,128]{2,1,0:T(8,128)S(1)}, f32[16,256,128]{2,1,0:T(8,128)S(1)}) custom-call(f32[16,1,384]{2,1,0:T(1,128)S(1)} %compare_select_fusion.bias_ref, bf16[512,1024]{1,0:T(8,128)(2,1)S(1)} %reshape.149.queries_ref, bf16[128,48,128]{2,1,0:T(8,128)(2,1)S(1)} %copy-done.14, bf16[128,48,128]{2,1,0:T(8,128)(2,1)S(1)} %copy-done.15), custom_call_target="tpu_custom_call" | custom-call | flops 2147483648 | bytes 8388608 | tf_op jit(solution)/shard_map/cached_attention/pallas_call | solution.py:204
  190.9 1.4 copy-done.2
  192.3 1.3 copy-done.4
  193.6 1.2 fusion.23
  195.0 1.8 maximum_select_fusion
  196.7 1.1 constant_dynamic-slice_fusion.8
  197.9 1.2 slice.15
  199.9 1.1 slice.16
  200.9 2.6 collective-permute-start.28
  203.5 2.0 collective-permute-start.26
  205.5 2.5 fusion.16
  208.0 1.7 convolution_add_fusion.2
  209.7 5.4 %collective-permute-done.27 = bf16[256,1024]{1,0:T(8,128)(2,1)S(1)} collective-permute-done((bf16[256,1024]{1,0:T(8,128)(2,1)S(1)}, bf16[256,1024]{1,0:T(8,128)(2,1)S(1)}, u32[]{:S(2)}, u32[]{:S(2)}) %collective-permute-start.27) | collective-permute-done | bytes 524320 | tf_op jit(solution)/shard_map/ppermute | solution.py:295
  216.9 1.6 copy-done.13
  218.5 10.6 %rank_products.1 = bf16[1792,128]{1,0:T(8,128)(2,1)} custom-call(s32[1,512]{1,0:T(1,128)S(1)} %select_n.168.slots_ref, bf16[1792,1024]{1,0:T(8,128)(2,1)} %bitcast.24.rows_ref, bf16[1024,1024]{1,0:T(8,128)(2,1)S(1)} %bitcast.176), custom_call_target="tpu_custom_call" | custom-call | flops 3758096384 | bytes 6291456 | tf_op jit(solution)/shard_map/rank_products/pallas_call | solution.py:138
  229.1 7.1 %all-to-all-start.1 = ((bf16[32,56,128]{2,1,0:T(8,128)(2,1)}), bf16[32,56,128]{2,1,0:T(8,128)(2,1)S(1)}, u32[]{:S(2)}, u32[]{:S(2)}) async-start(bf16[32,56,128]{2,1,0:T(8,128)(2,1)} %bitcast.26), calls=%async_computation.1 | async-start | bytes 917504 | tf_op jit(solution)/shard_map/all_to_all | solution.py:387
  236.2 2.8 fusion
  239.0 1.4 maximum_select_fusion.1
  240.5 2.5 fusion.8
  243.0 2.5 fusion.11
  245.4 8.6 %all-to-all-done.1 = bf16[32,56,128]{2,1,0:T(8,128)(2,1)S(1)} async-done(((bf16[32,56,128]{2,1,0:T(8,128)(2,1)}), bf16[32,56,128]{2,1,0:T(8,128)(2,1)S(1)}, u32[]{:S(2)}, u32[]{:S(2)}) %all-to-all-start.1) | async-done | bytes 458784 | tf_op jit(solution)/shard_map/all_to_all | solution.py:387
  254.9 1.9 collective-permute-start.9
  256.8 1.8 fusion.5
  258.7 1.3 collective-permute-done.9
  260.0 3.8 %collective-permute-start.10 = (f32[256,128]{1,0:T(8,128)S(1)}, f32[256,128]{1,0:T(8,128)S(1)}, u32[]{:S(2)}, u32[]{:S(2)}) collective-permute-start(f32[256,128]{1,0:T(8,128)S(1)} %add.190.a_ref), channel_id=1, source_target_pairs={{0,4},{1,5},{2,6},{3,7},{4,0},{5,1},{6,2},{7,3},{8,12},{9,13},{10,... | collective-permute-start | bytes 393224 | tf_op jit(solution)/shard_map/ppermute | solution.py:295
  264.4 2.6 collective-permute-start.12
  267.1 1.8 fusion.4.base_ref
  268.9 1.1 collective-permute-done.11.c_ref
  270.0 10.2 %finish.1 = (bf16[512,256]{1,0:T(8,128)(2,1)S(1)}, bf16[512,1024]{1,0:T(8,128)(2,1)S(1)}) custom-call(s32[512,1]{1,0:T(8,128)S(1)} %copy-done.9, f32[256,128]{1,0:T(8,128)S(1)} %add.190.a_ref, f32[256,128]{1,0:T(8,128)S(1)} %collective-permute-done.10.b_ref, f32[256,128]{1,0:T(8,128)S(1)} %collective-permute-done.11.c_ref, ...), custom_call_target="tpu_custom_call" | custom-call | tf_op jit(solution)/shard_map/finish/pallas_call | solution.py:277
  280.9 1.2 reshape.151
  (136 shorter events, 12.6 us)
Async XLA Ops:
  0.6 125.4 %copy-start = (bf16[16,2,32,128]{3,2,1,0:T(8,128)(2,1)S(1)}, bf16[16,2,32,128]{3,2,1,0:T(8,128)(2,1)}, u32[]{:S(2)}) copy-start(bf16[16,2,32,128]{3,2,1,0:T(8,128)(2,1)} %param.21) | copy-start | bytes 786436
  0.6 5.9 %copy-start.11 = (s32[32]{0:T(128)S(1)}, s32[32]{0:T(128)}, u32[]{:S(2)}) copy-start(s32[32]{0:T(128)} %param.17) | copy-start | bytes 388
  0.7 5.9 %copy-start.12 = (s32[128]{0:T(128)S(1)}, s32[128]{0:T(128)}, u32[]{:S(2)}) copy-start(s32[128]{0:T(128)} %param.16) | copy-start | bytes 1540
  0.7 5.8 %copy-start.10 = (s32[512]{0:T(512)S(1)}, s32[512]{0:T(512)}, u32[]{:S(2)}) copy-start(s32[512]{0:T(512)} %param.18) | copy-start | bytes 6148
  2.1 201.4 %collective-permute-start.22 = (bf16[512,1024]{1,0:T(8,128)(2,1)S(1)}, bf16[512,1024]{1,0:T(8,128)(2,1)}, u32[]{:S(2)}, u32[]{:S(2)}) collective-permute-start(bf16[512,1024]{1,0:T(8,128)(2,1)S(1)} %reshape.134.tokens_ref), channel_id=1, source_target_pairs={{0,1},{1,0},{2,3},{3,2},{4,5},{5,4},{6,7},{7,6},{8,9},{9,8},{10,11... | collective-permute-start | bytes 3145736 | tf_op jit(solution)/shard_map/ppermute | solution.py:295
  3.7 196.1 %collective-permute-start.24 = (bf16[512,1024]{1,0:T(8,128)(2,1)S(1)}, bf16[512,1024]{1,0:T(8,128)(2,1)}, u32[]{:S(2)}, u32[]{:S(2)}) collective-permute-start(bf16[512,1024]{1,0:T(8,128)(2,1)S(1)} %reshape.134.tokens_ref), channel_id=1, source_target_pairs={{0,6},{1,7},{2,0},{3,1},{4,2},{5,3},{6,4},{7,5},{8,14},{9,15},{10,... | collective-permute-start | bytes 3145736 | tf_op jit(solution)/shard_map/ppermute | solution.py:295
  6.5 191.4 %collective-permute-start.23 = (bf16[512,1024]{1,0:T(8,128)(2,1)S(1)}, bf16[512,1024]{1,0:T(8,128)(2,1)}, u32[]{:S(2)}, u32[]{:S(2)}) collective-permute-start(bf16[512,1024]{1,0:T(8,128)(2,1)S(1)} %reshape.134.tokens_ref), channel_id=1, source_target_pairs={{0,2},{1,3},{2,4},{3,5},{4,6},{5,7},{6,0},{7,1},{8,10},{9,11},{10,... | collective-permute-start | bytes 3145736 | tf_op jit(solution)/shard_map/ppermute | solution.py:295
  10.5 1.8 copy-start.1
  12.4 0.7 copy-start.8
  14.4 12.9 %collective-permute-start = (s32[2,2,16]{2,1,0:T(2,128)S(1)}, s32[2,2,16]{2,1,0:T(2,128)S(1)}, u32[]{:S(2)}, u32[]{:S(2)}) collective-permute-start(s32[2,2,16]{2,1,0:T(2,128)S(1)} %get-tuple-element.47), channel_id=1, source_target_pairs={{0,112},{8,120},{16,0},{24,8},{32,16},{40,24},{48,32},{56,40},{64,... | collective-permute-start | bytes 776 | tf_op jit(solution)/shard_map/ppermute | solution.py:309
  14.5 16.3 %collective-permute-start.1 = (s32[2,2,16]{2,1,0:T(2,128)S(1)}, s32[2,2,16]{2,1,0:T(2,128)S(1)}, u32[]{:S(2)}, u32[]{:S(2)}) collective-permute-start(s32[2,2,16]{2,1,0:T(2,128)S(1)} %get-tuple-element.46), channel_id=1, source_target_pairs={{0,96},{8,104},{16,112},{24,120},{32,0},{40,8},{48,16},{56,24},{64... | collective-permute-start | bytes 776 | tf_op jit(solution)/shard_map/ppermute | solution.py:309
  20.8 196.1 %all-to-all-start = ((bf16[32,56,1024]{2,1,0:T(8,128)(2,1)}), bf16[32,56,1024]{2,1,0:T(8,128)(2,1)}, u32[]{:S(2)}, u32[]{:S(2)}) async-start(bf16[32,56,1024]{2,1,0:T(8,128)(2,1)} %bitcast.171), calls=%async_computation | async-start | bytes 7340032 | tf_op jit(solution)/shard_map/all_to_all | solution.py:372
  27.2 79.0 %collective-permute-start.2 = (s32[2,2,16]{2,1,0:T(2,128)S(1)}, s32[2,2,16]{2,1,0:T(2,128)S(1)}, u32[]{:S(2)}, u32[]{:S(2)}) collective-permute-start(s32[2,2,16]{2,1,0:T(2,128)S(1)} %get-tuple-element.45), channel_id=1, source_target_pairs={{0,80},{8,88},{16,96},{24,104},{32,112},{40,120},{48,0},{56,8},{64... | collective-permute-start | bytes 776 | tf_op jit(solution)/shard_map/ppermute | solution.py:309
  30.9 81.6 %collective-permute-start.3 = (s32[2,2,16]{2,1,0:T(2,128)S(1)}, s32[2,2,16]{2,1,0:T(2,128)S(1)}, u32[]{:S(2)}, u32[]{:S(2)}) collective-permute-start(s32[2,2,16]{2,1,0:T(2,128)S(1)} %get-tuple-element.44), channel_id=1, source_target_pairs={{0,64},{8,72},{16,80},{24,88},{32,96},{40,104},{48,112},{56,120},{... | collective-permute-start | bytes 776 | tf_op jit(solution)/shard_map/ppermute | solution.py:309
  106.3 8.3 %collective-permute-start.4 = (s32[2,2,16]{2,1,0:T(2,128)S(1)}, s32[2,2,16]{2,1,0:T(2,128)S(1)}, u32[]{:S(2)}, u32[]{:S(2)}) collective-permute-start(s32[2,2,16]{2,1,0:T(2,128)S(1)} %get-tuple-element.43), channel_id=1, source_target_pairs={{0,48},{8,56},{16,64},{24,72},{32,80},{40,88},{48,96},{56,104},{64... | collective-permute-start | bytes 776 | tf_op jit(solution)/shard_map/ppermute | solution.py:309
  112.5 5.7 %collective-permute-start.5 = (s32[2,2,16]{2,1,0:T(2,128)S(1)}, s32[2,2,16]{2,1,0:T(2,128)S(1)}, u32[]{:S(2)}, u32[]{:S(2)}) collective-permute-start(s32[2,2,16]{2,1,0:T(2,128)S(1)} %get-tuple-element.42), channel_id=1, source_target_pairs={{0,32},{8,40},{16,48},{24,56},{32,64},{40,72},{48,80},{56,88},{64,... | collective-permute-start | bytes 776 | tf_op jit(solution)/shard_map/ppermute | solution.py:309
  114.6 4.6 %collective-permute-start.6 = (s32[2,2,16]{2,1,0:T(2,128)S(1)}, s32[2,2,16]{2,1,0:T(2,128)S(1)}, u32[]{:S(2)}, u32[]{:S(2)}) collective-permute-start(s32[2,2,16]{2,1,0:T(2,128)S(1)} %get-tuple-element.41), channel_id=1, source_target_pairs={{0,16},{8,24},{16,32},{24,40},{32,48},{40,56},{48,64},{56,72},{64,... | collective-permute-start | bytes 776 | tf_op jit(solution)/shard_map/ppermute | solution.py:309
  119.3 5.2 %collective-permute-start.7 = (s32[8,2,16]{2,1,0:T(2,128)S(1)}, s32[8,2,16]{2,1,0:T(2,128)S(1)}, u32[]{:S(2)}, u32[]{:S(2)}) collective-permute-start(s32[8,2,16]{2,1,0:T(2,128)S(1)} %get-tuple-element.38), channel_id=1, source_target_pairs={{0,128},{8,136},{16,144},{24,152},{32,160},{40,168},{48,176},{56,1... | collective-permute-start | bytes 3080 | tf_op jit(solution)/shard_map/ppermute | solution.py:309
  124.6 1.3 collective-permute-start.8
  127.6 8.8 %copy-start.27 = (s32[128]{0:T(128)S(1)}, s32[128]{0:T(128)}, u32[]{:S(2)}) copy-start(s32[128]{0:T(128)} %param.15) | copy-start | bytes 1540
  127.6 10.5 %collective-permute-start.13 = (bf16[2,2,128,128]{3,2,1,0:T(8,128)(2,1)S(1)}, bf16[2,2,128,128]{3,2,1,0:T(8,128)(2,1)S(1)}, u32[]{:S(2)}, u32[]{:S(2)}) collective-permute-start(bf16[2,2,128,128]{3,2,1,0:T(8,128)(2,1)S(1)} %get-tuple-element.36), channel_id=1, source_target_pairs={{0,112},{8,120},{16,0},{24,8},{32,16},{40,24},{48,32},{56,40},{64,... | collective-permute-start | bytes 393224 | tf_op jit(solution)/shard_map/ppermute | solution.py:309
  136.8 11.1 %collective-permute-start.14 = (bf16[2,2,128,128]{3,2,1,0:T(8,128)(2,1)}, bf16[2,2,128,128]{3,2,1,0:T(8,128)(2,1)S(1)}, u32[]{:S(2)}, u32[]{:S(2)}) collective-permute-start(bf16[2,2,128,128]{3,2,1,0:T(8,128)(2,1)} %get-tuple-element.35), channel_id=1, source_target_pairs={{0,96},{8,104},{16,112},{24,120},{32,0},{40,8},{48,16},{56,24},{64... | collective-permute-start | bytes 393224 | tf_op jit(solution)/shard_map/ppermute | solution.py:309
  138.2 15.6 %collective-permute-start.15 = (bf16[2,2,128,128]{3,2,1,0:T(8,128)(2,1)}, bf16[2,2,128,128]{3,2,1,0:T(8,128)(2,1)S(1)}, u32[]{:S(2)}, u32[]{:S(2)}) collective-permute-start(bf16[2,2,128,128]{3,2,1,0:T(8,128)(2,1)} %get-tuple-element.34), channel_id=1, source_target_pairs={{0,80},{8,88},{16,96},{24,104},{32,112},{40,120},{48,0},{56,8},{64... | collective-permute-start | bytes 393224 | tf_op jit(solution)/shard_map/ppermute | solution.py:309
  148.0 11.1 %collective-permute-start.16 = (bf16[2,2,128,128]{3,2,1,0:T(8,128)(2,1)}, bf16[2,2,128,128]{3,2,1,0:T(8,128)(2,1)S(1)}, u32[]{:S(2)}, u32[]{:S(2)}) collective-permute-start(bf16[2,2,128,128]{3,2,1,0:T(8,128)(2,1)} %get-tuple-element.33), channel_id=1, source_target_pairs={{0,64},{8,72},{16,80},{24,88},{32,96},{40,104},{48,112},{56,120},{... | collective-permute-start | bytes 393224 | tf_op jit(solution)/shard_map/ppermute | solution.py:309
  153.7 13.4 %collective-permute-start.17 = (bf16[2,2,128,128]{3,2,1,0:T(8,128)(2,1)S(1)}, bf16[2,2,128,128]{3,2,1,0:T(8,128)(2,1)S(1)}, u32[]{:S(2)}, u32[]{:S(2)}) collective-permute-start(bf16[2,2,128,128]{3,2,1,0:T(8,128)(2,1)S(1)} %get-tuple-element.32), channel_id=1, source_target_pairs={{0,48},{8,56},{16,64},{24,72},{32,80},{40,88},{48,96},{56,104},{64... | collective-permute-start | bytes 393224 | tf_op jit(solution)/shard_map/ppermute | solution.py:309
  159.1 13.2 %collective-permute-start.18 = (bf16[2,2,128,128]{3,2,1,0:T(8,128)(2,1)S(1)}, bf16[2,2,128,128]{3,2,1,0:T(8,128)(2,1)S(1)}, u32[]{:S(2)}, u32[]{:S(2)}) collective-permute-start(bf16[2,2,128,128]{3,2,1,0:T(8,128)(2,1)S(1)} %get-tuple-element.31), channel_id=1, source_target_pairs={{0,32},{8,40},{16,48},{24,56},{32,64},{40,72},{48,80},{56,88},{64,... | collective-permute-start | bytes 393224 | tf_op jit(solution)/shard_map/ppermute | solution.py:309
  167.1 9.2 %collective-permute-start.19 = (bf16[2,2,128,128]{3,2,1,0:T(8,128)(2,1)S(1)}, bf16[2,2,128,128]{3,2,1,0:T(8,128)(2,1)S(1)}, u32[]{:S(2)}, u32[]{:S(2)}) collective-permute-start(bf16[2,2,128,128]{3,2,1,0:T(8,128)(2,1)S(1)} %get-tuple-element.30), channel_id=1, source_target_pairs={{0,16},{8,24},{16,32},{24,40},{32,48},{40,56},{48,64},{56,72},{64,... | collective-permute-start | bytes 393224 | tf_op jit(solution)/shard_map/ppermute | solution.py:309
  177.6 17.3 %collective-permute-start.20 = (bf16[8,2,128,128]{3,2,1,0:T(8,128)(2,1)}, bf16[8,2,128,128]{3,2,1,0:T(8,128)(2,1)}, u32[]{:S(2)}, u32[]{:S(2)}) collective-permute-start(bf16[8,2,128,128]{3,2,1,0:T(8,128)(2,1)} %get-tuple-element.27), channel_id=1, source_target_pairs={{0,128},{8,136},{16,144},{24,152},{32,160},{40,168},{48,176},{56,1... | collective-permute-start | bytes 1572872 | tf_op jit(solution)/shard_map/ppermute | solution.py:309
  182.1 1.4 copy-start.14
  183.5 1.4 copy-start.15
  184.9 8.7 %copy-start.26 = (bf16[1024,2,128]{2,1,0:T(2,128)(2,1)S(1)}, bf16[1024,2,128]{2,1,0:T(2,128)(2,1)}, u32[]{:S(2)}) copy-start(bf16[1024,2,128]{2,1,0:T(2,128)(2,1)} %get-tuple-element.23) | copy-start | bytes 1572868
  190.9 1.4 copy-start.2
  192.3 1.3 copy-start.4
  196.7 8.8 %copy-start.25 = (bf16[1024,2,128]{2,1,0:T(2,128)(2,1)S(1)}, bf16[1024,2,128]{2,1,0:T(2,128)(2,1)}, u32[]{:S(2)}) copy-start(bf16[1024,2,128]{2,1,0:T(2,128)(2,1)} %get-tuple-element.20) | copy-start | bytes 1572868
  197.8 10.2 %copy-start.18 = (bf16[1024,2,128]{2,1,0:T(2,128)(2,1)S(1)}, bf16[1024,2,128]{2,1,0:T(2,128)(2,1)}, u32[]{:S(2)}) copy-start(bf16[1024,2,128]{2,1,0:T(2,128)(2,1)} %get-tuple-element.22) | copy-start | bytes 1572868
  197.9 10.2 %copy-start.20 = (f32[256,512]{0,1:T(8,128)S(1)}, f32[256,512]{0,1:T(8,128)}, u32[]{:S(2)}) copy-start(f32[256,512]{0,1:T(8,128)} %fusion.23) | copy-start | bytes 1572868
  197.9 41.1 %collective-permute-start.21 = (bf16[2,8,128,128]{3,2,1,0:T(8,128)(2,1)}, bf16[2,8,128,128]{3,2,1,0:T(8,128)(2,1)}, u32[]{:S(2)}, u32[]{:S(2)}) collective-permute-start(bf16[2,8,128,128]{3,2,1,0:T(8,128)(2,1)} %get-tuple-element.29), channel_id=1, source_target_pairs={{0,8},{8,0},{16,24},{24,16},{32,40},{40,32},{48,56},{56,48},{64,72... | collective-permute-start | bytes 1572872 | tf_op jit(solution)/shard_map/ppermute | solution.py:309
  199.0 16.1 %collective-permute-start.27 = (bf16[256,1024]{1,0:T(8,128)(2,1)S(1)}, bf16[256,1024]{1,0:T(8,128)(2,1)S(1)}, u32[]{:S(2)}, u32[]{:S(2)}) collective-permute-start(bf16[256,1024]{1,0:T(8,128)(2,1)S(1)} %slice.15), channel_id=1, source_target_pairs={{0,2},{1,3},{2,4},{3,5},{4,6},{5,7},{6,0},{7,1},{8,10},{9,11},{10,... | collective-permute-start | bytes 1572872 | tf_op jit(solution)/shard_map/ppermute | solution.py:295
  200.9 15.0 %collective-permute-start.28 = (bf16[256,1024]{1,0:T(8,128)(2,1)S(1)}, bf16[256,1024]{1,0:T(8,128)(2,1)S(1)}, u32[]{:S(2)}, u32[]{:S(2)}) collective-permute-start(bf16[256,1024]{1,0:T(8,128)(2,1)S(1)} %slice.16), channel_id=1, source_target_pairs={{0,6},{1,7},{2,0},{3,1},{4,2},{5,3},{6,4},{7,5},{8,14},{9,15},{10,... | collective-permute-start | bytes 1572872 | tf_op jit(solution)/shard_map/ppermute | solution.py:295
  203.5 39.5 %collective-permute-start.26 = (bf16[512,1024]{1,0:T(8,128)(2,1)}, bf16[512,1024]{1,0:T(8,128)(2,1)}, u32[]{:S(2)}, u32[]{:S(2)}) collective-permute-start(bf16[512,1024]{1,0:T(8,128)(2,1)} %collective-permute-done.22), channel_id=1, source_target_pairs={{0,6},{1,7},{2,0},{3,1},{4,2},{5,3},{6,4},{7,5},{8,14},{9,15},{10,... | collective-permute-start | bytes 3145736 | tf_op jit(solution)/shard_map/ppermute | solution.py:295
  205.5 61.5 %collective-permute-start.25 = (bf16[512,1024]{1,0:T(8,128)(2,1)}, bf16[512,1024]{1,0:T(8,128)(2,1)}, u32[]{:S(2)}, u32[]{:S(2)}) collective-permute-start(bf16[512,1024]{1,0:T(8,128)(2,1)} %collective-permute-done.22), channel_id=1, source_target_pairs={{0,2},{1,3},{2,4},{3,5},{4,6},{5,7},{6,0},{7,1},{8,10},{9,11},{10,... | collective-permute-start | bytes 3145736 | tf_op jit(solution)/shard_map/ppermute | solution.py:295
  216.8 40.0 %collective-permute-start.29 = (bf16[512,1024]{1,0:T(8,128)(2,1)}, bf16[512,1024]{1,0:T(8,128)(2,1)}, u32[]{:S(2)}, u32[]{:S(2)}) collective-permute-start(bf16[512,1024]{1,0:T(8,128)(2,1)} %constant_dynamic-update-slice_fusion.16), channel_id=1, source_target_pairs={{0,1},{1,0},{2,3},{3,2},{4,5},{5,4},{6,7},{7,6},{8,9},{9,8},{10,11... | collective-permute-start | bytes 3145736 | tf_op jit(solution)/shard_map/ppermute | solution.py:295
  216.9 1.6 copy-start.13
  229.1 9.9 %copy-start.16 = (bf16[2,8,1,128,128]{4,3,2,1,0:T(8,128)(2,1)S(1)}, bf16[2,8,1,128,128]{4,3,2,1,0:T(8,128)(2,1)}, u32[]{:S(2)}) copy-start(bf16[2,8,1,128,128]{4,3,2,1,0:T(8,128)(2,1)} %get-tuple-element.28) | copy-start | bytes 1572868
  229.1 25.0 %all-to-all-start.1 = ((bf16[32,56,128]{2,1,0:T(8,128)(2,1)}), bf16[32,56,128]{2,1,0:T(8,128)(2,1)S(1)}, u32[]{:S(2)}, u32[]{:S(2)}) async-start(bf16[32,56,128]{2,1,0:T(8,128)(2,1)} %bitcast.26), calls=%async_computation.1 | async-start | bytes 917504 | tf_op jit(solution)/shard_map/all_to_all | solution.py:387
  239.0 1.5 copy-start.24
  240.4 2.6 copy-start.23
  254.1 13.0 %copy-start.17 = (f32[256,512]{0,1:T(8,128)S(1)}, f32[256,512]{0,1:T(8,128)}, u32[]{:S(2)}) copy-start(f32[256,512]{0,1:T(8,128)} %fusion) | copy-start | bytes 1572868
  254.1 13.0 %copy-start.19 = (bf16[1024,2,128]{2,1,0:T(2,128)(2,1)S(1)}, bf16[1024,2,128]{2,1,0:T(2,128)(2,1)}, u32[]{:S(2)}) copy-start(bf16[1024,2,128]{2,1,0:T(2,128)(2,1)} %get-tuple-element.18) | copy-start | bytes 1572868
  254.1 13.0 %copy-start.21 = (f32[512,256]{1,0:T(8,128)S(1)}, f32[512,256]{1,0:T(8,128)}, u32[]{:S(2)}) copy-start(f32[512,256]{1,0:T(8,128)} %fusion.8) | copy-start | bytes 1572868
  254.1 13.0 %copy-start.22 = (f32[256,512]{0,1:T(8,128)S(1)}, f32[256,512]{0,1:T(8,128)}, u32[]{:S(2)}) copy-start(f32[256,512]{0,1:T(8,128)} %fusion.11) | copy-start | bytes 1572868
  254.9 5.1 %collective-permute-start.9 = (f32[256,128]{1,0:T(8,128)S(1)}, f32[256,128]{1,0:T(8,128)S(1)}, u32[]{:S(2)}, u32[]{:S(2)}) collective-permute-start(f32[256,128]{1,0:T(8,128)S(1)} %collect.1), channel_id=1, source_target_pairs={{0,1},{1,0},{2,3},{3,2},{4,5},{5,4},{6,7},{7,6},{8,9},{9,8},{10,11... | collective-permute-start | bytes 393224 | tf_op jit(solution)/shard_map/ppermute | solution.py:295
  256.8 13.1 %copy-start.9 = (s32[512,1]{1,0:T(8,128)S(1)}, s32[512,1]{1,0:T(8,128)}, u32[]{:S(2)}) copy-start(s32[512,1]{1,0:T(8,128)} %copy-done.8) | copy-start | bytes 6148
  260.0 8.9 %collective-permute-start.10 = (f32[256,128]{1,0:T(8,128)S(1)}, f32[256,128]{1,0:T(8,128)S(1)}, u32[]{:S(2)}, u32[]{:S(2)}) collective-permute-start(f32[256,128]{1,0:T(8,128)S(1)} %add.190.a_ref), channel_id=1, source_target_pairs={{0,4},{1,5},{2,6},{3,7},{4,0},{5,1},{6,2},{7,3},{8,12},{9,13},{10,... | collective-permute-start | bytes 393224 | tf_op jit(solution)/shard_map/ppermute | solution.py:295
  263.8 6.2 %collective-permute-start.11 = (f32[256,128]{1,0:T(8,128)S(1)}, f32[256,128]{1,0:T(8,128)S(1)}, u32[]{:S(2)}, u32[]{:S(2)}) collective-permute-start(f32[256,128]{1,0:T(8,128)S(1)} %add.190.a_ref), channel_id=1, source_target_pairs={{0,2},{1,3},{2,4},{3,5},{4,6},{5,7},{6,0},{7,1},{8,10},{9,11},{10,... | collective-permute-start | bytes 393224 | tf_op jit(solution)/shard_map/ppermute | solution.py:295
  264.4 5.6 %collective-permute-start.12 = (f32[256,128]{1,0:T(8,128)S(1)}, f32[256,128]{1,0:T(8,128)S(1)}, u32[]{:S(2)}, u32[]{:S(2)}) collective-permute-start(f32[256,128]{1,0:T(8,128)S(1)} %add.190.a_ref), channel_id=1, source_target_pairs={{0,6},{1,7},{2,0},{3,1},{4,2},{5,3},{6,4},{7,5},{8,14},{9,15},{10,... | collective-permute-start | bytes 393224 | tf_op jit(solution)/shard_map/ppermute | solution.py:295
  267.0 2.9 %copy-start.3 = (f32[16,256,128]{2,1,0:T(8,128)S(1)}, f32[16,256,128]{2,1,0:T(8,128)}, u32[]{:S(2)}) copy-start(f32[16,256,128]{2,1,0:T(8,128)} %copy-done.2) | copy-start | bytes 6291460
  267.1 2.9 %copy-start.5 = (f32[16,256,128]{2,1,0:T(8,128)S(1)}, f32[16,256,128]{2,1,0:T(8,128)}, u32[]{:S(2)}) copy-start(f32[16,256,128]{2,1,0:T(8,128)} %copy-done.4) | copy-start | bytes 6291460
  280.2 0.7 copy-start.6
  280.9 1.2 copy-start.7

commit v3 on v2

v3 whole, which is shorter than its diff:
```python
import functools

import jax
import jax.numpy as jnp
from jax import lax
from jax.experimental import pallas as pl
from jax.experimental.pallas import tpu as pltpu
from jax.sharding import PartitionSpec as P

HD = 128
BLK = 7
PAIR = 2
PAIR_ROWS = PAIR * BLK
ASK_ROWS = 16
RETURN_ROWS = 64
LANES = 128
GROUP = 8

masked_score = -1e30


def iota(shape, dim):
    return lax.broadcasted_iota(jnp.int32, shape, dim)


def total(value, axis):
    return jnp.sum(value, axis=axis, keepdims=True)


def place_kernel(steps, first_ref, request_ref, owner_ref, tokens_ref, sent_ref, column_ref, fetch_ref, row_ref, info_ref):
    here, _, lanes = sent_ref.shape
    each = PAIR_ROWS * steps
    token_count, depth = tokens_ref.shape

    @pl.when(pl.program_id(0) == 0)
    def _():
        first = first_ref[...]
        blocks = first.shape[1]
        rows = request_ref.shape[1]
        pool = owner_ref.shape[1]
        owners = owner_ref[...]
        i, j = iota((blocks, blocks), 0), iota((blocks, blocks), 1)

        def down(value):
            return total(jnp.where(i == j, value, 0), 1)

        def across(value):
            return total(jnp.where(i == j, value, 0), 0)

        first_c = down(first)
        after_c = total(jnp.where(j == i + 1, first, 0), 1) + jnp.where(i[:, :1] == blocks - 1, rows, 0)
        after = across(after_c)
        adapter_c = total(jnp.where(iota((blocks, rows), 1) == first_c, request_ref[...], 0), 1)
        ids = iota((blocks, pool), 1)
        owner_c = total(jnp.where(ids == adapter_c, owners, 0), 1)
        slot_c = total(jnp.where((owners == owner_c) & (ids < adapter_c), 1, 0), 1)
        owner, slot = across(owner_c), across(slot_c)
        before = (owner == owner_c) & (j < i)
        turn_c = total(jnp.where(before, 1, 0), 1)
        offset_c = total(jnp.where(before, after - first, 0), 1)
        turn, offset = across(turn_c), across(offset_c)

        r, b = iota((rows, blocks), 0), iota((rows, blocks), 1)
        member = (first <= r) & (r < after)
        spot = r[:, :1] + total(jnp.where(member, offset - first, 0), 1)
        row_slot = total(jnp.where(member, slot, 0), 1)
        r_row = iota((blocks, rows), 1)
        row_owner = total(jnp.where((first_c <= r_row) & (r_row < after_c), owner_c, 0), 0)
        count = info_ref.shape[0]
        goes = jnp.where(iota((count, rows), 0) == row_owner, 1.0, 0.0).astype(jnp.bfloat16)
        asks = jnp.where(iota((rows, lanes), 1) == spot, row_slot, 0).astype(jnp.float32).astype(jnp.bfloat16)
        info = jnp.dot(goes, asks, preferred_element_type=jnp.float32)
        goes = jnp.where(iota((count, blocks), 0) == owner, 1.0, 0.0).astype(jnp.bfloat16)
        asks = jnp.where(iota((blocks, lanes), 1) == PAIR_ROWS + turn_c, slot_c, 0)
        asks = asks.astype(jnp.float32).astype(jnp.bfloat16)
        info_ref[...] = info + jnp.dot(goes, asks, preferred_element_type=jnp.float32)

        t = iota((blocks, token_count), 1)
        member = (first_c * steps <= t) & (t < after_c * steps)
        row_ref[...] = t[:1] + total(
            jnp.where(member, (owner_c * PAIR_ROWS + offset_c - first_c) * steps, 0), 0
        )
        t = iota((token_count, blocks), 0)
        member = (first * steps <= t) & (t < after * steps)
        column_ref[...] = t[:, :1] + total(
            jnp.where(member, owner * RETURN_ROWS + (offset - first) * steps, 0), 1
        )
        fetch_ref[...] = total(jnp.where(member, owner * PAIR + turn, 0), 1)

    spots = iota((here * each, token_count), 0) + pl.program_id(0) * (here * each)
    pick = jnp.where(spots == row_ref[...], 1.0, 0.0).astype(jnp.bfloat16)
    picked = jnp.dot(pick, tokens_ref[...], preferred_element_type=jnp.float32)
    for k in range(here):
        asked = info_ref[pl.ds(pl.program_id(0) * here + k, 1), :]
        parts = [picked[k * each:(k + 1) * each, c * lanes:(c + 1) * lanes] for c in range(depth // lanes)]
        parts.append(jnp.where(iota((ASK_ROWS, lanes), 0) == 0, asked, 0.0))
        sent_ref[k] = jnp.concatenate(parts, axis=0).astype(jnp.bfloat16)


def place(first, request, owners, tokens, steps, replicas):
    token_count, depth = tokens.shape
    rows = PAIR_ROWS * steps * depth // LANES + ASK_ROWS
    here = 4
    whole = lambda shape: pl.BlockSpec(shape, lambda i: (0, 0))
    return pl.pallas_call(
        functools.partial(place_kernel, steps),
        grid=(replicas // here,),
        in_specs=[
            whole((1, first.shape[0])), whole((1, request.shape[0])), whole((1, owners.shape[0])),
            whole((token_count, depth)),
        ],
        out_specs=[
            pl.BlockSpec((here, rows, LANES), lambda i: (i, 0, 0)),
            whole((token_count, 1)), whole((token_count, 1)),
        ],
        out_shape=[
            jax.ShapeDtypeStruct((replicas, rows, LANES), jnp.bfloat16),
            jax.ShapeDtypeStruct((token_count, 1), jnp.int32),
            jax.ShapeDtypeStruct((token_count, 1), jnp.int32),
        ],
        scratch_shapes=[pltpu.VMEM((1, token_count), jnp.int32), pltpu.VMEM((replicas, LANES), jnp.float32)],
        compiler_params=pltpu.CompilerParams(vmem_limit_bytes=24 * 2**20),
        name="place_rows",
    )(first[None], request[None], owners[None], tokens)


def rank_kernel(steps, rows_ref, maps_ref, ups_ref, out_ref):
    here, _, lanes = rows_ref.shape
    each = PAIR_ROWS * steps
    width = lanes // 2
    depth = maps_ref.shape[0]
    tokens, slots, picks = [], [], []
    for k in range(here):
        got = rows_ref[k].astype(jnp.float32)
        chunks = [got[c * each:(c + 1) * each] for c in range(depth // lanes)]
        tokens.append(jnp.concatenate(chunks, axis=1))
        asked = got[each * (depth // lanes):][:1]
        shape = (each, lanes)
        slots.append(total(jnp.where(iota(shape, 1) == iota(shape, 0) // steps, asked, 0.0), 1))
        shape = (PAIR * width, ups_ref.shape[0])
        i = iota((PAIR * width, 1), 0)
        turn = total(jnp.where(iota((PAIR * width, lanes), 1) == PAIR_ROWS + i // width, asked, 0.0), 1)
        at = turn.astype(jnp.int32) * width + i % width
        picks.append(jnp.where(iota(shape, 1) == at, 1.0, 0.0).astype(jnp.bfloat16))
    every = jnp.dot(
        jnp.concatenate(tokens, axis=0).astype(jnp.bfloat16), maps_ref[...], preferred_element_type=jnp.float32
    )
    slot = jnp.concatenate(slots, axis=0).astype(jnp.int32)
    two = jnp.zeros((here * each, lanes), jnp.float32)
    for pair in range(every.shape[1] // lanes):
        two = jnp.where(slot // 2 == pair, every[:, pair * lanes:(pair + 1) * lanes], two)
    own = jnp.where(slot % 2 == 1, two[:, width:], two[:, :width])
    high = own.astype(jnp.bfloat16).astype(jnp.float32)
    both = jnp.concatenate([high, own - high], axis=1)
    ups = jnp.dot(jnp.concatenate(picks, axis=0), ups_ref[...], preferred_element_type=jnp.float32)
    for k in range(here):
        out_ref[k] = jnp.concatenate(
            [
                both[k * each:(k + 1) * each],
                jnp.zeros((RETURN_ROWS - each, lanes), jnp.float32),
                ups[k * PAIR * width:(k + 1) * PAIR * width],
            ],
            axis=0,
        ).astype(jnp.bfloat16)


def rank_products(rows, maps, ups, steps):
    replicas, count, lanes = rows.shape
    here = 8
    out_rows = RETURN_ROWS + PAIR * lanes // 2
    whole = lambda x: pl.BlockSpec(x.shape, lambda i: (0, 0))
    return pl.pallas_call(
        functools.partial(rank_kernel, steps),
        grid=(replicas // here,),
        in_specs=[pl.BlockSpec((here, count, lanes), lambda i: (i, 0, 0)), whole(maps), whole(ups)],
        out_specs=pl.BlockSpec((here, out_rows, lanes), lambda i: (i, 0, 0)),
        out_shape=jax.ShapeDtypeStruct((replicas, out_rows, lanes), jnp.bfloat16),
        compiler_params=pltpu.CompilerParams(vmem_limit_bytes=60 * 2**20),
        cost_estimate=pl.CostEstimate(flops=2**32, bytes_accessed=8 * 2**20, transcendentals=0),
        name="rank_products",
    )(rows, maps, ups)


def collect_kernel(column_ref, returned_ref, out_ref):
    replicas, rows, lanes = returned_ref.shape
    tokens, width = column_ref.shape[0], lanes // 2
    pick = jnp.where(iota((tokens, replicas * rows), 1) == column_ref[...], 1.0, 0.0).astype(jnp.bfloat16)
    both = jnp.dot(pick, returned_ref[...].reshape(replicas * rows, lanes), preferred_element_type=jnp.float32)
    value = both[:, :width] + both[:, width:]
    out_ref[...] = jnp.concatenate([value[: tokens // 2], value[tokens // 2:]], axis=1)


def collect(column, returned):
    tokens = column.shape[0]
    replicas, _, lanes = returned.shape
    return pl.pallas_call(
        collect_kernel,
        grid=(1,),
        in_specs=[
            pl.BlockSpec((tokens, 1), lambda i: (0, 0)),
            pl.BlockSpec((replicas, RETURN_ROWS, lanes), lambda i: (0, 0, 0)),
        ],
        out_specs=pl.BlockSpec((tokens // 2, lanes), lambda i: (0, 0)),
        out_shape=jax.ShapeDtypeStruct((tokens // 2, lanes), jnp.float32),
        compiler_params=pltpu.CompilerParams(vmem_limit_bytes=24 * 2**20),
        name="collect",
    )(column, returned)


def heads_first(value, heads):
    return jnp.concatenate([value[:, h * HD:(h + 1) * HD] for h in range(heads)], axis=0)


def cached_kernel(steps, bias_ref, queries_ref, keys_ref, values_ref, mixed_ref, weight_ref):
    heads = queries_ref.shape[1] // HD
    rows = keys_ref.shape[0] // GROUP if keys_ref.ndim == 3 else 1
    cache = keys_ref.shape[1]
    count = GROUP * steps
    for g in range(rows):
        query = heads_first(queries_ref[g * count:(g + 1) * count, :], heads)
        keys = keys_ref[g * GROUP:(g + 1) * GROUP].reshape(GROUP * cache, HD)
        values = values_ref[g * GROUP:(g + 1) * GROUP].reshape(GROUP * cache, HD)
        score = lax.dot_general(query, keys, (((1,), (1,)), ((), ())), preferred_element_type=jnp.float32)
        shape = score.shape
        own = (iota(shape, 0) // steps) % GROUP == iota(shape, 1) // cache
        score = jnp.where(own, score * HD ** -0.5 + bias_ref[g], masked_score)
        highest = jnp.max(score, axis=1, keepdims=True)
        exped = jnp.exp(score - highest)
        summed = total(exped, 1)
        mixed = jnp.dot(exped.astype(jnp.bfloat16), values, preferred_element_type=jnp.float32)
        mixed_ref[g] = mixed / summed
        weight_ref[g] = jnp.broadcast_to(highest + jnp.log(summed), mixed.shape)


def cached_attention(lengths, queries, keys, values, steps):
    rows, cache = keys.shape[:2]
    heads = queries.shape[1] // HD
    groups = rows // GROUP
    count = GROUP * steps * heads
    live = jnp.arange(cache, dtype=jnp.int32)[None, :] < lengths[:, None]
    bias = jnp.where(live, 0.0, masked_score).astype(jnp.float32).reshape(groups, 1, GROUP * cache)
    per = 2
    return pl.pallas_call(
        functools.partial(cached_kernel, steps),
        grid=(groups // per,),
        in_specs=[
            pl.BlockSpec((per, 1, GROUP * cache), lambda i: (i, 0, 0)),
            pl.BlockSpec((per * GROUP * steps, heads * HD), lambda i: (i, 0)),
            pl.BlockSpec((per * GROUP, cache, HD), lambda i: (i, 0, 0)),
            pl.BlockSpec((per * GROUP, cache, HD), lambda i: (i, 0, 0)),
        ],
        out_specs=[pl.BlockSpec((per, count, HD), lambda i: (i, 0, 0))] * 2,
        out_shape=[jax.ShapeDtypeStruct((groups, count, HD), jnp.float32)] * 2,
        compiler_params=pltpu.CompilerParams(vmem_limit_bytes=24 * 2**20),
        cost_estimate=pl.CostEstimate(flops=2**31, bytes_accessed=8 * 2**20, transcendentals=2**20),
        name="cached_attention",
    )(bias, queries, keys, values)


def finish_kernel(steps, rank, fetch_ref, a_ref, b_ref, c_ref, d_ref, first_ref, second_ref, base_ref, queries_ref, mixed_ref, weight_ref, fresh_ref, out_ref, held_ref):
    heads = queries_ref.shape[1] // HD
    count = GROUP * steps
    tokens = fetch_ref.shape[0]

    @pl.when(pl.program_id(0) == 0)
    def _():
        summed = (a_ref[...] + b_ref[...]) + (c_ref[...] + d_ref[...])
        width = summed.shape[1] // 2
        low = jnp.concatenate([summed[:, :width], summed[:, width:]], axis=0)
        fetch = fetch_ref[...]
        lanes = iota((tokens, LANES), 1) // rank
        owners = first_ref.shape[0]
        for side in range(2):
            four = jnp.concatenate([low[:, side * rank:(side + 1) * rank]] * (LANES // rank), axis=1)
            delta = jnp.zeros((tokens, HD), jnp.float32)
            for turn, maps_ref in enumerate((first_ref, second_ref)):
                spread = jnp.concatenate(
                    [
                        jnp.where(fetch == PAIR * (lanes + k * (LANES // rank)) + turn, four, 0.0).astype(jnp.bfloat16)
                        for k in range(owners * rank // LANES)
                    ],
                    axis=1,
                )
                maps = maps_ref[:, side * rank:(side + 1) * rank, :].reshape(owners * rank, HD)
                delta += jnp.dot(spread, maps, preferred_element_type=jnp.float32)
            new = base_ref[:, side * HD:(side + 1) * HD] + delta
            held_ref[:, side * HD:(side + 1) * HD] = new.astype(jnp.bfloat16)
        fresh_ref[...] = held_ref[...]

    for g in range(mixed_ref.shape[0]):
        start = pl.multiple_of((pl.program_id(0) * mixed_ref.shape[0] + g) * count, count)
        new = held_ref[pl.ds(start, count), :]
        query = heads_first(queries_ref[g * count:(g + 1) * count, :], heads)
        score = lax.dot_general(
            query, new[:, :HD], (((1,), (1,)), ((), ())), preferred_element_type=jnp.float32
        )
        i, j = iota(score.shape, 0), iota(score.shape, 1)
        seen = ((i // steps) % GROUP == j // steps) & (j % steps <= i % steps)
        score = jnp.where(seen, score * HD ** -0.5, masked_score)
        weight = weight_ref[g]
        highest = jnp.maximum(jnp.max(score, axis=1, keepdims=True), weight)
        exped = jnp.exp(score - highest[:, :count]).astype(jnp.bfloat16)
        cached = jnp.exp(weight - highest)
        ones = jnp.ones((count, HD), jnp.bfloat16)
        both = jnp.dot(
            exped, jnp.concatenate([new[:, HD:], ones], axis=1), preferred_element_type=jnp.float32
        )
        mixed = (mixed_ref[g] * cached + both[:, :HD]) / (cached + both[:, HD:])
        for h in range(heads):
            part = mixed[h * count:(h + 1) * count].reshape(GROUP, steps, HD)
            out_ref[g * GROUP:(g + 1) * GROUP, :, h * HD:(h + 1) * HD] = part.astype(jnp.bfloat16)


def finish(fetch, parts, returned, base, queries, mixed, weight, steps, rank):
    tokens, features = queries.shape
    groups, rows = mixed.shape[:2]
    per = 4
    whole = lambda x: pl.BlockSpec(x.shape, lambda i: (0,) * x.ndim)
    block = pl.BlockSpec((per * GROUP * steps, features), lambda i: (i, 0))
    ups = lambda k: pl.BlockSpec((returned.shape[0], PAIR * rank, HD), lambda i: (0, k, 0))
    return pl.pallas_call(
        functools.partial(finish_kernel, steps, rank),
        grid=(groups // per,),
        in_specs=[whole(fetch)] + [whole(p) for p in parts] + [ups(1), ups(2), whole(base), block]
        + [pl.BlockSpec((per, rows, HD), lambda i: (i, 0, 0))] * 2,
        out_specs=[
            pl.BlockSpec(base.shape, lambda i: (0, 0)),
            pl.BlockSpec((per * GROUP, steps, features), lambda i: (i, 0, 0)),
        ],
        out_shape=[
            jax.ShapeDtypeStruct(base.shape, jnp.bfloat16),
            jax.ShapeDtypeStruct((tokens // steps, steps, features), jnp.bfloat16),
        ],
        scratch_shapes=[pltpu.VMEM(base.shape, jnp.bfloat16)],
        compiler_params=pltpu.CompilerParams(vmem_limit_bytes=32 * 2**20),
        name="finish",
    )(fetch, *parts, returned, returned, base, queries, mixed, weight)


def shifted(value, dx, dy):
    pairs = [(t, ((t // 2 + dx) % 4) * 2 + ((t % 2) ^ dy)) for t in range(8)]
    return lax.ppermute(value, "tensor", pairs)


def project(tokens, key_value_weight):
    half = tokens.shape[0] // 2
    here = lax.axis_index("tensor")
    x, y = here >> 1, here & 1
    depth = tokens.shape[1]

    def product(piece, dx, dy):
        start = ((((x - dx) & 3) << 1) | (y ^ dy)) * depth
        part = lax.dynamic_slice_in_dim(key_value_weight, start, depth, 0)
        return jnp.dot(piece, part.reshape(depth, -1), preferred_element_type=jnp.float32)

    right = shifted(tokens, 1, 0)
    left = shifted(tokens, -1, 0)
    across = shifted(tokens, 0, 1)
    right_across = shifted(across, 1, 0)
    left_across = shifted(across, -1, 0)
    far = jnp.concatenate([shifted(right[:half], 1, 0), shifted(left[half:], -1, 0)], axis=0)
    far_across = shifted(far, 0, 1)
    base = product(tokens, 0, 0) + product(across, 0, 1)
    base = base + product(right, 1, 0) + product(left, -1, 0)
    base = base + product(far, 2, 0) + product(right_across, 1, 1) + product(left_across, -1, 1)
    return base + product(far_across, 2, 1)


def per_device(
    hidden,
    queries,
    key_cache_rows,
    value_cache_rows,
    lengths,
    request_adapter,
    block_first_row,
    adapter_owner_group,
    key_value_weight,
    adapter_down_weight,
    adapter_up_weight,
):
    row_count, steps, depth = hidden.shape
    replicas = lax.axis_size("replica")
    token_count = row_count * steps
    held, sides, rank = adapter_down_weight.shape[:3]
    tokens = hidden.reshape(token_count, depth)

    sent, column, fetch = place(
        block_first_row, request_adapter, adapter_owner_group, tokens, steps, replicas
    )
    received = lax.all_to_all(sent, "replica", split_axis=0, concat_axis=0, tiled=True)

    base = project(tokens, key_value_weight)
    query_tokens = queries.reshape(token_count, -1)
    mixed, weight = cached_attention(lengths, query_tokens, key_cache_rows, value_cache_rows, steps)

    down = adapter_down_weight.reshape(held * sides * rank, depth).T
    received, base, mixed, weight, down = lax.optimization_barrier((received, base, mixed, weight, down))
    products = rank_products(
        received,
        down,
        adapter_up_weight.reshape(held * sides * rank, HD),
        steps,
    )
    returned = lax.all_to_all(products, "replica", split_axis=0, concat_axis=0, tiled=True)
    mine = collect(column, returned)
    mine = mine + shifted(mine, 0, 1)
    parts = (mine, shifted(mine, 2, 0), shifted(mine, 1, 0), shifted(mine, -1, 0))
    fresh, attended = finish(fetch, parts, returned, base, query_tokens, mixed, weight, steps, rank)
    return fresh.reshape(row_count, steps, sides, HD), attended


def solution(mesh):
    placed = (
        P("replica", None, "tensor"),
        P("replica", None, "tensor"),
        P("replica", None, "tensor"),
        P("replica", None, "tensor"),
        P("replica"),
        P("replica"),
        P("replica"),
        P(),
        P(None, None, "tensor"),
        P("replica", None, None, "tensor"),
        P("replica", None, None, "tensor"),
    )
    return jax.shard_map(
        per_device,
        mesh=mesh,
        in_specs=placed,
        out_specs=(P("replica", None, None, "tensor"), P("replica", None, "tensor")),
        check_vma=False,
    )
```

time: 285 us -> 199 us (0.70)
  starting transfers between devices: 82.4 us -> 28.2 us
  waiting for transfers between devices: 117 us -> 64.1 us
  blocking collectives: 0 us -> 50.3 us
  matrix products: 16.8 us -> 6.98 us
  local copies, waits for them, and re-layouts: 29.9 us -> 21 us
  Pallas kernels: 31.6 us -> 27.1 us
  other arithmetic: 3.98 us -> 0.04 us
    ppermute x18 -> x0, waiting for transfers between devices: 101 us -> none  [send(): return lax.ppermute(piece, 'replica', pairs)]
    ppermute x12, waiting for transfers between devices: 7.77 us -> 64.1 us  [shifted(): return lax.ppermute(value, 'tensor', pairs)]
    all_to_all x0 -> x1, blocking collectives: none -> 50.3 us  [per_device(): lax.all_to_all(products, 'replica', split_axis=0, concat_axis=0, tiled=True)]
    ppermute x18 -> x0, starting transfers between devices: 50 us -> none  [send(): return lax.ppermute(piece, 'replica', pairs)]
    dot_general x8, matrix products: 16.8 us -> 6.98 us  [product(): jnp.dot(piece, part.reshape(depth, -1), preferred_element_type=jnp.float32)]
    all_to_all x2 -> x1, waiting for transfers between devices: 8.61 us -> 0.01 us  [per_device(): lax.all_to_all(sent, 'replica', split_axis=0, concat_axis=0, tiled=True)]
    unnamed x87 -> x41, local copies, waits for them, and re-layouts: 11.6 us -> 5.83 us
    pallas_call x1, Pallas kernels: 10.2 us -> 6.19 us  [finish(): pl.pallas_call(functools.partial(finish_kernel, steps, rank), grid=(group...]
  transfers between devices with their start and end apart: 32 -> 13, of which waited for: 15 -> 8; matrix products, arithmetic and copies ran while one was open for 13% -> 11% of each run, Pallas kernels for 8% -> 3%
where the time goes in v3:
time: 199 us
  waiting for transfers between devices  64.1 us (32%)
  blocking collectives  50.3 us (25%)
  starting transfers between devices  28.2 us (14%)
  Pallas kernels  27.1 us (14%)
  local copies, waits for them, and re-layouts  21 us (11%)
  matrix products  6.98 us (4%)
    ppermute x12, waiting for transfers between devices, shifted(): return lax.ppermute(value, 'tensor', pairs)  64.1 us
    all_to_all x1, blocking collectives, per_device(): lax.all_to_all(products, 'replica', split_axis=0, concat_axis=0, tiled=True)  50.3 us
    ppermute x12, starting transfers between devices, shifted(): return lax.ppermute(value, 'tensor', pairs)  16.7 us
    all_to_all x1, starting transfers between devices, per_device(): lax.all_to_all(sent, 'replica', split_axis=0, concat_axis=0, tiled=True)  11.5 us
    pallas_call x1, Pallas kernels, rank_products(): pl.pallas_call(functools.partial(rank_kernel, steps), grid=(replicas // h...  9.78 us
    dot_general x8, matrix products, product(): jnp.dot(piece, part.reshape(depth, -1), preferred_element_type=jnp.float32)  6.98 us
    pallas_call x1, Pallas kernels, finish(): pl.pallas_call(functools.partial(finish_kernel, steps, rank), grid=(group...  6.19 us
    pallas_call x1, Pallas kernels, cached_attention(): pl.pallas_call(functools.partial(cached_kernel, steps), grid=(groups // p...  6 us
  transfers between devices with their start and end apart: 13, of which 8 were waited for; matrix products, arithmetic and copies ran while one was open for 11% of the time, Pallas kernels for 3%

profile of v3, /device:TPU:32, one launch (start us, length us, event | category | flops | bytes accessed | tf_op | source)
XLA Modules:
  0.0 198.7 jit_solution(16849027894377197552)
XLA Ops:
  0.6 0.0 copy-start.6
  0.6 0.0 copy-start.7
  0.7 0.0 copy-start.5
  0.7 1.4 reshape.87.tokens_ref
  2.0 0.0 copy-done.6
  2.0 0.0 copy-done.7
  2.1 4.2 %place_rows.1 = (bf16[32,464,128]{2,1,0:T(8,128)(2,1)S(1)}, s32[512,1]{1,0:T(8,128)S(1)}, s32[512,1]{1,0:T(8,128)S(1)}) custom-call(s32[1,32]{1,0:T(1,128)S(1)} %bitcast.61, s32[1,128]{1,0:T(1,128)S(1)} %bitcast.62, s32[1,512]{1,0:T(1,128)S(1)} %bitcast.60, bf16[512,1024]{1,0:T(8,128)(2,1)S(1)} %reshape.87.tokens_ref), custom_call_target="tpu_custom_call" | custom-call | tf_op jit(solution)/shard_map/place_rows/pallas_call | solution.py:105
  6.2 1.8 copy-done
  8.0 11.5 %all-to-all-start = ((bf16[32,464,128]{2,1,0:T(8,128)(2,1)}), bf16[32,464,128]{2,1,0:T(8,128)(2,1)}, u32[]{:S(2)}, u32[]{:S(2)}) async-start(bf16[32,464,128]{2,1,0:T(8,128)(2,1)} %copy-done), calls=%async_computation | async-start | bytes 7602176 | tf_op jit(solution)/shard_map/all_to_all | solution.py:391
  19.6 1.6 collective-permute-start.1
  21.2 1.7 collective-permute-start.2
  22.9 0.7 collective-permute-start
  23.6 0.0 copy-done.19
  23.6 0.1 lt.63
  23.7 0.1 lt.64
  23.7 0.1 lt.65
  23.9 0.1 lt.61
  24.0 5.4 %constant_dynamic-slice_fusion.1 = (bf16[1024,2,128]{2,1,0:T(2,128)(2,1)}, bf16[1024,2,128]{2,1,0:T(2,128)(2,1)S(1)}, bf16[1024,2,128]{2,1,0:T(2,128)(2,1)}, bf1...) fusion(bf16[8192,2,128]{2,1,0:T(2,128)(2,1)} %param.19, ...), kind=kLoop, calls=%fused_computation.34 | loop fusion | bytes 8388640 | tf_op jit(solution)/shard_map/dynamic_slice | solution.py:353
  29.4 1.2 fusion.23
  30.6 15.4 %collective-permute-done.1 = bf16[512,1024]{1,0:T(8,128)(2,1)S(1)} collective-permute-done((bf16[512,1024]{1,0:T(8,128)(2,1)S(1)}, bf16[512,1024]{1,0:T(8,128)(2,1)S(1)}, u32[]{:S(2)}, u32[]{:S(2)}) %collective-permute-start.1) | collective-permute-done | bytes 1048608 | tf_op jit(solution)/shard_map/ppermute | solution.py:342
  46.1 0.9 slice.8
  47.0 0.3 collective-permute-start.3
  47.3 1.3 reshape.96.queries_ref
  48.7 4.0 %copy.26 = bf16[1024,1024]{0,1:T(8,128)(2,1)} copy(bf16[1024,1024]{1,0:T(8,128)(2,1)} %bitcast.63) | data formatting | bytes 4194304 | tf_op jit(solution)/shard_map/reshape | solution.py:397
  52.6 0.0 collective-permute-done.2
  52.6 1.1 slice.9
  53.7 3.0 %collective-permute-start.4 = (bf16[256,1024]{1,0:T(8,128)(2,1)S(1)}, bf16[256,1024]{1,0:T(8,128)(2,1)S(1)}, u32[]{:S(2)}, u32[]{:S(2)}) collective-permute-start(bf16[256,1024]{1,0:T(8,128)(2,1)S(1)} %slice.9), channel_id=1, source_target_pairs={{0,6},{1,7},{2,0},{3,1},{4,2},{5,3},{6,4},{7,5},{8,14},{9,15},{10,... | collective-permute-start | bytes 1572872 | tf_op jit(solution)/shard_map/ppermute | solution.py:342
  56.7 1.4 copy-done.8
  58.1 1.4 copy-done.9
  59.5 6.0 %cached_attention.1 = (f32[16,256,128]{2,1,0:T(8,128)S(1)}, f32[16,256,128]{2,1,0:T(8,128)S(1)}) custom-call(f32[16,1,384]{2,1,0:T(1,128)S(1)} %compare_select_fusion.bias_ref, bf16[512,1024]{1,0:T(8,128)(2,1)S(1)} %reshape.96.queries_ref, bf16[128,48,128]{2,1,0:T(8,128)(2,1)S(1)} %copy-done.8, bf16[128,48,128]{2,1,0:T(8,128)(2,1)S(1)} %copy-done.9), custom_call_target="tpu_custom_call" | custom-call | flops 2147483648 | bytes 8388608 | tf_op jit(solution)/shard_map/cached_attention/pallas_call | solution.py:243
  65.6 4.8 %collective-permute-done = bf16[512,1024]{1,0:T(8,128)(2,1)} collective-permute-done((bf16[512,1024]{1,0:T(8,128)(2,1)S(1)}, bf16[512,1024]{1,0:T(8,128)(2,1)}, u32[]{:S(2)}, u32[]{:S(2)}) %collective-permute-start) | collective-permute-done | bytes 1048608 | tf_op jit(solution)/shard_map/ppermute | solution.py:342
  70.3 1.5 collective-permute-start.5
  71.8 1.7 collective-permute-start.6
  73.6 1.7 convolution_add_fusion.1
  75.3 0.0 collective-permute-done.3
  75.4 1.1 constant_dynamic-update-slice_fusion.1
  76.5 0.0 collective-permute-done.4
  76.6 1.6 collective-permute-start.7
  78.2 1.8 fusion.16
  80.0 0.4 fusion.13
  80.4 0.0 copy-done.11
  80.4 0.0 copy-done.12
  80.5 0.4 fusion.5
  80.9 0.0 copy-start.16
  80.9 15.5 %collective-permute-done.5 = bf16[512,1024]{1,0:T(8,128)(2,1)S(1)} collective-permute-done((bf16[512,1024]{1,0:T(8,128)(2,1)}, bf16[512,1024]{1,0:T(8,128)(2,1)S(1)}, u32[]{:S(2)}, u32[]{:S(2)}) %collective-permute-start.5) | collective-permute-done | bytes 1048608 | tf_op jit(solution)/shard_map/ppermute | solution.py:342
  96.4 0.4 fusion.4
  96.8 18.0 %collective-permute-done.7 = bf16[512,1024]{1,0:T(8,128)(2,1)S(1)} collective-permute-done((bf16[512,1024]{1,0:T(8,128)(2,1)S(1)}, bf16[512,1024]{1,0:T(8,128)(2,1)S(1)}, u32[]{:S(2)}, u32[]{:S(2)}) %collective-permute-start.7) | collective-permute-done | bytes 1048608 | tf_op jit(solution)/shard_map/ppermute | solution.py:342
  114.9 0.4 fusion.6
  115.3 0.0 collective-permute-done.6
  115.4 0.4 fusion.3.base_ref
  115.8 0.0 all-to-all-done.rows_ref
  115.8 9.8 %rank_products.1 = bf16[32,192,128]{2,1,0:T(8,128)(2,1)} custom-call(bf16[32,464,128]{2,1,0:T(8,128)(2,1)} %all-to-all-done.rows_ref, bf16[1024,1024]{1,0:T(8,128)(2,1)} %bitcast.64, bf16[1024,128]{1,0:T(8,128)(2,1)} %bitcast.73), custom_call_target="tpu_custom_call" | custom-call | flops 4294967296 | bytes 8388608 | tf_op jit(solution)/shard_map/rank_products/pallas_call | solution.py:172
  125.6 50.3 %all_to_all.10.returned_ref.first_ref.second_ref = bf16[32,192,128]{2,1,0:T(8,128)(2,1)S(1)} all-to-all(bf16[32,192,128]{2,1,0:T(8,128)(2,1)} %rank_products.1), channel_id=1, replica_groups=mesh['replica'=32,'tensor'=8] {'replica'}, dimensions={0} | all-to-all | bytes 3145728 | tf_op jit(solution)/shard_map/all_to_all | solution.py:405
  175.9 0.9 collect.1
  176.8 0.2 collective-permute-start.8
  177.0 4.8 %collective-permute-done.8 = f32[256,128]{1,0:T(8,128)S(1)} collective-permute-done((f32[256,128]{1,0:T(8,128)S(1)}, f32[256,128]{1,0:T(8,128)S(1)}, u32[]{:S(2)}, u32[]{:S(2)}) %collective-permute-start.8) | collective-permute-done | bytes 131104 | tf_op jit(solution)/shard_map/ppermute | solution.py:342
  181.9 0.7 collective-permute-start.10
  182.6 2.6 %collective-permute-start.11 = (f32[256,128]{1,0:T(8,128)S(1)}, f32[256,128]{1,0:T(8,128)S(1)}, u32[]{:S(2)}, u32[]{:S(2)}) collective-permute-start(f32[256,128]{1,0:T(8,128)S(1)} %add.72.a_ref), channel_id=1, source_target_pairs={{0,6},{1,7},{2,0},{3,1},{4,2},{5,3},{6,4},{7,5},{8,14},{9,15},{10,... | collective-permute-start | bytes 393224 | tf_op jit(solution)/shard_map/ppermute | solution.py:342
  185.2 1.0 collective-permute-start.9
  186.2 2.9 %collective-permute-done.10.c_ref = f32[256,128]{1,0:T(8,128)S(1)} collective-permute-done((f32[256,128]{1,0:T(8,128)S(1)}, f32[256,128]{1,0:T(8,128)S(1)}, u32[]{:S(2)}, u32[]{:S(2)}) %collective-permute-start.10) | collective-permute-done | bytes 131104 | tf_op jit(solution)/shard_map/ppermute | solution.py:342
  189.1 0.1 collective-permute-done.11.d_ref
  189.1 2.5 %collective-permute-done.9.b_ref = f32[256,128]{1,0:T(8,128)S(1)} collective-permute-done((f32[256,128]{1,0:T(8,128)S(1)}, f32[256,128]{1,0:T(8,128)S(1)}, u32[]{:S(2)}, u32[]{:S(2)}) %collective-permute-start.9) | collective-permute-done | bytes 131104 | tf_op jit(solution)/shard_map/ppermute | solution.py:342
  191.7 6.2 %finish.1 = (bf16[512,256]{1,0:T(8,128)(2,1)S(1)}, bf16[128,4,1024]{2,1,0:T(4,128)(2,1)}) custom-call(s32[512,1]{1,0:T(8,128)S(1)} %get-tuple-element.14.fetch_ref, f32[256,128]{1,0:T(8,128)S(1)} %add.72.a_ref, f32[256,128]{1,0:T(8,128)S(1)} %collective-permute-done.9.b_ref, f32[256,128]{1,0:T(8,128)S(1)} %collective-permute-done.10.c_ref, ...), custom_call_target="tpu_custom_call" | custom-call | tf_op jit(solution)/shard_map/finish/pallas_call | solution.py:321
  197.9 0.8 reshape.99
  (32 shorter events, 0.1 us)
Async XLA Ops:
  0.6 1.4 copy-start.6
  0.6 1.4 copy-start.7
  0.7 1.4 copy-start.5
  6.2 1.8 copy-start
  8.0 15.5 %copy-start.19 = (s32[128]{0:T(128)S(1)}, s32[128]{0:T(128)}, u32[]{:S(2)}) copy-start(s32[128]{0:T(128)} %param.15) | copy-start | bytes 1540
  8.0 107.8 %all-to-all-start = ((bf16[32,464,128]{2,1,0:T(8,128)(2,1)}), bf16[32,464,128]{2,1,0:T(8,128)(2,1)}, u32[]{:S(2)}, u32[]{:S(2)}) async-start(bf16[32,464,128]{2,1,0:T(8,128)(2,1)} %copy-done), calls=%async_computation | async-start | bytes 7602176 | tf_op jit(solution)/shard_map/all_to_all | solution.py:391
  19.6 26.5 %collective-permute-start.1 = (bf16[512,1024]{1,0:T(8,128)(2,1)S(1)}, bf16[512,1024]{1,0:T(8,128)(2,1)S(1)}, u32[]{:S(2)}, u32[]{:S(2)}) collective-permute-start(bf16[512,1024]{1,0:T(8,128)(2,1)S(1)} %reshape.87.tokens_ref), channel_id=1, source_target_pairs={{0,2},{1,3},{2,4},{3,5},{4,6},{5,7},{6,0},{7,1},{8,10},{9,11},{10,... | collective-permute-start | bytes 3145736 | tf_op jit(solution)/shard_map/ppermute | solution.py:342
  21.2 31.4 %collective-permute-start.2 = (bf16[512,1024]{1,0:T(8,128)(2,1)S(1)}, bf16[512,1024]{1,0:T(8,128)(2,1)}, u32[]{:S(2)}, u32[]{:S(2)}) collective-permute-start(bf16[512,1024]{1,0:T(8,128)(2,1)S(1)} %reshape.87.tokens_ref), channel_id=1, source_target_pairs={{0,6},{1,7},{2,0},{3,1},{4,2},{5,3},{6,4},{7,5},{8,14},{9,15},{10,... | collective-permute-start | bytes 3145736 | tf_op jit(solution)/shard_map/ppermute | solution.py:342
  22.9 47.4 %collective-permute-start = (bf16[512,1024]{1,0:T(8,128)(2,1)S(1)}, bf16[512,1024]{1,0:T(8,128)(2,1)}, u32[]{:S(2)}, u32[]{:S(2)}) collective-permute-start(bf16[512,1024]{1,0:T(8,128)(2,1)S(1)} %reshape.87.tokens_ref), channel_id=1, source_target_pairs={{0,1},{1,0},{2,3},{3,2},{4,5},{5,4},{6,7},{7,6},{8,9},{9,8},{10,11... | collective-permute-start | bytes 3145736 | tf_op jit(solution)/shard_map/ppermute | solution.py:342
  46.1 1.2 copy-start.10
  47.0 28.4 %collective-permute-start.3 = (bf16[256,1024]{1,0:T(8,128)(2,1)}, bf16[256,1024]{1,0:T(8,128)(2,1)}, u32[]{:S(2)}, u32[]{:S(2)}) collective-permute-start(bf16[256,1024]{1,0:T(8,128)(2,1)} %slice.8), channel_id=1, source_target_pairs={{0,2},{1,3},{2,4},{3,5},{4,6},{5,7},{6,0},{7,1},{8,10},{9,11},{10,... | collective-permute-start | bytes 1572872 | tf_op jit(solution)/shard_map/ppermute | solution.py:342
  53.7 22.8 %collective-permute-start.4 = (bf16[256,1024]{1,0:T(8,128)(2,1)S(1)}, bf16[256,1024]{1,0:T(8,128)(2,1)S(1)}, u32[]{:S(2)}, u32[]{:S(2)}) collective-permute-start(bf16[256,1024]{1,0:T(8,128)(2,1)S(1)} %slice.9), channel_id=1, source_target_pairs={{0,6},{1,7},{2,0},{3,1},{4,2},{5,3},{6,4},{7,5},{8,14},{9,15},{10,... | collective-permute-start | bytes 1572872 | tf_op jit(solution)/shard_map/ppermute | solution.py:342
  56.7 1.4 copy-start.8
  58.1 1.4 copy-start.9
  59.5 14.1 %copy-start.13 = (bf16[1024,2,128]{2,1,0:T(2,128)(2,1)S(1)}, bf16[1024,2,128]{2,1,0:T(2,128)(2,1)}, u32[]{:S(2)}) copy-start(bf16[1024,2,128]{2,1,0:T(2,128)(2,1)} %get-tuple-element.31) | copy-start | bytes 1572868
  59.5 14.1 %copy-start.15 = (f32[256,512]{0,1:T(8,128)S(1)}, f32[256,512]{0,1:T(8,128)}, u32[]{:S(2)}) copy-start(f32[256,512]{0,1:T(8,128)} %fusion.23) | copy-start | bytes 1572868
  65.5 11.0 %copy-start.1 = (f32[16,256,128]{2,1,0:T(8,128)}, f32[16,256,128]{2,1,0:T(8,128)S(1)}, u32[]{:S(2)}) copy-start(f32[16,256,128]{2,1,0:T(8,128)S(1)} %get-tuple-element.22.mixed_ref) | copy-start | bytes 6291460
  65.6 11.0 %copy-start.3 = (f32[16,256,128]{2,1,0:T(8,128)}, f32[16,256,128]{2,1,0:T(8,128)S(1)}, u32[]{:S(2)}) copy-start(f32[16,256,128]{2,1,0:T(8,128)S(1)} %get-tuple-element.23.weight_ref) | copy-start | bytes 6291460
  70.3 26.0 %collective-permute-start.5 = (bf16[512,1024]{1,0:T(8,128)(2,1)}, bf16[512,1024]{1,0:T(8,128)(2,1)S(1)}, u32[]{:S(2)}, u32[]{:S(2)}) collective-permute-start(bf16[512,1024]{1,0:T(8,128)(2,1)} %collective-permute-done), channel_id=1, source_target_pairs={{0,2},{1,3},{2,4},{3,5},{4,6},{5,7},{6,0},{7,1},{8,10},{9,11},{10,... | collective-permute-start | bytes 3145736 | tf_op jit(solution)/shard_map/ppermute | solution.py:342
  71.8 43.5 %collective-permute-start.6 = (bf16[512,1024]{1,0:T(8,128)(2,1)}, bf16[512,1024]{1,0:T(8,128)(2,1)S(1)}, u32[]{:S(2)}, u32[]{:S(2)}) collective-permute-start(bf16[512,1024]{1,0:T(8,128)(2,1)} %collective-permute-done), channel_id=1, source_target_pairs={{0,6},{1,7},{2,0},{3,1},{4,2},{5,3},{6,4},{7,5},{8,14},{9,15},{10,... | collective-permute-start | bytes 3145736 | tf_op jit(solution)/shard_map/ppermute | solution.py:342
  73.6 4.6 %copy-start.18 = (bf16[1024,2,128]{2,1,0:T(2,128)(2,1)S(1)}, bf16[1024,2,128]{2,1,0:T(2,128)(2,1)}, u32[]{:S(2)}) copy-start(bf16[1024,2,128]{2,1,0:T(2,128)(2,1)} %get-tuple-element.29) | copy-start | bytes 1572868
  75.3 4.6 %copy-start.17 = (bf16[1024,2,128]{2,1,0:T(2,128)(2,1)S(1)}, bf16[1024,2,128]{2,1,0:T(2,128)(2,1)}, u32[]{:S(2)}) copy-start(bf16[1024,2,128]{2,1,0:T(2,128)(2,1)} %get-tuple-element.28) | copy-start | bytes 1572868
  76.6 38.3 %collective-permute-start.7 = (bf16[512,1024]{1,0:T(8,128)(2,1)S(1)}, bf16[512,1024]{1,0:T(8,128)(2,1)S(1)}, u32[]{:S(2)}, u32[]{:S(2)}) collective-permute-start(bf16[512,1024]{1,0:T(8,128)(2,1)S(1)} %constant_dynamic-update-slice_fusion), channel_id=1, source_target_pairs={{0,1},{1,0},{2,3},{3,2},{4,5},{5,4},{6,7},{7,6},{8,9},{9,8},{10,11... | collective-permute-start | bytes 3145736 | tf_op jit(solution)/shard_map/ppermute | solution.py:342
  78.2 2.3 %copy-start.11 = (bf16[512,1024]{1,0:T(8,128)(2,1)S(1)}, bf16[512,1024]{1,0:T(8,128)(2,1)}, u32[]{:S(2)}) copy-start(bf16[512,1024]{1,0:T(8,128)(2,1)} %copy-done.10) | copy-start | bytes 3145732
  78.2 2.3 %copy-start.12 = (bf16[1024,2,128]{2,1,0:T(2,128)(2,1)S(1)}, bf16[1024,2,128]{2,1,0:T(2,128)(2,1)}, u32[]{:S(2)}) copy-start(bf16[1024,2,128]{2,1,0:T(2,128)(2,1)} %get-tuple-element.30) | copy-start | bytes 1572868
  80.9 34.0 %copy-start.16 = (bf16[1024,2,128]{2,1,0:T(2,128)(2,1)S(1)}, bf16[1024,2,128]{2,1,0:T(2,128)(2,1)}, u32[]{:S(2)}) copy-start(bf16[1024,2,128]{2,1,0:T(2,128)(2,1)} %get-tuple-element.33) | copy-start | bytes 1572868
  96.4 19.0 %copy-start.14 = (bf16[1024,2,128]{2,1,0:T(2,128)(2,1)S(1)}, bf16[1024,2,128]{2,1,0:T(2,128)(2,1)}, u32[]{:S(2)}) copy-start(bf16[1024,2,128]{2,1,0:T(2,128)(2,1)} %get-tuple-element.26) | copy-start | bytes 1572868
  125.6 66.1 %copy-start.2 = (f32[16,256,128]{2,1,0:T(8,128)S(1)}, f32[16,256,128]{2,1,0:T(8,128)}, u32[]{:S(2)}) copy-start(f32[16,256,128]{2,1,0:T(8,128)} %copy-done.1) | copy-start | bytes 6291460
  125.6 66.1 %copy-start.4 = (f32[16,256,128]{2,1,0:T(8,128)S(1)}, f32[16,256,128]{2,1,0:T(8,128)}, u32[]{:S(2)}) copy-start(f32[16,256,128]{2,1,0:T(8,128)} %copy-done.3) | copy-start | bytes 6291460
  176.8 5.1 %collective-permute-start.8 = (f32[256,128]{1,0:T(8,128)S(1)}, f32[256,128]{1,0:T(8,128)S(1)}, u32[]{:S(2)}, u32[]{:S(2)}) collective-permute-start(f32[256,128]{1,0:T(8,128)S(1)} %collect.1), channel_id=1, source_target_pairs={{0,1},{1,0},{2,3},{3,2},{4,5},{5,4},{6,7},{7,6},{8,9},{9,8},{10,11... | collective-permute-start | bytes 393224 | tf_op jit(solution)/shard_map/ppermute | solution.py:342
  181.9 7.2 %collective-permute-start.10 = (f32[256,128]{1,0:T(8,128)S(1)}, f32[256,128]{1,0:T(8,128)S(1)}, u32[]{:S(2)}, u32[]{:S(2)}) collective-permute-start(f32[256,128]{1,0:T(8,128)S(1)} %add.72.a_ref), channel_id=1, source_target_pairs={{0,2},{1,3},{2,4},{3,5},{4,6},{5,7},{6,0},{7,1},{8,10},{9,11},{10,... | collective-permute-start | bytes 393224 | tf_op jit(solution)/shard_map/ppermute | solution.py:342
  182.6 6.5 %collective-permute-start.11 = (f32[256,128]{1,0:T(8,128)S(1)}, f32[256,128]{1,0:T(8,128)S(1)}, u32[]{:S(2)}, u32[]{:S(2)}) collective-permute-start(f32[256,128]{1,0:T(8,128)S(1)} %add.72.a_ref), channel_id=1, source_target_pairs={{0,6},{1,7},{2,0},{3,1},{4,2},{5,3},{6,4},{7,5},{8,14},{9,15},{10,... | collective-permute-start | bytes 393224 | tf_op jit(solution)/shard_map/ppermute | solution.py:342
  185.2 6.5 %collective-permute-start.9 = (f32[256,128]{1,0:T(8,128)S(1)}, f32[256,128]{1,0:T(8,128)S(1)}, u32[]{:S(2)}, u32[]{:S(2)}) collective-permute-start(f32[256,128]{1,0:T(8,128)S(1)} %add.72.a_ref), channel_id=1, source_target_pairs={{0,4},{1,5},{2,6},{3,7},{4,0},{5,1},{6,2},{7,3},{8,12},{9,13},{10,... | collective-permute-start | bytes 393224 | tf_op jit(solution)/shard_map/ppermute | solution.py:342

commit v4 on v3

--- a/solution.py
+++ b/solution.py
@@ -11,7 +11,7 @@
 BLK = 7
 PAIR = 2
 PAIR_ROWS = PAIR * BLK
-ASK_ROWS = 16
+ASK_ROWS = 8
 RETURN_ROWS = 64
 LANES = 128
 GROUP = 8
@@ -363,7 +363,7 @@
     base = product(tokens, 0, 0) + product(across, 0, 1)
     base = base + product(right, 1, 0) + product(left, -1, 0)
     base = base + product(far, 2, 0) + product(right_across, 1, 1) + product(left_across, -1, 1)
-    return base + product(far_across, 2, 1)
+    return base, lambda: product(far_across, 2, 1)
 
 
 def per_device(
@@ -390,12 +390,12 @@
     )
     received = lax.all_to_all(sent, "replica", split_axis=0, concat_axis=0, tiled=True)
 
-    base = project(tokens, key_value_weight)
+    near, last = project(tokens, key_value_weight)
     query_tokens = queries.reshape(token_count, -1)
     mixed, weight = cached_attention(lengths, query_tokens, key_cache_rows, value_cache_rows, steps)
 
     down = adapter_down_weight.reshape(held * sides * rank, depth).T
-    received, base, mixed, weight, down = lax.optimization_barrier((received, base, mixed, weight, down))
+    received, near, mixed, weight, down = lax.optimization_barrier((received, near, mixed, weight, down))
     products = rank_products(
         received,
         down,
@@ -406,7 +406,7 @@
     mine = collect(column, returned)
     mine = mine + shifted(mine, 0, 1)
     parts = (mine, shifted(mine, 2, 0), shifted(mine, 1, 0), shifted(mine, -1, 0))
-    fresh, attended = finish(fetch, parts, returned, base, query_tokens, mixed, weight, steps, rank)
+    fresh, attended = finish(fetch, parts, returned, near + last(), query_tokens, mixed, weight, steps, rank)
     return fresh.reshape(row_count, steps, sides, HD), attended
 
 

time: 199 us -> 189 us (0.950)
  blocking collectives: 50.3 us -> 0 us
  waiting for transfers between devices: 64.1 us -> 95.9 us
  starting transfers between devices: 28.2 us -> 36 us
  matrix products: 6.98 us -> 9.44 us
  local copies, waits for them, and re-layouts: 21 us -> 18.8 us
    all_to_all x1 -> x0, blocking collectives: 50.3 us -> none  [per_device(): lax.all_to_all(products, 'replica', split_axis=0, concat_axis=0, tiled=True)]
    all_to_all x0 -> x1, waiting for transfers between devices: none -> 41.1 us  [per_device(): lax.all_to_all(products, 'replica', split_axis=0, concat_axis=0, tiled=True)]
    ppermute x12, waiting for transfers between devices: 64.1 us -> 47.5 us  [shifted(): return lax.ppermute(value, 'tensor', pairs)]
    all_to_all x0 -> x1, starting transfers between devices: none -> 7.9 us  [per_device(): lax.all_to_all(products, 'replica', split_axis=0, concat_axis=0, tiled=True)]
    all_to_all x1, waiting for transfers between devices: 0.01 us -> 7.38 us  [per_device(): lax.all_to_all(sent, 'replica', split_axis=0, concat_axis=0, tiled=True)]
    dot_general x8, matrix products: 6.98 us -> 9.44 us  [product(): jnp.dot(piece, part.reshape(depth, -1), preferred_element_type=jnp.float32)]
    unnamed x41 -> x29, local copies, waits for them, and re-layouts: 5.83 us -> 5.2 us
  transfers between devices with their start and end apart: 13 -> 14, of which waited for: 8 -> 9; matrix products, arithmetic and copies ran while one was open for 11% -> 11% of each run, Pallas kernels for 3% -> 4%
where the time goes in v4:
time: 189 us; the launch traced here: 188 us
  waiting for transfers between devices  95.9 us (51%)
  starting transfers between devices  36 us (19%)
  Pallas kernels  27.1 us (14%)
  local copies, waits for them, and re-layouts  18.8 us (10%)
  matrix products  9.44 us (5%)
    ppermute x12, waiting for transfers between devices, shifted(): return lax.ppermute(value, 'tensor', pairs)  47.5 us
    all_to_all x1, waiting for transfers between devices, per_device(): lax.all_to_all(products, 'replica', split_axis=0, concat_axis=0, tiled=True)  41.1 us
    ppermute x12, starting transfers between devices, shifted(): return lax.ppermute(value, 'tensor', pairs)  16.7 us
    all_to_all x1, starting transfers between devices, per_device(): lax.all_to_all(sent, 'replica', split_axis=0, concat_axis=0, tiled=True)  11.4 us
    pallas_call x1, Pallas kernels, rank_products(): pl.pallas_call(functools.partial(rank_kernel, steps), grid=(replicas // h...  9.77 us
    dot_general x8, matrix products, product(): jnp.dot(piece, part.reshape(depth, -1), preferred_element_type=jnp.float32)  9.44 us
    all_to_all x1, starting transfers between devices, per_device(): lax.all_to_all(products, 'replica', split_axis=0, concat_axis=0, tiled=True)  7.9 us
    all_to_all x1, waiting for transfers between devices, per_device(): lax.all_to_all(sent, 'replica', split_axis=0, concat_axis=0, tiled=True)  7.38 us
  transfers between devices with their start and end apart: 14, of which 9 were waited for; matrix products, arithmetic and copies ran while one was open for 11% of the time, Pallas kernels for 4%

profile of v4, /device:TPU:32, one launch (start us, length us, event | category | flops | bytes accessed | tf_op | source)
XLA Modules:
  0.0 188.2 jit_solution(15766363535354243069)
XLA Ops:
  0.6 0.0 copy-start.6
  0.6 0.0 copy-start.7
  0.7 0.0 copy-start.5
  0.7 1.4 reshape.87.tokens_ref
  2.0 0.0 copy-done.6
  2.0 0.0 copy-done.7
  2.1 4.2 %place_rows.1 = (bf16[32,456,128]{2,1,0:T(8,128)(2,1)S(1)}, s32[512,1]{1,0:T(8,128)S(1)}, s32[512,1]{1,0:T(8,128)S(1)}) custom-call(s32[1,32]{1,0:T(1,128)S(1)} %bitcast.59, s32[1,128]{1,0:T(1,128)S(1)} %bitcast.60, s32[1,512]{1,0:T(1,128)S(1)} %bitcast.58, bf16[512,1024]{1,0:T(8,128)(2,1)S(1)} %reshape.87.tokens_ref), custom_call_target="tpu_custom_call" | custom-call | tf_op jit(solution)/shard_map/place_rows/pallas_call | solution.py:105
  6.2 1.8 copy-done
  8.1 11.4 %all-to-all-start = ((bf16[32,456,128]{2,1,0:T(8,128)(2,1)}), bf16[32,456,128]{2,1,0:T(8,128)(2,1)}, u32[]{:S(2)}, u32[]{:S(2)}) async-start(bf16[32,456,128]{2,1,0:T(8,128)(2,1)} %copy-done), calls=%async_computation | async-start | bytes 7471104 | tf_op jit(solution)/shard_map/all_to_all | solution.py:391
  19.5 0.0 copy-start.13
  19.5 1.6 collective-permute-start.1
  21.1 1.7 collective-permute-start.2
  22.8 0.7 collective-permute-start
  23.5 1.3 reshape.95.queries_ref
  24.8 0.1 lt.62
  24.9 0.1 lt.63
  25.0 0.1 lt.64
  25.1 0.1 lt.60
  25.2 3.9 %copy.26 = bf16[1024,1024]{0,1:T(8,128)(2,1)} copy(bf16[1024,1024]{1,0:T(8,128)(2,1)} %bitcast.61) | data formatting | bytes 4194304 | tf_op jit(solution)/shard_map/reshape | solution.py:397
  29.2 0.0 copy-start.8
  29.2 1.4 copy-done.8
  30.6 1.4 copy-done.9
  32.0 6.0 %cached_attention.1 = (f32[16,256,128]{2,1,0:T(8,128)S(1)}, f32[16,256,128]{2,1,0:T(8,128)S(1)}) custom-call(f32[16,1,384]{2,1,0:T(1,128)S(1)} %compare_select_fusion.bias_ref, bf16[512,1024]{1,0:T(8,128)(2,1)S(1)} %reshape.95.queries_ref, bf16[128,48,128]{2,1,0:T(8,128)(2,1)S(1)} %copy-done.8, bf16[128,48,128]{2,1,0:T(8,128)(2,1)S(1)} %copy-done.9), custom_call_target="tpu_custom_call" | custom-call | flops 2147483648 | bytes 8388608 | tf_op jit(solution)/shard_map/cached_attention/pallas_call | solution.py:243
  38.0 3.6 %constant_dynamic-slice_fusion = (bf16[1024,2,128]{2,1,0:T(2,128)(2,1)}, bf16[1024,2,128]{2,1,0:T(2,128)(2,1)S(1)}, bf16[1024,2,128]{2,1,0:T(2,128)(2,1)S(1)}, b...) fusion(bf16[8192,2,128]{2,1,0:T(2,128)(2,1)S(1)} %copy-done.10,, ...), kind=kLoop, calls=%fused_computation.32 | loop fusion | bytes 8388640 | tf_op jit(solution)/shard_map/dynamic_slice | solution.py:353
  41.7 0.5 fusion.21
  42.1 3.9 %collective-permute-done.1 = bf16[512,1024]{1,0:T(8,128)(2,1)} collective-permute-done((bf16[512,1024]{1,0:T(8,128)(2,1)S(1)}, bf16[512,1024]{1,0:T(8,128)(2,1)}, u32[]{:S(2)}, u32[]{:S(2)}) %collective-permute-start.1) | collective-permute-done | bytes 1048608 | tf_op jit(solution)/shard_map/ppermute | solution.py:342
  46.1 1.1 slice.8
  47.2 0.4 collective-permute-start.3
  47.5 0.0 collective-permute-done.2
  47.5 1.1 slice.9
  48.6 3.0 %collective-permute-start.4 = (bf16[256,1024]{1,0:T(8,128)(2,1)S(1)}, bf16[256,1024]{1,0:T(8,128)(2,1)S(1)}, u32[]{:S(2)}, u32[]{:S(2)}) collective-permute-start(bf16[256,1024]{1,0:T(8,128)(2,1)S(1)} %slice.9), channel_id=1, source_target_pairs={{0,6},{1,7},{2,0},{3,1},{4,2},{5,3},{6,4},{7,5},{8,14},{9,15},{10,... | collective-permute-start | bytes 1572872 | tf_op jit(solution)/shard_map/ppermute | solution.py:342
  51.6 18.2 %collective-permute-done = bf16[512,1024]{1,0:T(8,128)(2,1)} collective-permute-done((bf16[512,1024]{1,0:T(8,128)(2,1)S(1)}, bf16[512,1024]{1,0:T(8,128)(2,1)}, u32[]{:S(2)}, u32[]{:S(2)}) %collective-permute-start) | collective-permute-done | bytes 1048608 | tf_op jit(solution)/shard_map/ppermute | solution.py:342
  69.8 1.5 collective-permute-start.5
  71.3 1.7 collective-permute-start.6
  73.1 1.7 convolution_add_fusion.1
  74.8 1.7 fusion.14
  76.5 0.0 collective-permute-done.3
  76.5 0.0 collective-permute-done.4
  76.6 0.0 copy-start.12
  76.6 0.5 fusion.11
  77.0 0.5 copy-done.12
  77.5 1.7 fusion.4
  79.2 16.7 %collective-permute-done.5 = bf16[512,1024]{1,0:T(8,128)(2,1)S(1)} collective-permute-done((bf16[512,1024]{1,0:T(8,128)(2,1)}, bf16[512,1024]{1,0:T(8,128)(2,1)S(1)}, u32[]{:S(2)}, u32[]{:S(2)}) %collective-permute-start.5) | collective-permute-done | bytes 1048608 | tf_op jit(solution)/shard_map/ppermute | solution.py:342
  95.9 0.4 fusion.3
  96.3 0.0 collective-permute-done.6
  96.4 1.2 fusion.2
  97.6 7.4 %all-to-all-done.rows_ref = bf16[32,456,128]{2,1,0:T(8,128)(2,1)} async-done(((bf16[32,456,128]{2,1,0:T(8,128)(2,1)}), bf16[32,456,128]{2,1,0:T(8,128)(2,1)}, u32[]{:S(2)}, u32[]{:S(2)}) %all-to-all-start) | async-done | bytes 3735584 | tf_op jit(solution)/shard_map/all_to_all | solution.py:391
  105.0 9.8 %rank_products.1 = bf16[32,192,128]{2,1,0:T(8,128)(2,1)} custom-call(bf16[32,456,128]{2,1,0:T(8,128)(2,1)} %all-to-all-done.rows_ref, bf16[1024,1024]{1,0:T(8,128)(2,1)} %bitcast.62, bf16[1024,128]{1,0:T(8,128)(2,1)} %bitcast.71), custom_call_target="tpu_custom_call" | custom-call | flops 4294967296 | bytes 8388608 | tf_op jit(solution)/shard_map/rank_products/pallas_call | solution.py:172
  114.7 7.9 %all-to-all-start.1 = ((bf16[32,192,128]{2,1,0:T(8,128)(2,1)}), bf16[32,192,128]{2,1,0:T(8,128)(2,1)S(1)}, u32[]{:S(2)}, u32[]{:S(2)}) async-start(bf16[32,192,128]{2,1,0:T(8,128)(2,1)} %rank_products.1), calls=%async_computation.1 | async-start | bytes 3145728 | tf_op jit(solution)/shard_map/all_to_all | solution.py:405
  122.6 0.8 collective-permute-start.11
  123.4 41.1 %all-to-all-done.1.returned_ref.first_ref.second_ref = bf16[32,192,128]{2,1,0:T(8,128)(2,1)S(1)} async-done(((bf16[32,192,128]{2,1,0:T(8,128)(2,1)}), bf16[32,192,128]{2,1,0:T(8,128)(2,1)S(1)}, u32[]{:S(2)}, u32[]{:S(2)}) %all-to-all-start.1) | async-done | bytes 1572896 | tf_op jit(solution)/shard_map/all_to_all | solution.py:405
  164.5 0.9 collect.1
  165.4 0.8 collective-permute-start.7
  166.2 4.3 %collective-permute-done.7 = f32[256,128]{1,0:T(8,128)S(1)} collective-permute-done((f32[256,128]{1,0:T(8,128)S(1)}, f32[256,128]{1,0:T(8,128)S(1)}, u32[]{:S(2)}, u32[]{:S(2)}) %collective-permute-start.7) | collective-permute-done | bytes 131104 | tf_op jit(solution)/shard_map/ppermute | solution.py:342
  170.5 2.8 %collective-permute-start.10 = (f32[256,128]{1,0:T(8,128)S(1)}, f32[256,128]{1,0:T(8,128)S(1)}, u32[]{:S(2)}, u32[]{:S(2)}) collective-permute-start(f32[256,128]{1,0:T(8,128)S(1)} %add.70.a_ref), channel_id=1, source_target_pairs={{0,6},{1,7},{2,0},{3,1},{4,2},{5,3},{6,4},{7,5},{8,14},{9,15},{10,... | collective-permute-start | bytes 393224 | tf_op jit(solution)/shard_map/ppermute | solution.py:342
  173.3 0.8 collective-permute-start.8
  174.1 0.9 collective-permute-start.9
  175.0 0.0 collective-permute-done.11
  175.0 1.8 convolution_add_fusion.2.base_ref
  176.8 0.8 collective-permute-done.10.d_ref
  177.6 2.3 %collective-permute-done.8.b_ref = f32[256,128]{1,0:T(8,128)S(1)} collective-permute-done((f32[256,128]{1,0:T(8,128)S(1)}, f32[256,128]{1,0:T(8,128)S(1)}, u32[]{:S(2)}, u32[]{:S(2)}) %collective-permute-start.8) | collective-permute-done | bytes 131104 | tf_op jit(solution)/shard_map/ppermute | solution.py:342
  179.9 1.3 collective-permute-done.9.c_ref
  181.2 6.2 %finish.1 = (bf16[512,256]{1,0:T(8,128)(2,1)S(1)}, bf16[128,4,1024]{2,1,0:T(4,128)(2,1)}) custom-call(s32[512,1]{1,0:T(8,128)S(1)} %get-tuple-element.14.fetch_ref, f32[256,128]{1,0:T(8,128)S(1)} %add.70.a_ref, f32[256,128]{1,0:T(8,128)S(1)} %collective-permute-done.8.b_ref, f32[256,128]{1,0:T(8,128)S(1)} %collective-permute-done.9.c_ref, ...), custom_call_target="tpu_custom_call" | custom-call | tf_op jit(solution)/shard_map/finish/pallas_call | solution.py:321
  187.4 0.8 reshape.99
  (21 shorter events, 0.1 us)
Async XLA Ops:
  0.6 1.4 copy-start.6
  0.6 1.4 copy-start.7
  0.7 1.4 copy-start.5
  6.2 1.8 copy-start
  8.1 96.9 %all-to-all-start = ((bf16[32,456,128]{2,1,0:T(8,128)(2,1)}), bf16[32,456,128]{2,1,0:T(8,128)(2,1)}, u32[]{:S(2)}, u32[]{:S(2)}) async-start(bf16[32,456,128]{2,1,0:T(8,128)(2,1)} %copy-done), calls=%async_computation | async-start | bytes 7471104 | tf_op jit(solution)/shard_map/all_to_all | solution.py:391
  19.5 5.3 %copy-start.13 = (s32[128]{0:T(128)S(1)}, s32[128]{0:T(128)}, u32[]{:S(2)}) copy-start(s32[128]{0:T(128)} %param.15) | copy-start | bytes 1540
  19.5 26.6 %collective-permute-start.1 = (bf16[512,1024]{1,0:T(8,128)(2,1)S(1)}, bf16[512,1024]{1,0:T(8,128)(2,1)}, u32[]{:S(2)}, u32[]{:S(2)}) collective-permute-start(bf16[512,1024]{1,0:T(8,128)(2,1)S(1)} %reshape.87.tokens_ref), channel_id=1, source_target_pairs={{0,2},{1,3},{2,4},{3,5},{4,6},{5,7},{6,0},{7,1},{8,10},{9,11},{10,... | collective-permute-start | bytes 3145736 | tf_op jit(solution)/shard_map/ppermute | solution.py:342
  21.1 26.5 %collective-permute-start.2 = (bf16[512,1024]{1,0:T(8,128)(2,1)S(1)}, bf16[512,1024]{1,0:T(8,128)(2,1)}, u32[]{:S(2)}, u32[]{:S(2)}) collective-permute-start(bf16[512,1024]{1,0:T(8,128)(2,1)S(1)} %reshape.87.tokens_ref), channel_id=1, source_target_pairs={{0,6},{1,7},{2,0},{3,1},{4,2},{5,3},{6,4},{7,5},{8,14},{9,15},{10,... | collective-permute-start | bytes 3145736 | tf_op jit(solution)/shard_map/ppermute | solution.py:342
  22.8 47.0 %collective-permute-start = (bf16[512,1024]{1,0:T(8,128)(2,1)S(1)}, bf16[512,1024]{1,0:T(8,128)(2,1)}, u32[]{:S(2)}, u32[]{:S(2)}) collective-permute-start(bf16[512,1024]{1,0:T(8,128)(2,1)S(1)} %reshape.87.tokens_ref), channel_id=1, source_target_pairs={{0,1},{1,0},{2,3},{3,2},{4,5},{5,4},{6,7},{7,6},{8,9},{9,8},{10,11... | collective-permute-start | bytes 3145736 | tf_op jit(solution)/shard_map/ppermute | solution.py:342
  29.2 1.4 copy-start.8
  30.6 1.4 copy-start.9
  32.0 6.0 %copy-start.10 = (bf16[8192,2,128]{2,1,0:T(2,128)(2,1)S(1)}, bf16[8192,2,128]{2,1,0:T(2,128)(2,1)}, u32[]{:S(2)}) copy-start(bf16[8192,2,128]{2,1,0:T(2,128)(2,1)} %param.19) | copy-start | bytes 12582916
  38.0 3.7 %copy-start.1 = (f32[16,256,128]{2,1,0:T(8,128)}, f32[16,256,128]{2,1,0:T(8,128)S(1)}, u32[]{:S(2)}) copy-start(f32[16,256,128]{2,1,0:T(8,128)S(1)} %get-tuple-element.22.mixed_ref) | copy-start | bytes 6291460
  38.0 3.7 %copy-start.3 = (f32[16,256,128]{2,1,0:T(8,128)}, f32[16,256,128]{2,1,0:T(8,128)S(1)}, u32[]{:S(2)}) copy-start(f32[16,256,128]{2,1,0:T(8,128)S(1)} %get-tuple-element.23.weight_ref) | copy-start | bytes 6291460
  47.2 29.3 %collective-permute-start.3 = (bf16[256,1024]{1,0:T(8,128)(2,1)S(1)}, bf16[256,1024]{1,0:T(8,128)(2,1)S(1)}, u32[]{:S(2)}, u32[]{:S(2)}) collective-permute-start(bf16[256,1024]{1,0:T(8,128)(2,1)S(1)} %slice.8), channel_id=1, source_target_pairs={{0,2},{1,3},{2,4},{3,5},{4,6},{5,7},{6,0},{7,1},{8,10},{9,11},{10,... | collective-permute-start | bytes 1572872 | tf_op jit(solution)/shard_map/ppermute | solution.py:342
  48.6 27.9 %collective-permute-start.4 = (bf16[256,1024]{1,0:T(8,128)(2,1)S(1)}, bf16[256,1024]{1,0:T(8,128)(2,1)S(1)}, u32[]{:S(2)}, u32[]{:S(2)}) collective-permute-start(bf16[256,1024]{1,0:T(8,128)(2,1)S(1)} %slice.9), channel_id=1, source_target_pairs={{0,6},{1,7},{2,0},{3,1},{4,2},{5,3},{6,4},{7,5},{8,14},{9,15},{10,... | collective-permute-start | bytes 1572872 | tf_op jit(solution)/shard_map/ppermute | solution.py:342
  69.8 26.1 %collective-permute-start.5 = (bf16[512,1024]{1,0:T(8,128)(2,1)}, bf16[512,1024]{1,0:T(8,128)(2,1)S(1)}, u32[]{:S(2)}, u32[]{:S(2)}) collective-permute-start(bf16[512,1024]{1,0:T(8,128)(2,1)} %collective-permute-done), channel_id=1, source_target_pairs={{0,2},{1,3},{2,4},{3,5},{4,6},{5,7},{6,0},{7,1},{8,10},{9,11},{10,... | collective-permute-start | bytes 3145736 | tf_op jit(solution)/shard_map/ppermute | solution.py:342
  71.3 25.0 %collective-permute-start.6 = (bf16[512,1024]{1,0:T(8,128)(2,1)}, bf16[512,1024]{1,0:T(8,128)(2,1)S(1)}, u32[]{:S(2)}, u32[]{:S(2)}) collective-permute-start(bf16[512,1024]{1,0:T(8,128)(2,1)} %collective-permute-done), channel_id=1, source_target_pairs={{0,6},{1,7},{2,0},{3,1},{4,2},{5,3},{6,4},{7,5},{8,14},{9,15},{10,... | collective-permute-start | bytes 3145736 | tf_op jit(solution)/shard_map/ppermute | solution.py:342
  76.6 1.0 copy-start.12
  114.7 49.8 %all-to-all-start.1 = ((bf16[32,192,128]{2,1,0:T(8,128)(2,1)}), bf16[32,192,128]{2,1,0:T(8,128)(2,1)S(1)}, u32[]{:S(2)}, u32[]{:S(2)}) async-start(bf16[32,192,128]{2,1,0:T(8,128)(2,1)} %rank_products.1), calls=%async_computation.1 | async-start | bytes 3145728 | tf_op jit(solution)/shard_map/all_to_all | solution.py:405
  122.6 52.4 %collective-permute-start.11 = (bf16[512,1024]{1,0:T(8,128)(2,1)}, bf16[512,1024]{1,0:T(8,128)(2,1)}, u32[]{:S(2)}, u32[]{:S(2)}) collective-permute-start(bf16[512,1024]{1,0:T(8,128)(2,1)} %copy-done.12), channel_id=1, source_target_pairs={{0,1},{1,0},{2,3},{3,2},{4,5},{5,4},{6,7},{7,6},{8,9},{9,8},{10,11... | collective-permute-start | bytes 3145736 | tf_op jit(solution)/shard_map/ppermute | solution.py:342
  164.5 10.5 %copy-start.11 = (f32[512,256]{1,0:T(8,128)S(1)}, f32[512,256]{1,0:T(8,128)}, u32[]{:S(2)}) copy-start(f32[512,256]{1,0:T(8,128)} %fusion.2) | copy-start | bytes 1572868
  164.5 16.7 %copy-start.2 = (f32[16,256,128]{2,1,0:T(8,128)S(1)}, f32[16,256,128]{2,1,0:T(8,128)}, u32[]{:S(2)}) copy-start(f32[16,256,128]{2,1,0:T(8,128)} %copy-done.1) | copy-start | bytes 6291460
  164.5 16.7 %copy-start.4 = (f32[16,256,128]{2,1,0:T(8,128)S(1)}, f32[16,256,128]{2,1,0:T(8,128)}, u32[]{:S(2)}) copy-start(f32[16,256,128]{2,1,0:T(8,128)} %copy-done.3) | copy-start | bytes 6291460
  165.4 5.1 %collective-permute-start.7 = (f32[256,128]{1,0:T(8,128)S(1)}, f32[256,128]{1,0:T(8,128)S(1)}, u32[]{:S(2)}, u32[]{:S(2)}) collective-permute-start(f32[256,128]{1,0:T(8,128)S(1)} %collect.1), channel_id=1, source_target_pairs={{0,1},{1,0},{2,3},{3,2},{4,5},{5,4},{6,7},{7,6},{8,9},{9,8},{10,11... | collective-permute-start | bytes 393224 | tf_op jit(solution)/shard_map/ppermute | solution.py:342
  170.5 7.1 %collective-permute-start.10 = (f32[256,128]{1,0:T(8,128)S(1)}, f32[256,128]{1,0:T(8,128)S(1)}, u32[]{:S(2)}, u32[]{:S(2)}) collective-permute-start(f32[256,128]{1,0:T(8,128)S(1)} %add.70.a_ref), channel_id=1, source_target_pairs={{0,6},{1,7},{2,0},{3,1},{4,2},{5,3},{6,4},{7,5},{8,14},{9,15},{10,... | collective-permute-start | bytes 393224 | tf_op jit(solution)/shard_map/ppermute | solution.py:342
  173.3 6.6 %collective-permute-start.8 = (f32[256,128]{1,0:T(8,128)S(1)}, f32[256,128]{1,0:T(8,128)S(1)}, u32[]{:S(2)}, u32[]{:S(2)}) collective-permute-start(f32[256,128]{1,0:T(8,128)S(1)} %add.70.a_ref), channel_id=1, source_target_pairs={{0,4},{1,5},{2,6},{3,7},{4,0},{5,1},{6,2},{7,3},{8,12},{9,13},{10,... | collective-permute-start | bytes 393224 | tf_op jit(solution)/shard_map/ppermute | solution.py:342
  174.1 7.1 %collective-permute-start.9 = (f32[256,128]{1,0:T(8,128)S(1)}, f32[256,128]{1,0:T(8,128)S(1)}, u32[]{:S(2)}, u32[]{:S(2)}) collective-permute-start(f32[256,128]{1,0:T(8,128)S(1)} %add.70.a_ref), channel_id=1, source_target_pairs={{0,2},{1,3},{2,4},{3,5},{4,6},{5,7},{6,0},{7,1},{8,10},{9,11},{10,... | collective-permute-start | bytes 393224 | tf_op jit(solution)/shard_map/ppermute | solution.py:342

commit v5 on v4

--- a/solution.py
+++ b/solution.py
@@ -100,7 +100,7 @@
 def place(first, request, owners, tokens, steps, replicas):
     token_count, depth = tokens.shape
     rows = PAIR_ROWS * steps * depth // LANES + ASK_ROWS
-    here = 4
+    here = 8
     whole = lambda shape: pl.BlockSpec(shape, lambda i: (0, 0))
     return pl.pallas_call(
         functools.partial(place_kernel, steps),
@@ -362,8 +362,8 @@
     far_across = shifted(far, 0, 1)
     base = product(tokens, 0, 0) + product(across, 0, 1)
     base = base + product(right, 1, 0) + product(left, -1, 0)
-    base = base + product(far, 2, 0) + product(right_across, 1, 1) + product(left_across, -1, 1)
-    return base, lambda: product(far_across, 2, 1)
+    base = base + product(far, 2, 0)
+    return base, lambda: product(right_across, 1, 1) + product(left_across, -1, 1) + product(far_across, 2, 1)
 
 
 def per_device(

time: 189 us -> 187 us (0.989)
  waiting for transfers between devices: 95.9 us -> 89.7 us
  matrix products: 9.44 us -> 12.6 us
    all_to_all x1, waiting for transfers between devices: 41.1 us -> 13.7 us  [per_device(): lax.all_to_all(products, 'replica', split_axis=0, concat_axis=0, tiled=True)]
    all_to_all x1, waiting for transfers between devices: 7.38 us -> 29.9 us  [per_device(): lax.all_to_all(sent, 'replica', split_axis=0, concat_axis=0, tiled=True)]
    dot_general x8, matrix products: 9.44 us -> 12.6 us  [product(): jnp.dot(piece, part.reshape(depth, -1), preferred_element_type=jnp.float32)]
    unnamed x29 -> x33, local copies, waits for them, and re-layouts: 5.2 us -> 5.22 us
  transfers between devices with their start and end apart: 14 -> 14, of which waited for: 9 -> 7; matrix products, arithmetic and copies ran while one was open for 11% -> 13% of each run, Pallas kernels for 4% -> 4%
where the time goes in v5:
time: 187 us; the launch traced here: 186 us
  waiting for transfers between devices  89.7 us (48%)
  starting transfers between devices  37.5 us (20%)
  Pallas kernels  26.4 us (14%)
  local copies, waits for them, and re-layouts  18.9 us (10%)
  matrix products  12.6 us (7%)
    ppermute x12, waiting for transfers between devices, shifted(): return lax.ppermute(value, 'tensor', pairs)  46.1 us
    all_to_all x1, waiting for transfers between devices, per_device(): lax.all_to_all(sent, 'replica', split_axis=0, concat_axis=0, tiled=True)  29.9 us
    ppermute x12, starting transfers between devices, shifted(): return lax.ppermute(value, 'tensor', pairs)  18.2 us
    all_to_all x1, waiting for transfers between devices, per_device(): lax.all_to_all(products, 'replica', split_axis=0, concat_axis=0, tiled=True)  13.7 us
    dot_general x8, matrix products, product(): jnp.dot(piece, part.reshape(depth, -1), preferred_element_type=jnp.float32)  12.6 us
    all_to_all x1, starting transfers between devices, per_device(): lax.all_to_all(sent, 'replica', split_axis=0, concat_axis=0, tiled=True)  11.4 us
    pallas_call x1, Pallas kernels, rank_products(): pl.pallas_call(functools.partial(rank_kernel, steps), grid=(replicas // h...  9.77 us
    all_to_all x1, starting transfers between devices, per_device(): lax.all_to_all(products, 'replica', split_axis=0, concat_axis=0, tiled=True)  7.9 us
  transfers between devices with their start and end apart: 14, of which 7 were waited for; matrix products, arithmetic and copies ran while one was open for 13% of the time, Pallas kernels for 4%

profile of v5, /device:TPU:32, one launch (start us, length us, event | category | flops | bytes accessed | tf_op | source)
XLA Modules:
  0.0 186.1 jit_solution(8675173628788735050)
XLA Ops:
  0.7 1.4 reshape.87.tokens_ref
  2.0 0.0 copy-done.6
  2.0 0.0 copy-done.7
  2.0 0.0 copy-done.5
  2.1 3.5 %place_rows.1 = (bf16[32,456,128]{2,1,0:T(8,128)(2,1)S(1)}, s32[512,1]{1,0:T(8,128)S(1)}, s32[512,1]{1,0:T(8,128)S(1)}) custom-call(s32[1,32]{1,0:T(1,128)S(1)} %bitcast.57, s32[1,128]{1,0:T(1,128)S(1)} %bitcast.58, s32[1,512]{1,0:T(1,128)S(1)} %bitcast.56, bf16[512,1024]{1,0:T(8,128)(2,1)S(1)} %reshape.87.tokens_ref), custom_call_target="tpu_custom_call" | custom-call | tf_op jit(solution)/shard_map/place_rows/pallas_call | solution.py:105
  5.5 1.8 copy-done
  7.3 11.4 %all-to-all-start = ((bf16[32,456,128]{2,1,0:T(8,128)(2,1)}), bf16[32,456,128]{2,1,0:T(8,128)(2,1)}, u32[]{:S(2)}, u32[]{:S(2)}) async-start(bf16[32,456,128]{2,1,0:T(8,128)(2,1)} %copy-done), calls=%async_computation | async-start | bytes 7471104 | tf_op jit(solution)/shard_map/all_to_all | solution.py:391
  18.8 0.0 copy-start.15
  18.8 1.6 collective-permute-start.1
  20.3 1.7 collective-permute-start.2
  22.1 0.7 collective-permute-start
  22.8 1.3 reshape.93.queries_ref
  24.1 0.1 lt.60
  24.2 0.1 lt.61
  24.3 0.1 lt.62
  24.4 0.1 lt.58
  24.5 4.0 %copy.24 = bf16[1024,1024]{0,1:T(8,128)(2,1)} copy(bf16[1024,1024]{1,0:T(8,128)(2,1)} %bitcast.59) | data formatting | bytes 4194304 | tf_op jit(solution)/shard_map/reshape | solution.py:397
  28.5 0.0 copy-start.8
  28.5 1.4 copy-done.8
  29.9 1.4 copy-done.9
  31.3 6.0 %cached_attention.1 = (f32[16,256,128]{2,1,0:T(8,128)S(1)}, f32[16,256,128]{2,1,0:T(8,128)S(1)}) custom-call(f32[16,1,384]{2,1,0:T(1,128)S(1)} %compare_select_fusion.bias_ref, bf16[512,1024]{1,0:T(8,128)(2,1)S(1)} %reshape.93.queries_ref, bf16[128,48,128]{2,1,0:T(8,128)(2,1)S(1)} %copy-done.8, bf16[128,48,128]{2,1,0:T(8,128)(2,1)S(1)} %copy-done.9), custom_call_target="tpu_custom_call" | custom-call | flops 2147483648 | bytes 8388608 | tf_op jit(solution)/shard_map/cached_attention/pallas_call | solution.py:243
  37.3 0.0 copy-done.10
  37.3 0.0 copy-start.1
  37.3 3.7 %constant_dynamic-slice_fusion.2 = (bf16[1024,2,128]{2,1,0:T(2,128)(2,1)}, bf16[1024,2,128]{2,1,0:T(2,128)(2,1)S(1)}, bf16[1024,2,128]{2,1,0:T(2,128)(2,1)S(1)},...) fusion(bf16[8192,2,128]{2,1,0:T(2,128)(2,1)S(1)} %copy-done.10,, ...), kind=kLoop, calls=%fused_computation.35 | loop fusion | bytes 8388640 | tf_op jit(solution)/shard_map/dynamic_slice | solution.py:353
  41.1 0.4 fusion.24
  41.5 3.8 %collective-permute-done.1 = bf16[512,1024]{1,0:T(8,128)(2,1)} collective-permute-done((bf16[512,1024]{1,0:T(8,128)(2,1)S(1)}, bf16[512,1024]{1,0:T(8,128)(2,1)}, u32[]{:S(2)}, u32[]{:S(2)}) %collective-permute-start.1) | collective-permute-done | bytes 1048608 | tf_op jit(solution)/shard_map/ppermute | solution.py:342
  45.4 1.1 slice.8
  46.5 0.4 collective-permute-start.3
  46.8 0.0 collective-permute-done.2
  46.8 1.1 slice.9
  47.9 3.2 %collective-permute-start.4 = (bf16[256,1024]{1,0:T(8,128)(2,1)S(1)}, bf16[256,1024]{1,0:T(8,128)(2,1)S(1)}, u32[]{:S(2)}, u32[]{:S(2)}) collective-permute-start(bf16[256,1024]{1,0:T(8,128)(2,1)S(1)} %slice.9), channel_id=1, source_target_pairs={{0,6},{1,7},{2,0},{3,1},{4,2},{5,3},{6,4},{7,5},{8,14},{9,15},{10,... | collective-permute-start | bytes 1572872 | tf_op jit(solution)/shard_map/ppermute | solution.py:342
  51.1 1.7 fusion.17
  52.8 16.3 %collective-permute-done = bf16[512,1024]{1,0:T(8,128)(2,1)} collective-permute-done((bf16[512,1024]{1,0:T(8,128)(2,1)S(1)}, bf16[512,1024]{1,0:T(8,128)(2,1)}, u32[]{:S(2)}, u32[]{:S(2)}) %collective-permute-start) | collective-permute-done | bytes 1048608 | tf_op jit(solution)/shard_map/ppermute | solution.py:342
  69.1 1.7 convolution_add_fusion.2
  70.8 0.0 collective-permute-done.3
  70.9 0.0 collective-permute-done.4
  70.9 0.0 copy-start.14
  70.9 0.5 fusion.14
  71.4 0.5 copy-done.14
  71.9 2.5 %fusion.5 = f32[512,256]{1,0:T(8,128)} fusion(f32[512,256]{1,0:T(8,128)S(1)} %fusion.14, f32[256,512]{0,1:T(8,128)S(1)} %fusion.17, f32[256,512]{0,1:T(8,128)S(1)} %convolution_add_fusion.2, bf16[512,1024]{1,0:T(8,128)(2,1)} %collective-permute-done.1, bf16[128,8,2,128]{3,2,1,0:T(2,128)(2,1)S(1)} %bitcast.62), kind=kOutput, calls=%fused_computation.8 | convolution fusion | flops 268828672 | bytes 3670016 | tf_op jit(solution)/shard_map/dot_general | solution.py:354
  74.4 29.9 %all-to-all-done.rows_ref = bf16[32,456,128]{2,1,0:T(8,128)(2,1)} async-done(((bf16[32,456,128]{2,1,0:T(8,128)(2,1)}), bf16[32,456,128]{2,1,0:T(8,128)(2,1)}, u32[]{:S(2)}, u32[]{:S(2)}) %all-to-all-start) | async-done | bytes 3735584 | tf_op jit(solution)/shard_map/all_to_all | solution.py:391
  104.3 9.8 %rank_products.1 = bf16[32,192,128]{2,1,0:T(8,128)(2,1)} custom-call(bf16[32,456,128]{2,1,0:T(8,128)(2,1)} %all-to-all-done.rows_ref, bf16[1024,1024]{1,0:T(8,128)(2,1)} %bitcast.60, bf16[1024,128]{1,0:T(8,128)(2,1)} %bitcast.69), custom_call_target="tpu_custom_call" | custom-call | flops 4294967296 | bytes 8388608 | tf_op jit(solution)/shard_map/rank_products/pallas_call | solution.py:172
  114.0 7.9 %all-to-all-start.1 = ((bf16[32,192,128]{2,1,0:T(8,128)(2,1)}), bf16[32,192,128]{2,1,0:T(8,128)(2,1)S(1)}, u32[]{:S(2)}, u32[]{:S(2)}) async-start(bf16[32,192,128]{2,1,0:T(8,128)(2,1)} %rank_products.1), calls=%async_computation.1 | async-start | bytes 3145728 | tf_op jit(solution)/shard_map/all_to_all | solution.py:405
  121.9 2.8 %collective-permute-start.10 = (bf16[512,1024]{1,0:T(8,128)(2,1)}, bf16[512,1024]{1,0:T(8,128)(2,1)S(1)}, u32[]{:S(2)}, u32[]{:S(2)}) collective-permute-start(bf16[512,1024]{1,0:T(8,128)(2,1)} %collective-permute-done), channel_id=1, source_target_pairs={{0,6},{1,7},{2,0},{3,1},{4,2},{5,3},{6,4},{7,5},{8,14},{9,15},{10,... | collective-permute-start | bytes 3145736 | tf_op jit(solution)/shard_map/ppermute | solution.py:342
  124.8 0.7 collective-permute-start.11
  125.5 0.0 collective-permute-start.9
  125.5 22.4 %collective-permute-done.10 = bf16[512,1024]{1,0:T(8,128)(2,1)S(1)} collective-permute-done((bf16[512,1024]{1,0:T(8,128)(2,1)}, bf16[512,1024]{1,0:T(8,128)(2,1)S(1)}, u32[]{:S(2)}, u32[]{:S(2)}) %collective-permute-start.10) | collective-permute-done | bytes 1048608 | tf_op jit(solution)/shard_map/ppermute | solution.py:342
  147.8 2.3 %fusion.9 = f32[256,512]{0,1:T(8,128)} fusion(bf16[512,1024]{1,0:T(8,128)(2,1)S(1)} %collective-permute-done.10, bf16[128,8,2,128]{3,2,1,0:T(2,128)(2,1)} %bitcast.65), kind=kOutput, calls=%fused_computation.12 | convolution fusion | flops 268435456 | bytes 2097152 | tf_op jit(solution)/shard_map/dot_general | solution.py:354
  150.1 13.7 %all-to-all-done.1.returned_ref.first_ref.second_ref = bf16[32,192,128]{2,1,0:T(8,128)(2,1)S(1)} async-done(((bf16[32,192,128]{2,1,0:T(8,128)(2,1)}), bf16[32,192,128]{2,1,0:T(8,128)(2,1)S(1)}, u32[]{:S(2)}, u32[]{:S(2)}) %all-to-all-start.1) | async-done | bytes 1572896 | tf_op jit(solution)/shard_map/all_to_all | solution.py:405
  163.8 0.9 collect.1
  164.7 0.8 collective-permute-start.5
  165.5 0.0 collective-permute-done.11
  165.5 1.9 %fusion.6 = f32[512,256]{1,0:T(8,128)S(1)} fusion(bf16[512,1024]{1,0:T(8,128)(2,1)} %collective-permute-done.11, bf16[128,8,2,128]{3,2,1,0:T(2,128)(2,1)} %bitcast.64), kind=kOutput, calls=%fused_computation.9 | convolution fusion | flops 268435456 | bytes 2097152 | tf_op jit(solution)/shard_map/dot_general | solution.py:354
  167.5 2.3 %collective-permute-done.5 = f32[256,128]{1,0:T(8,128)S(1)} collective-permute-done((f32[256,128]{1,0:T(8,128)S(1)}, f32[256,128]{1,0:T(8,128)S(1)}, u32[]{:S(2)}, u32[]{:S(2)}) %collective-permute-start.5) | collective-permute-done | bytes 131104 | tf_op jit(solution)/shard_map/ppermute | solution.py:342
  169.8 3.1 %collective-permute-start.6 = (f32[256,128]{1,0:T(8,128)S(1)}, f32[256,128]{1,0:T(8,128)S(1)}, u32[]{:S(2)}, u32[]{:S(2)}) collective-permute-start(f32[256,128]{1,0:T(8,128)S(1)} %add.69.a_ref), channel_id=1, source_target_pairs={{0,4},{1,5},{2,6},{3,7},{4,0},{5,1},{6,2},{7,3},{8,12},{9,13},{10,... | collective-permute-start | bytes 393224 | tf_op jit(solution)/shard_map/ppermute | solution.py:342
  172.9 0.6 collective-permute-start.7
  173.5 2.7 %collective-permute-start.8 = (f32[256,128]{1,0:T(8,128)S(1)}, f32[256,128]{1,0:T(8,128)S(1)}, u32[]{:S(2)}, u32[]{:S(2)}) collective-permute-start(f32[256,128]{1,0:T(8,128)S(1)} %add.69.a_ref), channel_id=1, source_target_pairs={{0,6},{1,7},{2,0},{3,1},{4,2},{5,3},{6,4},{7,5},{8,14},{9,15},{10,... | collective-permute-start | bytes 393224 | tf_op jit(solution)/shard_map/ppermute | solution.py:342
  176.2 0.0 collective-permute-done.9
  176.2 1.7 fusion.4.base_ref
  177.9 0.0 collective-permute-done.6.b_ref
  177.9 1.2 collective-permute-done.7.c_ref
  179.1 0.0 collective-permute-done.8.d_ref
  179.1 6.2 %finish.1 = (bf16[512,256]{1,0:T(8,128)(2,1)S(1)}, bf16[128,4,1024]{2,1,0:T(4,128)(2,1)}) custom-call(s32[512,1]{1,0:T(8,128)S(1)} %get-tuple-element.14.fetch_ref, f32[256,128]{1,0:T(8,128)S(1)} %add.69.a_ref, f32[256,128]{1,0:T(8,128)S(1)} %collective-permute-done.6.b_ref, f32[256,128]{1,0:T(8,128)S(1)} %collective-permute-done.7.c_ref, ...), custom_call_target="tpu_custom_call" | custom-call | tf_op jit(solution)/shard_map/finish/pallas_call | solution.py:321
  185.3 0.8 reshape.99
  (25 shorter events, 0.2 us)
Async XLA Ops:
  0.6 1.4 copy-start.6
  0.6 1.4 copy-start.7
  0.7 1.4 copy-start.5
  5.5 1.8 copy-start
  7.3 96.9 %all-to-all-start = ((bf16[32,456,128]{2,1,0:T(8,128)(2,1)}), bf16[32,456,128]{2,1,0:T(8,128)(2,1)}, u32[]{:S(2)}, u32[]{:S(2)}) async-start(bf16[32,456,128]{2,1,0:T(8,128)(2,1)} %copy-done), calls=%async_computation | async-start | bytes 7471104 | tf_op jit(solution)/shard_map/all_to_all | solution.py:391
  18.8 5.3 %copy-start.15 = (s32[128]{0:T(128)S(1)}, s32[128]{0:T(128)}, u32[]{:S(2)}) copy-start(s32[128]{0:T(128)} %param.15) | copy-start | bytes 1540
  18.8 26.6 %collective-permute-start.1 = (bf16[512,1024]{1,0:T(8,128)(2,1)S(1)}, bf16[512,1024]{1,0:T(8,128)(2,1)}, u32[]{:S(2)}, u32[]{:S(2)}) collective-permute-start(bf16[512,1024]{1,0:T(8,128)(2,1)S(1)} %reshape.87.tokens_ref), channel_id=1, source_target_pairs={{0,2},{1,3},{2,4},{3,5},{4,6},{5,7},{6,0},{7,1},{8,10},{9,11},{10,... | collective-permute-start | bytes 3145736 | tf_op jit(solution)/shard_map/ppermute | solution.py:342
  20.3 26.5 %collective-permute-start.2 = (bf16[512,1024]{1,0:T(8,128)(2,1)S(1)}, bf16[512,1024]{1,0:T(8,128)(2,1)}, u32[]{:S(2)}, u32[]{:S(2)}) collective-permute-start(bf16[512,1024]{1,0:T(8,128)(2,1)S(1)} %reshape.87.tokens_ref), channel_id=1, source_target_pairs={{0,6},{1,7},{2,0},{3,1},{4,2},{5,3},{6,4},{7,5},{8,14},{9,15},{10,... | collective-permute-start | bytes 3145736 | tf_op jit(solution)/shard_map/ppermute | solution.py:342
  22.1 47.0 %collective-permute-start = (bf16[512,1024]{1,0:T(8,128)(2,1)S(1)}, bf16[512,1024]{1,0:T(8,128)(2,1)}, u32[]{:S(2)}, u32[]{:S(2)}) collective-permute-start(bf16[512,1024]{1,0:T(8,128)(2,1)S(1)} %reshape.87.tokens_ref), channel_id=1, source_target_pairs={{0,1},{1,0},{2,3},{3,2},{4,5},{5,4},{6,7},{7,6},{8,9},{9,8},{10,11... | collective-permute-start | bytes 3145736 | tf_op jit(solution)/shard_map/ppermute | solution.py:342
  28.5 1.4 copy-start.8
  29.9 1.4 copy-start.9
  31.3 6.0 %copy-start.10 = (bf16[8192,2,128]{2,1,0:T(2,128)(2,1)S(1)}, bf16[8192,2,128]{2,1,0:T(2,128)(2,1)}, u32[]{:S(2)}) copy-start(bf16[8192,2,128]{2,1,0:T(2,128)(2,1)} %param.19) | copy-start | bytes 12582916
  37.3 3.8 %copy-start.1 = (f32[16,256,128]{2,1,0:T(8,128)}, f32[16,256,128]{2,1,0:T(8,128)S(1)}, u32[]{:S(2)}) copy-start(f32[16,256,128]{2,1,0:T(8,128)S(1)} %get-tuple-element.22.mixed_ref) | copy-start | bytes 6291460
  37.3 3.8 %copy-start.3 = (f32[16,256,128]{2,1,0:T(8,128)}, f32[16,256,128]{2,1,0:T(8,128)S(1)}, u32[]{:S(2)}) copy-start(f32[16,256,128]{2,1,0:T(8,128)S(1)} %get-tuple-element.23.weight_ref) | copy-start | bytes 6291460
  46.5 24.4 %collective-permute-start.3 = (bf16[256,1024]{1,0:T(8,128)(2,1)S(1)}, bf16[256,1024]{1,0:T(8,128)(2,1)S(1)}, u32[]{:S(2)}, u32[]{:S(2)}) collective-permute-start(bf16[256,1024]{1,0:T(8,128)(2,1)S(1)} %slice.8), channel_id=1, source_target_pairs={{0,2},{1,3},{2,4},{3,5},{4,6},{5,7},{6,0},{7,1},{8,10},{9,11},{10,... | collective-permute-start | bytes 1572872 | tf_op jit(solution)/shard_map/ppermute | solution.py:342
  47.9 23.0 %collective-permute-start.4 = (bf16[256,1024]{1,0:T(8,128)(2,1)S(1)}, bf16[256,1024]{1,0:T(8,128)(2,1)S(1)}, u32[]{:S(2)}, u32[]{:S(2)}) collective-permute-start(bf16[256,1024]{1,0:T(8,128)(2,1)S(1)} %slice.9), channel_id=1, source_target_pairs={{0,6},{1,7},{2,0},{3,1},{4,2},{5,3},{6,4},{7,5},{8,14},{9,15},{10,... | collective-permute-start | bytes 1572872 | tf_op jit(solution)/shard_map/ppermute | solution.py:342
  70.9 1.0 copy-start.14
  114.0 49.7 %all-to-all-start.1 = ((bf16[32,192,128]{2,1,0:T(8,128)(2,1)}), bf16[32,192,128]{2,1,0:T(8,128)(2,1)S(1)}, u32[]{:S(2)}, u32[]{:S(2)}) async-start(bf16[32,192,128]{2,1,0:T(8,128)(2,1)} %rank_products.1), calls=%async_computation.1 | async-start | bytes 3145728 | tf_op jit(solution)/shard_map/all_to_all | solution.py:405
  121.9 25.9 %collective-permute-start.10 = (bf16[512,1024]{1,0:T(8,128)(2,1)}, bf16[512,1024]{1,0:T(8,128)(2,1)S(1)}, u32[]{:S(2)}, u32[]{:S(2)}) collective-permute-start(bf16[512,1024]{1,0:T(8,128)(2,1)} %collective-permute-done), channel_id=1, source_target_pairs={{0,6},{1,7},{2,0},{3,1},{4,2},{5,3},{6,4},{7,5},{8,14},{9,15},{10,... | collective-permute-start | bytes 3145736 | tf_op jit(solution)/shard_map/ppermute | solution.py:342
  124.8 40.7 %collective-permute-start.11 = (bf16[512,1024]{1,0:T(8,128)(2,1)}, bf16[512,1024]{1,0:T(8,128)(2,1)}, u32[]{:S(2)}, u32[]{:S(2)}) collective-permute-start(bf16[512,1024]{1,0:T(8,128)(2,1)} %copy-done.14), channel_id=1, source_target_pairs={{0,1},{1,0},{2,3},{3,2},{4,5},{5,4},{6,7},{7,6},{8,9},{9,8},{10,11... | collective-permute-start | bytes 3145736 | tf_op jit(solution)/shard_map/ppermute | solution.py:342
  125.5 50.7 %collective-permute-start.9 = (bf16[512,1024]{1,0:T(8,128)(2,1)}, bf16[512,1024]{1,0:T(8,128)(2,1)}, u32[]{:S(2)}, u32[]{:S(2)}) collective-permute-start(bf16[512,1024]{1,0:T(8,128)(2,1)} %collective-permute-done), channel_id=1, source_target_pairs={{0,2},{1,3},{2,4},{3,5},{4,6},{5,7},{6,0},{7,1},{8,10},{9,11},{10,... | collective-permute-start | bytes 3145736 | tf_op jit(solution)/shard_map/ppermute | solution.py:342
  163.8 12.4 %copy-start.11 = (f32[512,256]{1,0:T(8,128)S(1)}, f32[512,256]{1,0:T(8,128)}, u32[]{:S(2)}) copy-start(f32[512,256]{1,0:T(8,128)} %fusion.5) | copy-start | bytes 1572868
  163.8 12.4 %copy-start.12 = (bf16[1024,2,128]{2,1,0:T(2,128)(2,1)S(1)}, bf16[1024,2,128]{2,1,0:T(2,128)(2,1)}, u32[]{:S(2)}) copy-start(bf16[1024,2,128]{2,1,0:T(2,128)(2,1)} %get-tuple-element.26) | copy-start | bytes 1572868
  163.8 12.4 %copy-start.13 = (f32[256,512]{0,1:T(8,128)S(1)}, f32[256,512]{0,1:T(8,128)}, u32[]{:S(2)}) copy-start(f32[256,512]{0,1:T(8,128)} %fusion.9) | copy-start | bytes 1572868
  164.7 5.1 %collective-permute-start.5 = (f32[256,128]{1,0:T(8,128)S(1)}, f32[256,128]{1,0:T(8,128)S(1)}, u32[]{:S(2)}, u32[]{:S(2)}) collective-permute-start(f32[256,128]{1,0:T(8,128)S(1)} %collect.1), channel_id=1, source_target_pairs={{0,1},{1,0},{2,3},{3,2},{4,5},{5,4},{6,7},{7,6},{8,9},{9,8},{10,11... | collective-permute-start | bytes 393224 | tf_op jit(solution)/shard_map/ppermute | solution.py:342
  165.5 13.6 %copy-start.4 = (f32[16,256,128]{2,1,0:T(8,128)S(1)}, f32[16,256,128]{2,1,0:T(8,128)}, u32[]{:S(2)}) copy-start(f32[16,256,128]{2,1,0:T(8,128)} %copy-done.3) | copy-start | bytes 6291460
  167.4 11.7 %copy-start.2 = (f32[16,256,128]{2,1,0:T(8,128)S(1)}, f32[16,256,128]{2,1,0:T(8,128)}, u32[]{:S(2)}) copy-start(f32[16,256,128]{2,1,0:T(8,128)} %copy-done.1) | copy-start | bytes 6291460
  169.8 8.1 %collective-permute-start.6 = (f32[256,128]{1,0:T(8,128)S(1)}, f32[256,128]{1,0:T(8,128)S(1)}, u32[]{:S(2)}, u32[]{:S(2)}) collective-permute-start(f32[256,128]{1,0:T(8,128)S(1)} %add.69.a_ref), channel_id=1, source_target_pairs={{0,4},{1,5},{2,6},{3,7},{4,0},{5,1},{6,2},{7,3},{8,12},{9,13},{10,... | collective-permute-start | bytes 393224 | tf_op jit(solution)/shard_map/ppermute | solution.py:342
  172.9 6.2 %collective-permute-start.7 = (f32[256,128]{1,0:T(8,128)S(1)}, f32[256,128]{1,0:T(8,128)S(1)}, u32[]{:S(2)}, u32[]{:S(2)}) collective-permute-start(f32[256,128]{1,0:T(8,128)S(1)} %add.69.a_ref), channel_id=1, source_target_pairs={{0,2},{1,3},{2,4},{3,5},{4,6},{5,7},{6,0},{7,1},{8,10},{9,11},{10,... | collective-permute-start | bytes 393224 | tf_op jit(solution)/shard_map/ppermute | solution.py:342
  173.5 5.6 %collective-permute-start.8 = (f32[256,128]{1,0:T(8,128)S(1)}, f32[256,128]{1,0:T(8,128)S(1)}, u32[]{:S(2)}, u32[]{:S(2)}) collective-permute-start(f32[256,128]{1,0:T(8,128)S(1)} %add.69.a_ref), channel_id=1, source_target_pairs={{0,6},{1,7},{2,0},{3,1},{4,2},{5,3},{6,4},{7,5},{8,14},{9,15},{10,... | collective-permute-start | bytes 393224 | tf_op jit(solution)/shard_map/ppermute | solution.py:342

commit v6 on v5

--- a/solution.py
+++ b/solution.py
@@ -12,7 +12,6 @@
 PAIR = 2
 PAIR_ROWS = PAIR * BLK
 ASK_ROWS = 8
-RETURN_ROWS = 64
 LANES = 128
 GROUP = 8
 
@@ -83,7 +82,7 @@
         t = iota((token_count, blocks), 0)
         member = (first * steps <= t) & (t < after * steps)
         column_ref[...] = t[:, :1] + total(
-            jnp.where(member, owner * RETURN_ROWS + (offset - first) * steps, 0), 1
+            jnp.where(member, (owner * PAIR_ROWS + offset - first) * steps, 0), 1
         )
         fetch_ref[...] = total(jnp.where(member, owner * PAIR + turn, 0), 1)
 
@@ -100,7 +99,7 @@
 def place(first, request, owners, tokens, steps, replicas):
     token_count, depth = tokens.shape
     rows = PAIR_ROWS * steps * depth // LANES + ASK_ROWS
-    here = 8
+    here = 16
     whole = lambda shape: pl.BlockSpec(shape, lambda i: (0, 0))
     return pl.pallas_call(
         functools.partial(place_kernel, steps),
@@ -156,9 +155,8 @@
     for k in range(here):
         out_ref[k] = jnp.concatenate(
             [
+                ups[k * PAIR * width:(k + 1) * PAIR * width],
                 both[k * each:(k + 1) * each],
-                jnp.zeros((RETURN_ROWS - each, lanes), jnp.float32),
-                ups[k * PAIR * width:(k + 1) * PAIR * width],
             ],
             axis=0,
         ).astype(jnp.bfloat16)
@@ -167,7 +165,7 @@
 def rank_products(rows, maps, ups, steps):
     replicas, count, lanes = rows.shape
     here = 8
-    out_rows = RETURN_ROWS + PAIR * lanes // 2
+    out_rows = PAIR * lanes // 2 + PAIR_ROWS * steps
     whole = lambda x: pl.BlockSpec(x.shape, lambda i: (0, 0))
     return pl.pallas_call(
         functools.partial(rank_kernel, steps),
@@ -184,21 +182,24 @@
 def collect_kernel(column_ref, returned_ref, out_ref):
     replicas, rows, lanes = returned_ref.shape
     tokens, width = column_ref.shape[0], lanes // 2
+    rows -= PAIR * width
+    got = returned_ref[...].astype(jnp.float32)[:, PAIR * width:]
+    got = got.reshape(replicas * rows, lanes).astype(jnp.bfloat16)
     pick = jnp.where(iota((tokens, replicas * rows), 1) == column_ref[...], 1.0, 0.0).astype(jnp.bfloat16)
-    both = jnp.dot(pick, returned_ref[...].reshape(replicas * rows, lanes), preferred_element_type=jnp.float32)
+    both = jnp.dot(pick, got, preferred_element_type=jnp.float32)
     value = both[:, :width] + both[:, width:]
     out_ref[...] = jnp.concatenate([value[: tokens // 2], value[tokens // 2:]], axis=1)
 
 
 def collect(column, returned):
     tokens = column.shape[0]
-    replicas, _, lanes = returned.shape
+    lanes = returned.shape[2]
     return pl.pallas_call(
         collect_kernel,
         grid=(1,),
         in_specs=[
             pl.BlockSpec((tokens, 1), lambda i: (0, 0)),
-            pl.BlockSpec((replicas, RETURN_ROWS, lanes), lambda i: (0, 0, 0)),
+            pl.BlockSpec(returned.shape, lambda i: (0, 0, 0)),
         ],
         out_specs=pl.BlockSpec((tokens // 2, lanes), lambda i: (0, 0)),
         out_shape=jax.ShapeDtypeStruct((tokens // 2, lanes), jnp.float32),
@@ -321,7 +322,7 @@
     return pl.pallas_call(
         functools.partial(finish_kernel, steps, rank),
         grid=(groups // per,),
-        in_specs=[whole(fetch)] + [whole(p) for p in parts] + [ups(1), ups(2), whole(base), block]
+        in_specs=[whole(fetch)] + [whole(p) for p in parts] + [ups(0), ups(1), whole(base), block]
         + [pl.BlockSpec((per, rows, HD), lambda i: (i, 0, 0))] * 2,
         out_specs=[
             pl.BlockSpec(base.shape, lambda i: (0, 0)),

time: 187 us -> 185 us (0.989)
  no operation moved by 1% of the time
where the time goes in v6:
time: 185 us; the launch traced here: 184 us
  waiting for transfers between devices  88.2 us (48%)
  starting transfers between devices  37.5 us (20%)
  Pallas kernels  25.9 us (14%)
  local copies, waits for them, and re-layouts  18.9 us (10%)
  matrix products  12.6 us (7%)
    ppermute x12, waiting for transfers between devices, shifted(): return lax.ppermute(value, 'tensor', pairs)  46.1 us
    all_to_all x1, waiting for transfers between devices, per_device(): lax.all_to_all(sent, 'replica', split_axis=0, concat_axis=0, tiled=True)  29.9 us
    ppermute x12, starting transfers between devices, shifted(): return lax.ppermute(value, 'tensor', pairs)  18.2 us
    dot_general x8, matrix products, product(): jnp.dot(piece, part.reshape(depth, -1), preferred_element_type=jnp.float32)  12.6 us
    all_to_all x1, waiting for transfers between devices, per_device(): lax.all_to_all(products, 'replica', split_axis=0, concat_axis=0, tiled=True)  12.2 us
    all_to_all x1, starting transfers between devices, per_device(): lax.all_to_all(sent, 'replica', split_axis=0, concat_axis=0, tiled=True)  11.4 us
    pallas_call x1, Pallas kernels, rank_products(): pl.pallas_call(functools.partial(rank_kernel, steps), grid=(replicas // h...  9.77 us
    all_to_all x1, starting transfers between devices, per_device(): lax.all_to_all(products, 'replica', split_axis=0, concat_axis=0, tiled=True)  7.9 us
  transfers between devices with their start and end apart: 14, of which 7 were waited for; matrix products, arithmetic and copies ran while one was open for 13% of the time, Pallas kernels for 4%

profile of v6, /device:TPU:32, one launch (start us, length us, event | category | flops | bytes accessed | tf_op | source)
XLA Modules:
  0.0 184.2 jit_solution(16867811789054259767)
XLA Ops:
  0.7 1.4 reshape.87.tokens_ref
  2.1 3.1 %place_rows.1 = (bf16[32,456,128]{2,1,0:T(8,128)(2,1)S(1)}, s32[512,1]{1,0:T(8,128)S(1)}, s32[512,1]{1,0:T(8,128)S(1)}) custom-call(s32[1,32]{1,0:T(1,128)S(1)} %bitcast.57, s32[1,128]{1,0:T(1,128)S(1)} %bitcast.58, s32[1,512]{1,0:T(1,128)S(1)} %bitcast.56, bf16[512,1024]{1,0:T(8,128)(2,1)S(1)} %reshape.87.tokens_ref), custom_call_target="tpu_custom_call" | custom-call | tf_op jit(solution)/shard_map/place_rows/pallas_call | solution.py:104
  5.1 0.0 copy-start
  5.2 1.8 copy-done
  7.0 11.4 %all-to-all-start = ((bf16[32,456,128]{2,1,0:T(8,128)(2,1)}), bf16[32,456,128]{2,1,0:T(8,128)(2,1)}, u32[]{:S(2)}, u32[]{:S(2)}) async-start(bf16[32,456,128]{2,1,0:T(8,128)(2,1)} %copy-done), calls=%async_computation | async-start | bytes 7471104 | tf_op jit(solution)/shard_map/all_to_all | solution.py:392
  18.4 0.0 copy-start.15
  18.4 1.6 collective-permute-start.1
  20.0 1.7 collective-permute-start.2
  21.7 0.7 collective-permute-start
  22.4 1.3 reshape.93.queries_ref
  23.7 0.1 lt.60
  23.8 0.1 lt.61
  23.9 0.1 lt.62
  24.0 0.1 lt.58
  24.1 4.0 %copy.24 = bf16[1024,1024]{0,1:T(8,128)(2,1)} copy(bf16[1024,1024]{1,0:T(8,128)(2,1)} %bitcast.59) | data formatting | bytes 4194304 | tf_op jit(solution)/shard_map/reshape | solution.py:398
  28.1 0.0 copy-start.8
  28.1 1.4 copy-done.8
  29.5 1.4 copy-done.9
  30.9 6.0 %cached_attention.1 = (f32[16,256,128]{2,1,0:T(8,128)S(1)}, f32[16,256,128]{2,1,0:T(8,128)S(1)}) custom-call(f32[16,1,384]{2,1,0:T(1,128)S(1)} %compare_select_fusion.bias_ref, bf16[512,1024]{1,0:T(8,128)(2,1)S(1)} %reshape.93.queries_ref, bf16[128,48,128]{2,1,0:T(8,128)(2,1)S(1)} %copy-done.8, bf16[128,48,128]{2,1,0:T(8,128)(2,1)S(1)} %copy-done.9), custom_call_target="tpu_custom_call" | custom-call | flops 2147483648 | bytes 8388608 | tf_op jit(solution)/shard_map/cached_attention/pallas_call | solution.py:244
  36.9 0.0 copy-done.10
  36.9 0.0 copy-start.1
  37.0 0.0 copy-start.3
  37.0 3.7 %constant_dynamic-slice_fusion.2 = (bf16[1024,2,128]{2,1,0:T(2,128)(2,1)}, bf16[1024,2,128]{2,1,0:T(2,128)(2,1)S(1)}, bf16[1024,2,128]{2,1,0:T(2,128)(2,1)S(1)},...) fusion(bf16[8192,2,128]{2,1,0:T(2,128)(2,1)S(1)} %copy-done.10,, ...), kind=kLoop, calls=%fused_computation.35 | loop fusion | bytes 8388640 | tf_op jit(solution)/shard_map/dynamic_slice | solution.py:354
  40.7 0.0 copy-done.1
  40.7 0.4 fusion.24
  41.2 3.8 %collective-permute-done.1 = bf16[512,1024]{1,0:T(8,128)(2,1)} collective-permute-done((bf16[512,1024]{1,0:T(8,128)(2,1)S(1)}, bf16[512,1024]{1,0:T(8,128)(2,1)}, u32[]{:S(2)}, u32[]{:S(2)}) %collective-permute-start.1) | collective-permute-done | bytes 1048608 | tf_op jit(solution)/shard_map/ppermute | solution.py:343
  45.0 1.1 slice.8
  46.1 0.4 collective-permute-start.3
  46.4 0.0 collective-permute-done.2
  46.4 1.1 slice.9
  47.5 3.2 %collective-permute-start.4 = (bf16[256,1024]{1,0:T(8,128)(2,1)S(1)}, bf16[256,1024]{1,0:T(8,128)(2,1)S(1)}, u32[]{:S(2)}, u32[]{:S(2)}) collective-permute-start(bf16[256,1024]{1,0:T(8,128)(2,1)S(1)} %slice.9), channel_id=1, source_target_pairs={{0,6},{1,7},{2,0},{3,1},{4,2},{5,3},{6,4},{7,5},{8,14},{9,15},{10,... | collective-permute-start | bytes 1572872 | tf_op jit(solution)/shard_map/ppermute | solution.py:343
  50.7 1.7 fusion.17
  52.4 16.3 %collective-permute-done = bf16[512,1024]{1,0:T(8,128)(2,1)} collective-permute-done((bf16[512,1024]{1,0:T(8,128)(2,1)S(1)}, bf16[512,1024]{1,0:T(8,128)(2,1)}, u32[]{:S(2)}, u32[]{:S(2)}) %collective-permute-start) | collective-permute-done | bytes 1048608 | tf_op jit(solution)/shard_map/ppermute | solution.py:343
  68.7 1.7 convolution_add_fusion.2
  70.4 0.0 collective-permute-done.3
  70.5 0.0 collective-permute-done.4
  70.5 0.0 copy-start.14
  70.6 0.5 fusion.14
  71.0 0.5 copy-done.14
  71.5 2.5 %fusion.5 = f32[512,256]{1,0:T(8,128)} fusion(f32[512,256]{1,0:T(8,128)S(1)} %fusion.14, f32[256,512]{0,1:T(8,128)S(1)} %fusion.17, f32[256,512]{0,1:T(8,128)S(1)} %convolution_add_fusion.2, bf16[512,1024]{1,0:T(8,128)(2,1)} %collective-permute-done.1, bf16[128,8,2,128]{3,2,1,0:T(2,128)(2,1)S(1)} %bitcast.62), kind=kOutput, calls=%fused_computation.8 | convolution fusion | flops 268828672 | bytes 3670016 | tf_op jit(solution)/shard_map/dot_general | solution.py:355
  74.0 29.9 %all-to-all-done.rows_ref = bf16[32,456,128]{2,1,0:T(8,128)(2,1)} async-done(((bf16[32,456,128]{2,1,0:T(8,128)(2,1)}), bf16[32,456,128]{2,1,0:T(8,128)(2,1)}, u32[]{:S(2)}, u32[]{:S(2)}) %all-to-all-start) | async-done | bytes 3735584 | tf_op jit(solution)/shard_map/all_to_all | solution.py:392
  103.9 9.8 %rank_products.1 = bf16[32,184,128]{2,1,0:T(8,128)(2,1)} custom-call(bf16[32,456,128]{2,1,0:T(8,128)(2,1)} %all-to-all-done.rows_ref, bf16[1024,1024]{1,0:T(8,128)(2,1)} %bitcast.60, bf16[1024,128]{1,0:T(8,128)(2,1)} %bitcast.69), custom_call_target="tpu_custom_call" | custom-call | flops 4294967296 | bytes 8388608 | tf_op jit(solution)/shard_map/rank_products/pallas_call | solution.py:170
  113.6 7.9 %all-to-all-start.1 = ((bf16[32,184,128]{2,1,0:T(8,128)(2,1)}), bf16[32,184,128]{2,1,0:T(8,128)(2,1)S(1)}, u32[]{:S(2)}, u32[]{:S(2)}) async-start(bf16[32,184,128]{2,1,0:T(8,128)(2,1)} %rank_products.1), calls=%async_computation.1 | async-start | bytes 3014656 | tf_op jit(solution)/shard_map/all_to_all | solution.py:406
  121.6 2.8 %collective-permute-start.10 = (bf16[512,1024]{1,0:T(8,128)(2,1)}, bf16[512,1024]{1,0:T(8,128)(2,1)S(1)}, u32[]{:S(2)}, u32[]{:S(2)}) collective-permute-start(bf16[512,1024]{1,0:T(8,128)(2,1)} %collective-permute-done), channel_id=1, source_target_pairs={{0,6},{1,7},{2,0},{3,1},{4,2},{5,3},{6,4},{7,5},{8,14},{9,15},{10,... | collective-permute-start | bytes 3145736 | tf_op jit(solution)/shard_map/ppermute | solution.py:343
  124.4 0.7 collective-permute-start.11
  125.1 0.0 collective-permute-start.9
  125.1 22.4 %collective-permute-done.10 = bf16[512,1024]{1,0:T(8,128)(2,1)S(1)} collective-permute-done((bf16[512,1024]{1,0:T(8,128)(2,1)}, bf16[512,1024]{1,0:T(8,128)(2,1)S(1)}, u32[]{:S(2)}, u32[]{:S(2)}) %collective-permute-start.10) | collective-permute-done | bytes 1048608 | tf_op jit(solution)/shard_map/ppermute | solution.py:343
  147.4 2.3 %fusion.9 = f32[256,512]{0,1:T(8,128)} fusion(bf16[512,1024]{1,0:T(8,128)(2,1)S(1)} %collective-permute-done.10, bf16[128,8,2,128]{3,2,1,0:T(2,128)(2,1)} %bitcast.65), kind=kOutput, calls=%fused_computation.12 | convolution fusion | flops 268435456 | bytes 2097152 | tf_op jit(solution)/shard_map/dot_general | solution.py:355
  149.7 12.2 %all-to-all-done.1.returned_ref.first_ref.second_ref = bf16[32,184,128]{2,1,0:T(8,128)(2,1)S(1)} async-done(((bf16[32,184,128]{2,1,0:T(8,128)(2,1)}), bf16[32,184,128]{2,1,0:T(8,128)(2,1)S(1)}, u32[]{:S(2)}, u32[]{:S(2)}) %all-to-all-start.1) | async-done | bytes 1507360 | tf_op jit(solution)/shard_map/all_to_all | solution.py:406
  162.0 0.8 collect.1
  162.8 0.8 collective-permute-start.5
  163.6 0.0 collective-permute-done.11
  163.6 1.9 %fusion.6 = f32[512,256]{1,0:T(8,128)S(1)} fusion(bf16[512,1024]{1,0:T(8,128)(2,1)} %collective-permute-done.11, bf16[128,8,2,128]{3,2,1,0:T(2,128)(2,1)} %bitcast.64), kind=kOutput, calls=%fused_computation.9 | convolution fusion | flops 268435456 | bytes 2097152 | tf_op jit(solution)/shard_map/dot_general | solution.py:355
  165.5 2.3 %collective-permute-done.5 = f32[256,128]{1,0:T(8,128)S(1)} collective-permute-done((f32[256,128]{1,0:T(8,128)S(1)}, f32[256,128]{1,0:T(8,128)S(1)}, u32[]{:S(2)}, u32[]{:S(2)}) %collective-permute-start.5) | collective-permute-done | bytes 131104 | tf_op jit(solution)/shard_map/ppermute | solution.py:343
  167.9 3.1 %collective-permute-start.6 = (f32[256,128]{1,0:T(8,128)S(1)}, f32[256,128]{1,0:T(8,128)S(1)}, u32[]{:S(2)}, u32[]{:S(2)}) collective-permute-start(f32[256,128]{1,0:T(8,128)S(1)} %add.69.a_ref), channel_id=1, source_target_pairs={{0,4},{1,5},{2,6},{3,7},{4,0},{5,1},{6,2},{7,3},{8,12},{9,13},{10,... | collective-permute-start | bytes 393224 | tf_op jit(solution)/shard_map/ppermute | solution.py:343
  171.0 0.6 collective-permute-start.7
  171.6 2.7 %collective-permute-start.8 = (f32[256,128]{1,0:T(8,128)S(1)}, f32[256,128]{1,0:T(8,128)S(1)}, u32[]{:S(2)}, u32[]{:S(2)}) collective-permute-start(f32[256,128]{1,0:T(8,128)S(1)} %add.69.a_ref), channel_id=1, source_target_pairs={{0,6},{1,7},{2,0},{3,1},{4,2},{5,3},{6,4},{7,5},{8,14},{9,15},{10,... | collective-permute-start | bytes 393224 | tf_op jit(solution)/shard_map/ppermute | solution.py:343
  174.3 0.0 collective-permute-done.9
  174.3 1.7 fusion.4.base_ref
  176.0 0.0 collective-permute-done.6.b_ref
  176.0 1.2 collective-permute-done.7.c_ref
  177.2 0.0 collective-permute-done.8.d_ref
  177.2 6.2 %finish.1 = (bf16[512,256]{1,0:T(8,128)(2,1)S(1)}, bf16[128,4,1024]{2,1,0:T(4,128)(2,1)}) custom-call(s32[512,1]{1,0:T(8,128)S(1)} %get-tuple-element.14.fetch_ref, f32[256,128]{1,0:T(8,128)S(1)} %add.69.a_ref, f32[256,128]{1,0:T(8,128)S(1)} %collective-permute-done.6.b_ref, f32[256,128]{1,0:T(8,128)S(1)} %collective-permute-done.7.c_ref, ...), custom_call_target="tpu_custom_call" | custom-call | tf_op jit(solution)/shard_map/finish/pallas_call | solution.py:322
  183.5 0.8 reshape.99
  (25 shorter events, 0.2 us)
Async XLA Ops:
  0.6 1.4 copy-start.6
  0.6 1.4 copy-start.7
  0.7 1.4 copy-start.5
  5.1 1.8 copy-start
  7.0 96.9 %all-to-all-start = ((bf16[32,456,128]{2,1,0:T(8,128)(2,1)}), bf16[32,456,128]{2,1,0:T(8,128)(2,1)}, u32[]{:S(2)}, u32[]{:S(2)}) async-start(bf16[32,456,128]{2,1,0:T(8,128)(2,1)} %copy-done), calls=%async_computation | async-start | bytes 7471104 | tf_op jit(solution)/shard_map/all_to_all | solution.py:392
  18.4 5.3 %copy-start.15 = (s32[128]{0:T(128)S(1)}, s32[128]{0:T(128)}, u32[]{:S(2)}) copy-start(s32[128]{0:T(128)} %param.15) | copy-start | bytes 1540
  18.4 26.6 %collective-permute-start.1 = (bf16[512,1024]{1,0:T(8,128)(2,1)S(1)}, bf16[512,1024]{1,0:T(8,128)(2,1)}, u32[]{:S(2)}, u32[]{:S(2)}) collective-permute-start(bf16[512,1024]{1,0:T(8,128)(2,1)S(1)} %reshape.87.tokens_ref), channel_id=1, source_target_pairs={{0,2},{1,3},{2,4},{3,5},{4,6},{5,7},{6,0},{7,1},{8,10},{9,11},{10,... | collective-permute-start | bytes 3145736 | tf_op jit(solution)/shard_map/ppermute | solution.py:343
  20.0 26.5 %collective-permute-start.2 = (bf16[512,1024]{1,0:T(8,128)(2,1)S(1)}, bf16[512,1024]{1,0:T(8,128)(2,1)}, u32[]{:S(2)}, u32[]{:S(2)}) collective-permute-start(bf16[512,1024]{1,0:T(8,128)(2,1)S(1)} %reshape.87.tokens_ref), channel_id=1, source_target_pairs={{0,6},{1,7},{2,0},{3,1},{4,2},{5,3},{6,4},{7,5},{8,14},{9,15},{10,... | collective-permute-start | bytes 3145736 | tf_op jit(solution)/shard_map/ppermute | solution.py:343
  21.7 47.0 %collective-permute-start = (bf16[512,1024]{1,0:T(8,128)(2,1)S(1)}, bf16[512,1024]{1,0:T(8,128)(2,1)}, u32[]{:S(2)}, u32[]{:S(2)}) collective-permute-start(bf16[512,1024]{1,0:T(8,128)(2,1)S(1)} %reshape.87.tokens_ref), channel_id=1, source_target_pairs={{0,1},{1,0},{2,3},{3,2},{4,5},{5,4},{6,7},{7,6},{8,9},{9,8},{10,11... | collective-permute-start | bytes 3145736 | tf_op jit(solution)/shard_map/ppermute | solution.py:343
  28.1 1.4 copy-start.8
  29.5 1.4 copy-start.9
  30.9 6.0 %copy-start.10 = (bf16[8192,2,128]{2,1,0:T(2,128)(2,1)S(1)}, bf16[8192,2,128]{2,1,0:T(2,128)(2,1)}, u32[]{:S(2)}) copy-start(bf16[8192,2,128]{2,1,0:T(2,128)(2,1)} %param.19) | copy-start | bytes 12582916
  36.9 3.8 %copy-start.1 = (f32[16,256,128]{2,1,0:T(8,128)}, f32[16,256,128]{2,1,0:T(8,128)S(1)}, u32[]{:S(2)}) copy-start(f32[16,256,128]{2,1,0:T(8,128)S(1)} %get-tuple-element.22.mixed_ref) | copy-start | bytes 6291460
  37.0 3.8 %copy-start.3 = (f32[16,256,128]{2,1,0:T(8,128)}, f32[16,256,128]{2,1,0:T(8,128)S(1)}, u32[]{:S(2)}) copy-start(f32[16,256,128]{2,1,0:T(8,128)S(1)} %get-tuple-element.23.weight_ref) | copy-start | bytes 6291460
  46.1 24.3 %collective-permute-start.3 = (bf16[256,1024]{1,0:T(8,128)(2,1)S(1)}, bf16[256,1024]{1,0:T(8,128)(2,1)S(1)}, u32[]{:S(2)}, u32[]{:S(2)}) collective-permute-start(bf16[256,1024]{1,0:T(8,128)(2,1)S(1)} %slice.8), channel_id=1, source_target_pairs={{0,2},{1,3},{2,4},{3,5},{4,6},{5,7},{6,0},{7,1},{8,10},{9,11},{10,... | collective-permute-start | bytes 1572872 | tf_op jit(solution)/shard_map/ppermute | solution.py:343
  47.5 23.0 %collective-permute-start.4 = (bf16[256,1024]{1,0:T(8,128)(2,1)S(1)}, bf16[256,1024]{1,0:T(8,128)(2,1)S(1)}, u32[]{:S(2)}, u32[]{:S(2)}) collective-permute-start(bf16[256,1024]{1,0:T(8,128)(2,1)S(1)} %slice.9), channel_id=1, source_target_pairs={{0,6},{1,7},{2,0},{3,1},{4,2},{5,3},{6,4},{7,5},{8,14},{9,15},{10,... | collective-permute-start | bytes 1572872 | tf_op jit(solution)/shard_map/ppermute | solution.py:343
  70.5 1.0 copy-start.14
  113.6 48.3 %all-to-all-start.1 = ((bf16[32,184,128]{2,1,0:T(8,128)(2,1)}), bf16[32,184,128]{2,1,0:T(8,128)(2,1)S(1)}, u32[]{:S(2)}, u32[]{:S(2)}) async-start(bf16[32,184,128]{2,1,0:T(8,128)(2,1)} %rank_products.1), calls=%async_computation.1 | async-start | bytes 3014656 | tf_op jit(solution)/shard_map/all_to_all | solution.py:406
  121.6 25.9 %collective-permute-start.10 = (bf16[512,1024]{1,0:T(8,128)(2,1)}, bf16[512,1024]{1,0:T(8,128)(2,1)S(1)}, u32[]{:S(2)}, u32[]{:S(2)}) collective-permute-start(bf16[512,1024]{1,0:T(8,128)(2,1)} %collective-permute-done), channel_id=1, source_target_pairs={{0,6},{1,7},{2,0},{3,1},{4,2},{5,3},{6,4},{7,5},{8,14},{9,15},{10,... | collective-permute-start | bytes 3145736 | tf_op jit(solution)/shard_map/ppermute | solution.py:343
  124.4 39.2 %collective-permute-start.11 = (bf16[512,1024]{1,0:T(8,128)(2,1)}, bf16[512,1024]{1,0:T(8,128)(2,1)}, u32[]{:S(2)}, u32[]{:S(2)}) collective-permute-start(bf16[512,1024]{1,0:T(8,128)(2,1)} %copy-done.14), channel_id=1, source_target_pairs={{0,1},{1,0},{2,3},{3,2},{4,5},{5,4},{6,7},{7,6},{8,9},{9,8},{10,11... | collective-permute-start | bytes 3145736 | tf_op jit(solution)/shard_map/ppermute | solution.py:343
  125.1 49.2 %collective-permute-start.9 = (bf16[512,1024]{1,0:T(8,128)(2,1)}, bf16[512,1024]{1,0:T(8,128)(2,1)}, u32[]{:S(2)}, u32[]{:S(2)}) collective-permute-start(bf16[512,1024]{1,0:T(8,128)(2,1)} %collective-permute-done), channel_id=1, source_target_pairs={{0,2},{1,3},{2,4},{3,5},{4,6},{5,7},{6,0},{7,1},{8,10},{9,11},{10,... | collective-permute-start | bytes 3145736 | tf_op jit(solution)/shard_map/ppermute | solution.py:343
  162.0 12.3 %copy-start.11 = (f32[512,256]{1,0:T(8,128)S(1)}, f32[512,256]{1,0:T(8,128)}, u32[]{:S(2)}) copy-start(f32[512,256]{1,0:T(8,128)} %fusion.5) | copy-start | bytes 1572868
  162.0 12.3 %copy-start.12 = (bf16[1024,2,128]{2,1,0:T(2,128)(2,1)S(1)}, bf16[1024,2,128]{2,1,0:T(2,128)(2,1)}, u32[]{:S(2)}) copy-start(bf16[1024,2,128]{2,1,0:T(2,128)(2,1)} %get-tuple-element.26) | copy-start | bytes 1572868
  162.0 12.3 %copy-start.13 = (f32[256,512]{0,1:T(8,128)S(1)}, f32[256,512]{0,1:T(8,128)}, u32[]{:S(2)}) copy-start(f32[256,512]{0,1:T(8,128)} %fusion.9) | copy-start | bytes 1572868
  162.8 5.1 %collective-permute-start.5 = (f32[256,128]{1,0:T(8,128)S(1)}, f32[256,128]{1,0:T(8,128)S(1)}, u32[]{:S(2)}, u32[]{:S(2)}) collective-permute-start(f32[256,128]{1,0:T(8,128)S(1)} %collect.1), channel_id=1, source_target_pairs={{0,1},{1,0},{2,3},{3,2},{4,5},{5,4},{6,7},{7,6},{8,9},{9,8},{10,11... | collective-permute-start | bytes 393224 | tf_op jit(solution)/shard_map/ppermute | solution.py:343
  163.6 13.6 %copy-start.4 = (f32[16,256,128]{2,1,0:T(8,128)S(1)}, f32[16,256,128]{2,1,0:T(8,128)}, u32[]{:S(2)}) copy-start(f32[16,256,128]{2,1,0:T(8,128)} %copy-done.3) | copy-start | bytes 6291460
  165.5 11.7 %copy-start.2 = (f32[16,256,128]{2,1,0:T(8,128)S(1)}, f32[16,256,128]{2,1,0:T(8,128)}, u32[]{:S(2)}) copy-start(f32[16,256,128]{2,1,0:T(8,128)} %copy-done.1) | copy-start | bytes 6291460
  167.9 8.1 %collective-permute-start.6 = (f32[256,128]{1,0:T(8,128)S(1)}, f32[256,128]{1,0:T(8,128)S(1)}, u32[]{:S(2)}, u32[]{:S(2)}) collective-permute-start(f32[256,128]{1,0:T(8,128)S(1)} %add.69.a_ref), channel_id=1, source_target_pairs={{0,4},{1,5},{2,6},{3,7},{4,0},{5,1},{6,2},{7,3},{8,12},{9,13},{10,... | collective-permute-start | bytes 393224 | tf_op jit(solution)/shard_map/ppermute | solution.py:343
  171.0 6.2 %collective-permute-start.7 = (f32[256,128]{1,0:T(8,128)S(1)}, f32[256,128]{1,0:T(8,128)S(1)}, u32[]{:S(2)}, u32[]{:S(2)}) collective-permute-start(f32[256,128]{1,0:T(8,128)S(1)} %add.69.a_ref), channel_id=1, source_target_pairs={{0,2},{1,3},{2,4},{3,5},{4,6},{5,7},{6,0},{7,1},{8,10},{9,11},{10,... | collective-permute-start | bytes 393224 | tf_op jit(solution)/shard_map/ppermute | solution.py:343
  171.6 5.6 %collective-permute-start.8 = (f32[256,128]{1,0:T(8,128)S(1)}, f32[256,128]{1,0:T(8,128)S(1)}, u32[]{:S(2)}, u32[]{:S(2)}) collective-permute-start(f32[256,128]{1,0:T(8,128)S(1)} %add.69.a_ref), channel_id=1, source_target_pairs={{0,6},{1,7},{2,0},{3,1},{4,2},{5,3},{6,4},{7,5},{8,14},{9,15},{10,... | collective-permute-start | bytes 393224 | tf_op jit(solution)/shard_map/ppermute | solution.py:343
